TPU v7x, 512 devices: a whole 4x4x16 slice. The times are simulated.
512 devices in a mesh: seq: 128 (over x, z, core), head: 4 (over y).
Axes of the slice: x: 4, y: 4, z: 16, core: 2. Of those that a mesh axis runs over, the one named last changes fastest.
Arguments:
- tile_rows: bfloat16 [65536, 512], P('seq', 'head'), as said below
- tile_order: int32 [65536], P('seq'), may hold values from 0 to 65535, as said below
- tissue_mask: int32 [65536], P('seq'), may hold values from 0 to 1, as said below
- conv_weight: bfloat16 [512, 64, 512], P('seq', None, 'head'), may hold values from -0.03125 to 0.03125
- conv_bias: float32 [512], P('head'), may hold values from -3 to 3
- norm_gain: float32 [512], P('head'), may hold values from 0.1 to 1.9
- norm_bias: float32 [512], P('head'), may hold values from -3 to 3
- query_weight: bfloat16 [512, 512], P(None, 'head'), may hold values from -0.796875 to 0.796875
- key_weight: bfloat16 [512, 512], P(None, 'head'), may hold values from -0.25 to 0.25
- value_weight: bfloat16 [512, 512], P(None, 'head'), may hold values from -0.25 to 0.25
- out_weight: bfloat16 [512, 512], P('head'), may hold values from -0.25 to 0.25
Outputs:
- attention_out: bfloat16 [65536, 512], P('seq', 'head')
Inputs may be any that keep to these rules, and one draw needn't show every extreme that they name: `tile_rows`: features of the tiles. `tile_order`: A permutation of the grid positions. Grid blocks of 8 x 8 tiles are numbered row-major and owned in runs of 8 by the indices of seq in order; of the 512 tiles of one index of seq, at most 8 lie in the blocks of one owner, and every index of seq has 8 in the blocks of some owner. `tissue_mask`: 1 marks tissue, 0 background.
All inputs are finite; a program needn't handle non-finite values.
Results may differ from a plain program's by a relative error of at most 0.015.
The roundings to bfloat16 on the way count: a program that leaves them out, or rounds other values in their place, can miss the bound.
Values may be sent and summed in bfloat16 or wider, within the bound.
No kernel may reach another device: no remote copies, remote signals or barrier semaphores. Data moves between devices by JAX's collectives and lax.ppermute only.
A program may use at most 64 MiB of HBM per device.

v0:
```python
import math

import jax
import jax.numpy as jnp
from jax import lax
from jax.sharding import PartitionSpec as P

HEAD_SIZE = 64
REDUCE = 8
GRID_W = 512


def block_step(count):
    best = 1
    for candidate in range(1, min(count, 512) + 1):
        if count % candidate == 0:
            best = candidate
    return best


def make_fold(queries, heads_here, scale):

    def fold(carry, piece, start):
        count = piece.shape[0]
        step = block_step(count)
        blocks = piece.reshape(count // step, step, piece.shape[1])
        split_at = heads_here * HEAD_SIZE

        def visit(state, key_block):
            highest, totals, accum = state
            keys3 = key_block[:, :split_at].reshape(step, heads_here, HEAD_SIZE)
            values3 = key_block[:, split_at:].reshape(step, heads_here, HEAD_SIZE)
            scores = (
                jnp.einsum("thd,khd->htk", queries, keys3, preferred_element_type=jnp.float32)
                * scale
            )
            newest = jnp.maximum(highest, jnp.max(scores, -1))
            shrink = jnp.exp(highest - newest)
            weights = jnp.exp(scores - newest[:, :, None])
            totals = totals * shrink + jnp.sum(weights, -1)
            update = jnp.einsum(
                "htk,khd->thd",
                weights.astype(jnp.bfloat16),
                values3,
                preferred_element_type=jnp.float32,
            )
            accum = accum * shrink.T[:, :, None] + update
            return ((newest, totals, accum), None)

        carry, unused = lax.scan(visit, carry, blocks)
        return carry

    return fold


def local(
    tile_rows,
    tile_order,
    tissue_mask,
    conv_weight,
    conv_bias,
    norm_gain,
    norm_bias,
    query_weight,
    key_weight,
    value_weight,
    out_weight,
):
    devices = lax.axis_size("seq")
    local_rows, quarter = tile_rows.shape
    width = query_weight.shape[0]
    patch = conv_weight.shape[1]
    blocks_here = local_rows // patch
    capacity = 2 * (local_rows // devices)
    flags = tissue_mask.astype(jnp.bfloat16)
    masked = tile_rows * flags[:, None]
    grid_row = tile_order // GRID_W
    grid_col = tile_order % GRID_W
    block = grid_row // REDUCE * (GRID_W // REDUCE) + grid_col // REDUCE
    offset = grid_row % REDUCE * REDUCE + grid_col % REDUCE
    owner = block // blocks_here
    target = block % blocks_here * patch + offset
    onehot = (owner[:, None] == jnp.arange(devices, dtype=jnp.int32)[None, :]).astype(jnp.int32)
    ranks = jnp.sum(onehot * (jnp.cumsum(onehot, 0) - 1), 1)
    outgoing = jnp.zeros((devices, capacity, quarter), jnp.bfloat16).at[owner, ranks].set(masked)
    where_to = jnp.full((devices, capacity), -1, jnp.int32).at[owner, ranks].set(target)
    incoming, arrived = (
        lax.all_to_all(outgoing, "seq", split_axis=0, concat_axis=0, tiled=True),
        lax.all_to_all(where_to, "seq", split_axis=0, concat_axis=0, tiled=True),
    )
    places = arrived.reshape(-1)
    places = jnp.where(places >= 0, places, local_rows)
    patches = (
        jnp.zeros((local_rows + 1, quarter), jnp.bfloat16)
        .at[places]
        .set(incoming.reshape(-1, quarter))
    )
    patches = patches[:local_rows].reshape(blocks_here, patch, quarter)
    partial_conv = jnp.einsum(
        "bpc,opc->bo",
        patches,
        lax.all_gather(conv_weight, "seq", axis=0, tiled=True),
        preferred_element_type=jnp.float32,
    )
    shares = (
        lax.psum_scatter(partial_conv, "head", scatter_dimension=1, tiled=True) + conv_bias[None, :]
    )
    first_sum, second_sum = lax.psum((jnp.sum(shares, 1), jnp.sum(shares * shares, 1)), "head")
    center = (first_sum / width)[:, None]
    spread = (second_sum / width)[:, None]
    normed_share = (
        (shares - center) * lax.rsqrt(spread - center * center + 1e-05) * norm_gain + norm_bias
    ).astype(jnp.bfloat16)
    normed = lax.all_gather(normed_share, "head", axis=1, tiled=True)
    keys_here = jnp.dot(normed, key_weight, preferred_element_type=jnp.float32).astype(jnp.bfloat16)
    values_here = jnp.dot(normed, value_weight, preferred_element_type=jnp.float32).astype(
        jnp.bfloat16
    )
    key_value = jnp.concatenate([keys_here, values_here], 1)
    features = lax.all_gather(tile_rows, "head", axis=1, tiled=True)
    heads_here = quarter // HEAD_SIZE
    queries = jnp.dot(features, query_weight, preferred_element_type=jnp.float32).astype(
        jnp.bfloat16
    )
    queries = queries.reshape(local_rows, heads_here, HEAD_SIZE)
    scale = 1.0 / math.sqrt(HEAD_SIZE)
    start_state = (
        jnp.full((heads_here, local_rows), -1e30, jnp.float32),
        jnp.zeros((heads_here, local_rows), jnp.float32),
        jnp.zeros((local_rows, heads_here, HEAD_SIZE), jnp.float32),
    )
    folder = make_fold(queries, heads_here, scale)
    every_key = lax.all_gather(key_value, "seq", axis=0, tiled=True)
    highest, totals, accum = folder(start_state, every_key, 0)
    attended = (accum / totals.T[:, :, None]).reshape(local_rows, quarter).astype(jnp.bfloat16)
    projected = jnp.dot(attended, out_weight, preferred_element_type=jnp.float32)
    summed = lax.psum_scatter(
        projected.astype(jnp.bfloat16), "head", scatter_dimension=1, tiled=True
    ).astype(jnp.float32)
    return (summed * tissue_mask[:, None].astype(jnp.float32)).astype(jnp.bfloat16)


def solution(mesh):
    return jax.shard_map(
        local,
        mesh=mesh,
        in_specs=(
            P("seq", "head"),
            P("seq"),
            P("seq"),
            P("seq", None, "head"),
            P("head"),
            P("head"),
            P("head"),
            P(None, "head"),
            P(None, "head"),
            P(None, "head"),
            P("head", None),
        ),
        out_specs=P("seq", "head"),
        check_vma=False,
    )
```

profile of v0, /device:TPU:1, one launch (start us, length us, event | category | flops | bytes accessed | tf_op | source)
XLA Modules:
  0.0 349.2 jit_solution(16431818356530717991)
XLA Ops:
  6.5 0.7 all-gather.2.cloned.1.call-update
  8.7 22.0 %scatter_fusion = s32[128,8]{0,1:T(8,128)S(1)} fusion(s32[128,8]{0,1:T(8,128)S(1)} %broadcast_in_dim.22, s32[512]{0:T(512)S(1)} %bitcast.79, s32[512]{0:T(512)S(1)} %get-tuple-element.97), kind=kCustom, calls=%fused_computation | custom fusion | bytes 10240 | tf_op jit(solution)/shard_map/scatter | solution.py:86
  30.7 0.7 copy.25
  31.5 20.4 %all-to-all-start = ((s32[128,1,8]{2,1,0:T(1,128)}), s32[128,1,8]{2,1,0:T(1,128)S(1)}, u32[]{:S(2)}, u32[]{:S(2)}) async-start(s32[128,1,8]{2,1,0:T(1,128)} %copy.25), calls=%async_computation | async-start | bytes 131072 | tf_op jit(solution)/shard_map/all_to_all | solution.py:89
  52.0 0.7 broadcast_in_dim.48
  52.8 51.2 %scatter_fusion.1 = bf16[128,8,128]{2,1,0:T(8,128)(2,1)} fusion(bf16[128,8,128]{2,1,0:T(8,128)(2,1)} %broadcast_in_dim.48, s32[512]{0:T(512)S(1)} %bitcast.80, bf16[512,128]{1,0:T(8,128)(2,1)S(1)} %broadcast_multiply_fusion), kind=kCustom, calls=%fused_computation.1 | custom fusion | bytes 397312 | tf_op jit(solution)/shard_map/scatter | solution.py:85
  104.0 16.4 %all-to-all-start.1 = ((bf16[128,8,128]{2,1,0:T(8,128)(2,1)}), bf16[128,8,128]{2,1,0:T(8,128)(2,1)S(1)}, u32[]{:S(2)}, u32[]{:S(2)}) async-start(bf16[128,8,128]{2,1,0:T(8,128)(2,1)} %scatter_fusion.1), calls=%async_computation.1 | async-start | bytes 524288 | tf_op jit(solution)/shard_map/all_to_all | solution.py:88
  120.5 12.6 %all_gather.15 = bf16[512,512]{1,0:T(8,128)(2,1)S(1)} all-gather(bf16[512,128]{1,0:T(8,128)(2,1)S(1)} %copy-done.1), channel_id=1, replica_groups=mesh['seq'=128,'head'=4] {'head'}, dimensions={1}, use_global_device_ids=true | all-gather | bytes 655360 | tf_op jit(solution)/shard_map/all_gather | solution.py:120
  133.6 0.8 reduce.3
  134.5 11.4 %all-to-all-done.1 = bf16[128,8,128]{2,1,0:T(8,128)(2,1)S(1)} async-done(((bf16[128,8,128]{2,1,0:T(8,128)(2,1)}), bf16[128,8,128]{2,1,0:T(8,128)(2,1)S(1)}, u32[]{:S(2)}, u32[]{:S(2)}) %all-to-all-start.1) | async-done | bytes 262176 | tf_op jit(solution)/shard_map/all_to_all | solution.py:88
  145.9 3.4 scatter_custom_fusion.2
  149.3 22.2 %all-gather.2.cloned.1.call-done = bf16[512,64,128]{2,1,0:T(8,128)(2,1)} async-done(((bf16[4,64,128]{2,1,0:T(8,128)(2,1)}), bf16[512,64,128]{2,1,0:T(8,128)(2,1)}) %all-gather.2.cloned.1.call-update) | async-done | bytes 8388624 | tf_op jit(solution)/shard_map/all_gather | solution.py:102
  171.5 12.4 %fusion.13 = f32[8,512]{1,0:T(8,128)} fusion(bf16[512,64,128]{2,1,0:T(8,128)(2,1)} %all-gather.2.cloned.1.call-done, bf16[8,64,128]{2,1,0:T(8,128)(2,1)S(1)} %bitcast.87), kind=kOutput, calls=%fused_computation.25 | convolution fusion | flops 67108864 | bytes 8536064 | tf_op jit(solution)/shard_map/bpc,opc->bo/dot_general | solution.py:99
  184.3 19.5 %reduce-scatter.5.cloned.1.call-done = f32[8,128]{1,0:T(8,128)} async-done(((f32[8,512]{1,0:T(8,128)}), f32[8,128]{1,0:T(8,128)}) %reduce-scatter.5.cloned.1.call-update) | async-done | bytes 4112 | tf_op jit(solution)/shard_map/reduce_scatter | solution.py:106
  203.8 0.8 add_reduce_fusion
  204.6 6.8 %all-reduce = (f32[8]{0:T(128)S(1)}, f32[8]{0:T(128)S(1)}) all-reduce(f32[8]{0:T(128)S(1)} %get-tuple-element.80, f32[8]{0:T(128)S(1)} %get-tuple-element.79), channel_id=1, replica_groups=mesh['seq'=128,'head'=4] {'head'}, use_global_device_ids=true, to_apply=%region_10.11 | all-reduce | flops 16 | bytes 128 | tf_op jit(solution)/shard_map/psum | solution.py:108
  211.4 0.8 add_convert_fusion
  212.2 8.1 %all_gather.13 = bf16[8,512]{1,0:T(8,128)(2,1)S(1)} all-gather(bf16[8,128]{1,0:T(8,128)(2,1)S(1)} %add_convert_fusion), channel_id=1, replica_groups=mesh['seq'=128,'head'=4] {'head'}, dimensions={1}, use_global_device_ids=true | all-gather | bytes 10240 | tf_op jit(solution)/shard_map/all_gather | solution.py:114
  220.5 91.7 %all_gather.14 = bf16[1024,256]{1,0:T(8,128)(2,1)S(1)} all-gather(bf16[8,256]{1,0:T(8,128)(2,1)S(1)} %pad_maximum_fusion), channel_id=1, replica_groups=mesh['seq'=128,'head'=4] {'seq'}, dimensions={0}, use_global_device_ids=true | all-gather | bytes 528384 | tf_op jit(solution)/shard_map/all_gather | solution.py:133
  312.2 3.3 while.15
  315.9 1.0 copy.30
  316.9 23.9 %reduce-scatter.7.cloned.1.call-done = bf16[128,512]{1,0:T(8,128)(2,1)} async-done(((bf16[512,512]{1,0:T(8,128)(2,1)}), bf16[128,512]{1,0:T(8,128)(2,1)}) %reduce-scatter.7.cloned.1.call-update) | async-done | bytes 131088
  340.9 1.0 copy.31
  341.9 0.8 multiply_convert_fusion
  (70 shorter events, 6.4 us)
Async XLA Ops:
  6.5 309.0 %copy-start = (bf16[128,512]{1,0:T(8,128)(2,1)S(1)}, bf16[128,512]{1,0:T(8,128)(2,1)}, u32[]{:S(2)}) copy-start(bf16[128,512]{1,0:T(8,128)(2,1)} %param.23) | copy-start | bytes 393220
  6.5 164.9 %all-gather.2.cloned.1.call-start = ((), (), s32[]{:S(2)}) async-start(), calls=%async_computation.4 | async-start | bytes 8454144 | tf_op jit(solution)/shard_map/all_gather | solution.py:102
  8.7 43.2 %copy-start.5 = (s32[512]{0:T(512)S(1)}, s32[512]{0:T(512)}, u32[]{:S(2)}) copy-start(s32[512]{0:T(512)} %param.15) | copy-start | bytes 6148
  8.7 43.2 %copy-start.1 = (bf16[512,128]{1,0:T(8,128)(2,1)S(1)}, bf16[512,128]{1,0:T(8,128)(2,1)}, u32[]{:S(2)}) copy-start(bf16[512,128]{1,0:T(8,128)(2,1)} %param.13) | copy-start | bytes 393220
  31.5 72.5 %all-to-all-start = ((s32[128,1,8]{2,1,0:T(1,128)}), s32[128,1,8]{2,1,0:T(1,128)S(1)}, u32[]{:S(2)}, u32[]{:S(2)}) async-start(s32[128,1,8]{2,1,0:T(1,128)} %copy.25), calls=%async_computation | async-start | bytes 131072 | tf_op jit(solution)/shard_map/all_to_all | solution.py:89
  104.0 41.9 %all-to-all-start.1 = ((bf16[128,8,128]{2,1,0:T(8,128)(2,1)}), bf16[128,8,128]{2,1,0:T(8,128)(2,1)S(1)}, u32[]{:S(2)}, u32[]{:S(2)}) async-start(bf16[128,8,128]{2,1,0:T(8,128)(2,1)} %scatter_fusion.1), calls=%async_computation.1 | async-start | bytes 524288 | tf_op jit(solution)/shard_map/all_to_all | solution.py:88
  120.4 83.4 %reduce-scatter.5.cloned.1.call-start = ((), (), s32[]{:S(2)}) async-start(), calls=%async_computation.5 | async-start | bytes 20480 | tf_op jit(solution)/shard_map/reduce_scatter | solution.py:106
  171.4 12.5 %copy-start.4 = (bf16[512,128]{1,0:T(8,128)(2,1)S(1)}, bf16[512,128]{1,0:T(8,128)(2,1)}, u32[]{:S(2)}) copy-start(bf16[512,128]{1,0:T(8,128)(2,1)} %param.20) | copy-start | bytes 393220
  171.4 32.4 %copy-start.6 = (f32[128]{0:T(128)S(1)}, f32[128]{0:T(128)}, u32[]{:S(2)}) copy-start(f32[128]{0:T(128)} %param.17) | copy-start | bytes 1540
  171.4 40.0 %copy-start.7 = (f32[128]{0:T(128)S(1)}, f32[128]{0:T(128)}, u32[]{:S(2)}) copy-start(f32[128]{0:T(128)} %param.19) | copy-start | bytes 1540
  171.4 40.0 %copy-start.8 = (f32[128]{0:T(128)S(1)}, f32[128]{0:T(128)}, u32[]{:S(2)}) copy-start(f32[128]{0:T(128)} %param.18) | copy-start | bytes 1540
  171.4 48.8 %copy-start.2 = (bf16[512,128]{1,0:T(8,128)(2,1)S(1)}, bf16[512,128]{1,0:T(8,128)(2,1)}, u32[]{:S(2)}) copy-start(bf16[512,128]{1,0:T(8,128)(2,1)} %param.22) | copy-start | bytes 393220
  171.4 48.9 %copy-start.3 = (bf16[512,128]{1,0:T(8,128)(2,1)S(1)}, bf16[512,128]{1,0:T(8,128)(2,1)}, u32[]{:S(2)}) copy-start(bf16[512,128]{1,0:T(8,128)(2,1)} %param.21) | copy-start | bytes 393220
  183.9 157.0 %reduce-scatter.7.cloned.1.call-start = ((), (), s32[]{:S(2)}) async-start(), calls=%async_computation.6 | async-start | bytes 655360
Sparse Core Ops, SparseCore 0:
  10.5 160.8 all-gather.1
  184.0 19.7 reduce-scatter.4
  317.0 23.7 reduce-scatter.6
where the time goes:
time: 351 us; the launch traced here: 349 us
  blocking collectives  119 us (34%)
  local copies, waits for them, and re-layouts  81.2 us (23%)
  waiting for transfers between devices  77.7 us (22%)
  starting transfers between devices  36.9 us (11%)
  matrix products  15.3 us (4%)
  between operations  13.4 us (4%)
  other arithmetic  5.44 us (2%)
    all_gather x1, blocking collectives, local(): every_key = lax.all_gather(key_value, 'seq', axis=0, tiled=True)  91.7 us
    scatter x1, local copies, waits for them, and re-layouts, local(): jnp.zeros((devices, capacity, quarter), jnp.bfloat16).at[owner, ranks]  51.2 us
    unnamed x4, waiting for transfers between devices  24.7 us
    all_gather x1, waiting for transfers between devices, local(): lax.all_gather(conv_weight, 'seq', axis=0, tiled=True)  22.2 us
    scatter x1, local copies, waits for them, and re-layouts, local(): jnp.full((devices, capacity), -1, jnp.int32).at[owner, ranks].set(target)  22 us
    all_to_all x1, starting transfers between devices, local(): lax.all_to_all(where_to, 'seq', split_axis=0, concat_axis=0, tiled=True)  20.4 us
    reduce_scatter x1, waiting for transfers between devices, local(): lax.psum_scatter(partial_conv, 'head', scatter_dimension=1, tiled=True)  19.5 us
    all_to_all x1, starting transfers between devices, local(): lax.all_to_all(outgoing, 'seq', split_axis=0, concat_axis=0, tiled=True)  16.4 us
  transfers between devices with their start and end apart: 5, of which 4 were waited for; matrix products, arithmetic and copies ran while one was open for 23% of the time, Pallas kernels for 0%

commit v1 on v0

v1 whole, which is shorter than its diff:
```python
import math

import jax
import jax.numpy as jnp
from jax import lax
from jax.experimental import pallas as pl
from jax.experimental.pallas import tpu as pltpu
from jax.sharding import Mesh
from jax.sharding import PartitionSpec as P

NX, NZ, NC, NH = 4, 16, 2, 4
PLANE = NX * NC
SLOTS = 8
ROWS = PLANE * SLOTS
SEND = ROWS + 16
TOK = 512
LANES = 128
BLK = 8
PATCH = 64
EMPTY = 1024.0
F32 = jnp.float32
BF16 = jnp.bfloat16
NT = (((1,), (1,)), ((), ()))


def params(mib):
    return pltpu.CompilerParams(vmem_limit_bytes=mib * 1024 * 1024)


def iota(shape, dim):
    return lax.broadcasted_iota(jnp.int32, shape, dim)


def route_kernel(rows_ref, order_ref, mask_ref, out_ref):
    order = order_ref[...]
    row, col = order >> 9, order & 511
    owner = (row >> 3) * 8 + (col >> 6)
    plane = (owner >> 1) & 15
    place = (owner >> 5) * 2 + (owner & 1)
    target = ((row & 7) * 8 + (col & 7)) * BLK + ((col >> 3) & 7)
    code = plane * PLANE + place
    onehot = jnp.where(iota((128, TOK), 0) == code, 1.0, 0.0)
    before = jnp.where(iota((TOK, TOK), 0) < iota((TOK, TOK), 1), 1.0, 0.0).astype(BF16)
    counts = jnp.dot(onehot.astype(BF16), before, preferred_element_type=F32)
    rank = jnp.sum(onehot * counts, 0, keepdims=True).astype(jnp.int32)
    slot = place * SLOTS + rank
    here = iota((NZ, TOK), 0) == plane
    value = jnp.where(here, (target - 256).astype(F32), 0.0).astype(BF16)
    there = jnp.where(here, 1.0, 0.0).astype(BF16)
    lane_of = jnp.where(iota((LANES, TOK), 0) == slot, 1.0, 0.0).astype(BF16)
    values = lax.dot_general(value, lane_of, NT, preferred_element_type=F32)
    valid = lax.dot_general(there, lane_of, NT, preferred_element_type=F32)
    meta = jnp.where(valid > 0.5, values, EMPTY)
    wanted = jnp.where(mask_ref[...] != 0, plane * ROWS + slot, -1)
    rows = rows_ref[...]
    for z in range(NZ):
        pick = jnp.where(iota((ROWS, TOK), 0) + z * ROWS == wanted, 1.0, 0.0).astype(BF16)
        out_ref[z, 0:ROWS, :] = jnp.dot(pick, rows, preferred_element_type=F32).astype(BF16)
        out_ref[z, ROWS:SEND, :] = jnp.broadcast_to(meta[z : z + 1, :], (16, LANES)).astype(BF16)


def conv_kernel(near_ref, far_ref, weight_ref, param_ref, out_ref, patch_ref):
    spot = (iota((TOK, LANES), 0) - 256).astype(F32)
    for owner in range(PLANE):
        total = None
        for ref in (near_ref, far_ref):
            for x in range(NX):
                meta = ref[x, PLANE * 128 : PLANE * 128 + 16, :].astype(F32)[owner : owner + 1, :]
                pick = jnp.where(spot == meta, 1.0, 0.0).astype(BF16)
                part = jnp.dot(
                    pick,
                    ref[x, owner * 128 : owner * 128 + 128, :],
                    preferred_element_type=F32,
                )
                total = part if total is None else total + part
        patch_ref[:, owner * BLK : owner * BLK + BLK, :] = total.reshape(PATCH, BLK, LANES)
    acc = jnp.zeros((256, 256), F32)
    for quad in range(16):
        left = weight_ref[:, quad * 16 : quad * 16 + 16, :].reshape(256, LANES)
        right = patch_ref[quad * 4 : quad * 4 + 4, :, :].astype(BF16).reshape(256, LANES)
        acc = acc + lax.dot_general(right, left, NT, preferred_element_type=F32)
    column = iota((64, 256), 1)
    kept = jnp.zeros((64, 256), F32)
    for step in range(4):
        kept = kept + jnp.where(
            ((column >> 2) & 3) == step, acc[step * 64 : step * 64 + 64, :], 0.0
        )
    source, lane = iota((256, LANES), 0), iota((256, LANES), 1)
    merge = jnp.where(((source >> 4) * 4 + (source & 3)) == lane, 1.0, 0.0)
    sums = jnp.dot(
        kept, merge, precision=lax.Precision.HIGHEST, preferred_element_type=F32
    )
    sent = sums.reshape(PLANE, BLK, LANES) + param_ref[...][None]
    for head in range(NH):
        out_ref[:, head] = sent


def norm_kernel(sums_ref, key_ref, value_ref, out_ref):
    left = iota((BLK, LANES), 1) < 64
    shares, gains, biases = [], [], []
    for x in range(NX):
        for c in range(NC):
            total = sums_ref[x, c, 0]
            for head in range(1, NH):
                total = total + sums_ref[x, c, head]
            extra = pltpu.roll(sums_ref[x, c, x], 64, 1)
            gains.append(extra[c : c + 1, :])
            biases.append(extra[2 + c : 3 + c, :])
            shares.append(jnp.where(left, total + extra[4 + c : 5 + c, :], 0.0))
    first = shares[0]
    second = shares[0] * shares[0]
    for share in shares[1:]:
        first = first + share
        second = second + share * share
    center = jnp.sum(first, 1, keepdims=True) * (1.0 / 512)
    spread = jnp.sum(second, 1, keepdims=True) * (1.0 / 512)
    scale = lax.rsqrt(spread - center * center + 1e-05)
    keys = jnp.zeros((BLK, LANES), F32)
    values = jnp.zeros((BLK, LANES), F32)
    source, lane = iota((LANES, LANES), 0), iota((LANES, LANES), 1)
    for x in range(NX):
        spread_out = None
        for c in range(NC):
            index = x * NC + c
            normed = (shares[index] - center) * scale * gains[index] + biases[index]
            normed = jnp.where(left, normed, 0.0).astype(BF16)
            hit = (lane == (source >> 2) * 8 + c * 4 + (source & 3)) & (source < 64)
            part = jnp.dot(
                normed, jnp.where(hit, 1.0, 0.0).astype(BF16), preferred_element_type=F32
            )
            spread_out = part if spread_out is None else spread_out + part
        natural = spread_out.astype(BF16)
        keys = keys + jnp.dot(
            natural, key_ref[x * 128 : x * 128 + 128, :], preferred_element_type=F32
        )
        values = values + jnp.dot(
            natural, value_ref[x * 128 : x * 128 + 128, :], preferred_element_type=F32
        )
    both = jnp.concatenate([keys, values], 1).astype(BF16)
    for z in range(NZ):
        out_ref[z] = both


def query_kernel(features_ref, weight_ref, out_ref):
    total = None
    for head in range(NH):
        part = jnp.dot(
            features_ref[head],
            weight_ref[head * 128 : head * 128 + 128, :],
            preferred_element_type=F32,
        )
        total = part if total is None else total + part
    out_ref[...] = total.astype(BF16)


def attend_kernel(query_ref, key_value_ref, weight_ref, out_ref):
    factor = math.log2(math.e) / math.sqrt(64)
    step = 256
    keys = key_value_ref[:, 0:128]
    values = key_value_ref[:, 128:256]
    weight = weight_ref[...]
    lane = iota((step, LANES), 1)
    for start in range(0, TOK, step):
        query = query_ref[start : start + step, :]
        mixed = []
        for head in range(2):
            mine = (lane >> 6) == head
            masked = jnp.where(mine, query.astype(F32), 0.0).astype(BF16)
            scores = lax.dot_general(masked, keys, NT, preferred_element_type=F32)
            highest = jnp.max(scores, 1, keepdims=True)
            weights = jnp.exp2((scores - highest) * factor)
            totals = jnp.sum(weights, 1, keepdims=True)
            mix = jnp.dot(weights.astype(BF16), values, preferred_element_type=F32)
            mixed.append(mix / totals)
        attended = jnp.where(lane < 64, mixed[0], mixed[1]).astype(BF16)
        part = jnp.dot(attended, weight, preferred_element_type=F32).astype(BF16)
        for group in range(NH):
            out_ref[group, start : start + step, :] = part[:, group * 128 : group * 128 + 128]


def local(
    tile_rows,
    tile_order,
    tissue_mask,
    conv_weight,
    conv_bias,
    norm_gain,
    norm_bias,
    query_weight,
    key_weight,
    value_weight,
    out_weight,
):
    shape = jax.ShapeDtypeStruct
    turned = conv_weight.transpose(1, 0, 2).reshape(256, LANES)
    weights = lax.all_gather(turned, "z", axis=0, tiled=True).reshape(NZ, 256, LANES)
    sorted_rows = pl.pallas_call(
        route_kernel,
        out_shape=shape((NZ, SEND, LANES), BF16),
        compiler_params=params(32),
    )(tile_rows, tile_order.reshape(1, TOK), tissue_mask.reshape(1, TOK))
    arrived = lax.all_to_all(sorted_rows, "z", split_axis=0, concat_axis=0, tiled=True)
    payload = arrived[:, :ROWS].reshape(NZ, PLANE, SLOTS, LANES).transpose(1, 0, 2, 3)
    places = arrived[:, ROWS, :ROWS].reshape(NZ, PLANE, SLOTS).transpose(1, 0, 2)
    places = jnp.pad(places.reshape(PLANE, LANES), ((0, 8), (0, 0)))
    here = jnp.concatenate([payload.reshape(PLANE * 128, LANES), places], 0)
    near = lax.all_to_all(
        jnp.broadcast_to(here[None], (NX,) + here.shape), "x", split_axis=0, concat_axis=0, tiled=True
    )
    far = lax.ppermute(near, "core", [(0, 1), (1, 0)])
    features = lax.all_gather(tile_rows, "head", axis=0)
    queries = pl.pallas_call(
        query_kernel, out_shape=shape((TOK, LANES), BF16), compiler_params=params(32)
    )(features, query_weight)
    extra = jnp.stack([norm_gain, norm_bias, conv_bias]).reshape(3, NZ, NC, 4)
    extra = jnp.pad(extra.transpose(0, 2, 1, 3).reshape(6, 64), ((0, 2), (64, 0)))
    partial = pl.pallas_call(
        conv_kernel,
        out_shape=shape((PLANE, NH, BLK, LANES), F32),
        scratch_shapes=[pltpu.VMEM((PATCH, 64, LANES), F32)],
        compiler_params=params(48),
    )(near, far, weights, extra)
    sums = lax.all_to_all(
        partial.reshape(PLANE * NH, BLK, LANES),
        ("x", "core", "head"),
        split_axis=0,
        concat_axis=0,
        tiled=True,
    )
    key_value = pl.pallas_call(
        norm_kernel, out_shape=shape((NZ, BLK, 256), BF16), compiler_params=params(32)
    )(sums.reshape(NX, NC, NH, BLK, LANES), key_weight, value_weight)
    gathered = lax.all_to_all(key_value, "z", split_axis=0, concat_axis=0, tiled=True)
    gathered = gathered.reshape(NZ * BLK, 256)
    gathered = lax.all_gather(gathered, "x", axis=0, tiled=True)
    gathered = lax.all_gather(gathered, "core", axis=0, tiled=True)
    parts = pl.pallas_call(
        attend_kernel, out_shape=shape((NH, TOK, LANES), BF16), compiler_params=params(48)
    )(queries, gathered, out_weight)
    parts = lax.all_to_all(parts, "head", split_axis=0, concat_axis=0, tiled=True)
    summed = jnp.sum(parts.astype(F32), 0)
    return (summed * tissue_mask[:, None].astype(F32)).astype(BF16)


def solution(mesh):
    grid = Mesh(mesh.devices.reshape(NX, NZ, NC, NH), ("x", "z", "core", "head"))
    seq = ("x", "z", "core")
    return jax.shard_map(
        local,
        mesh=grid,
        in_specs=(
            P(seq, "head"),
            P(seq),
            P(seq),
            P(seq, None, "head"),
            P("head"),
            P("head"),
            P("head"),
            P(None, "head"),
            P(None, "head"),
            P(None, "head"),
            P("head", None),
        ),
        out_specs=P(seq, "head"),
        check_vma=False,
    )
```

time: 351 us -> 184 us (0.52)
  local copies, waits for them, and re-layouts: 81.2 us -> 5.65 us
  blocking collectives: 119 us -> 66 us
  waiting for transfers between devices: 77.7 us -> 49.9 us
  matrix products: 15.3 us -> 0 us
  Pallas kernels: 0 us -> 10.4 us
  other arithmetic: 5.44 us -> 0.89 us
    all_gather x3, blocking collectives: 112 us -> 27.5 us  [the longest x1 10.6 us: local(): features = lax.all_gather(tile_rows, 'head', axis=0)]
    scatter x3 -> x0, local copies, waits for them, and re-layouts: 76.5 us -> none  [the longest x1 51.2 us: local(): jnp.zeros((devices, capacity, quarter), jnp.bfloat16).at[owner, ranks]]
    all_to_all x0 -> x2, blocking collectives: none -> 38.5 us  [the longest x1 24.7 us: local(): lax.all_to_all(partial.reshape(PLANE * NH, BLK, LANES), ('x', 'core', 'he...]
    unnamed x4 -> x1, waiting for transfers between devices: 24.7 us -> 0.02 us
    reduce_scatter x1 -> x0, waiting for transfers between devices: 19.5 us -> none  [local(): lax.psum_scatter(partial_conv, 'head', scatter_dimension=1, tiled=True)]
    dot_general x9 -> x0, matrix products: 15.3 us -> none  [the longest x1 12.4 us: local(): jnp.einsum('bpc,opc->bo', patches, lax.all_gather(conv_weight, 'seq', axi...]
    all_to_all x2 -> x3, waiting for transfers between devices: 11.4 us -> 24.3 us  [the longest x1 14.5 us: local(): lax.all_to_all(sorted_rows, 'z', split_axis=0, concat_axis=0, tiled=True)]
    pallas_call x0 -> x5, Pallas kernels: none -> 10.4 us  [the longest x1 4.13 us: local(): pl.pallas_call(conv_kernel, out_shape=shape((PLANE, NH, BLK, LANES), F32)...]
  transfers between devices with their start and end apart: 5 -> 5, of which waited for: 4 -> 4; matrix products, arithmetic and copies ran while one was open for 23% -> 1% of each run, Pallas kernels for 0% -> 0%
where the time goes in v1:
time: 184 us; the launch traced here: 183 us
  blocking collectives  66 us (36%)
  waiting for transfers between devices  49.9 us (27%)
  starting transfers between devices  36.5 us (20%)
  between operations  13.6 us (7%)
  Pallas kernels  10.4 us (6%)
  local copies, waits for them, and re-layouts  5.65 us (3%)
    all_gather x1, waiting for transfers between devices, local(): lax.all_gather(turned, 'z', axis=0, tiled=True).reshape(NZ, 256, LANES)  25.5 us
    all_to_all x1, blocking collectives, local(): lax.all_to_all(partial.reshape(PLANE * NH, BLK, LANES), ('x', 'core', 'he...  24.7 us
    all_to_all x1, starting transfers between devices, local(): lax.all_to_all(sorted_rows, 'z', split_axis=0, concat_axis=0, tiled=True)  15.7 us
    all_to_all x1, waiting for transfers between devices, local(): lax.all_to_all(sorted_rows, 'z', split_axis=0, concat_axis=0, tiled=True)  14.5 us
    all_to_all x1, blocking collectives, local(): lax.all_to_all(jnp.broadcast_to(here[None], (NX,) + here.shape), 'x', spl...  13.9 us
    all_gather x1, blocking collectives, local(): features = lax.all_gather(tile_rows, 'head', axis=0)  10.6 us
    ppermute x1, starting transfers between devices, local(): far = lax.ppermute(near, 'core', [(0, 1), (1, 0)])  9.75 us
    all_gather x1, blocking collectives, local(): gathered = lax.all_gather(gathered, 'x', axis=0, tiled=True)  9.36 us
  transfers between devices with their start and end apart: 5, of which 4 were waited for; matrix products, arithmetic and copies ran while one was open for 1% of the time, Pallas kernels for 0%

profile of v1, /device:TPU:1, one launch (start us, length us, event | category | flops | bytes accessed | tf_op | source)
XLA Modules:
  0.0 183.0 jit_solution(15934169224640513758)
XLA Ops:
  6.5 0.9 copy-done.1
  7.4 0.7 copy-done.7
  8.1 0.7 copy-done.9
  8.8 1.5 shard_map.110
  10.3 15.7 %all-to-all-start = ((bf16[16,80,128]{2,1,0:T(8,128)(2,1)}), bf16[16,80,128]{2,1,0:T(8,128)(2,1)S(1)}, u32[]{:S(2)}, u32[]{:S(2)}) async-start(bf16[16,80,128]{2,1,0:T(8,128)(2,1)} %shard_map.110), calls=%async_computation | async-start | bytes 655360 | tf_op jit(solution)/shard_map/all_to_all | solution.py:202
  26.1 0.7 copy.23
  26.8 14.5 %all-to-all-done = bf16[16,80,128]{2,1,0:T(8,128)(2,1)S(1)} async-done(((bf16[16,80,128]{2,1,0:T(8,128)(2,1)}), bf16[16,80,128]{2,1,0:T(8,128)(2,1)S(1)}, u32[]{:S(2)}, u32[]{:S(2)}) %all-to-all-start) | async-done | bytes 327712 | tf_op jit(solution)/shard_map/all_to_all | solution.py:202
  41.9 13.9 %all_to_all.25.near_ref = bf16[4,1040,128]{2,1,0:T(8,128)(2,1)S(1)} all-to-all(bf16[4,1040,128]{2,1,0:T(8,128)(2,1)S(1)} %broadcast_in_dim.2), channel_id=1, replica_groups=mesh['x'=4,'z'=16,'core'=2,'head'=4] {'x'}, dimensions={0} | all-to-all | bytes 2129920 | tf_op jit(solution)/shard_map/all_to_all | solution.py:207
  55.7 9.8 %collective-permute-start = (bf16[4,1040,128]{2,1,0:T(8,128)(2,1)S(1)}, bf16[4,1040,128]{2,1,0:T(8,128)(2,1)S(1)}, u32[]{:S(2)}, u32[]{:S(2)}) collective-permute-start(bf16[4,1040,128]{2,1,0:T(8,128)(2,1)S(1)} %all_to_all.25.near_ref), channel_id=1, source_target_pairs={{0,4},{4,0},{1,5},{5,1},{2,6},{6,2},{3,7},{7,3},{8,12},{12,8},{9,1... | collective-permute-start | bytes 3194888 | tf_op jit(solution)/shard_map/ppermute | solution.py:210
  66.5 25.5 %all-gather.3.cloned.1.call-done = bf16[4096,128]{1,0:T(8,128)(2,1)} async-done(((bf16[256,128]{1,0:T(8,128)(2,1)}), bf16[4096,128]{1,0:T(8,128)(2,1)}) %all-gather.3.cloned.1.call-update) | async-done | bytes 1048592 | tf_op jit(solution)/shard_map/all_gather | solution.py:196
  92.0 1.2 copy-done
  93.2 4.1 %shard_map.111 = f32[8,4,8,128]{3,2,1,0:T(8,128)S(1)} custom-call(bf16[4,1040,128]{2,1,0:T(8,128)(2,1)S(1)} %all_to_all.25.near_ref, bf16[4,1040,128]{2,1,0:T(8,128)(2,1)S(1)} %collective-permute-done.far_ref, bf16[16,256,128]{2,1,0:T(8,128)(2,1)S(1)} %bitcast.22, f32[8,128]{1,0:T(8,128)S(1)} %pad.9.param_ref), custom_call_target="tpu_custom_call" | custom-call | tf_op jit(solution)/shard_map/pallas_call | solution.py:217
  97.4 24.7 %all_to_all.26 = f32[32,8,128]{2,1,0:T(8,128)S(1)} all-to-all(f32[32,8,128]{2,1,0:T(8,128)S(1)} %bitcast.23), channel_id=1, replica_groups=mesh['x'=4,'z'=16,'core'=2,'head'=4] {'x','core','head'}, dimensions={0} | all-to-all | bytes 262144 | tf_op jit(solution)/shard_map/all_to_all | solution.py:223
  122.1 1.3 shard_map.112
  123.4 7.5 %all-to-all-start.3 = ((bf16[16,8,256]{2,1,0:T(8,128)(2,1)}), bf16[16,8,256]{2,1,0:T(8,128)(2,1)S(1)}, u32[]{:S(2)}, u32[]{:S(2)}) async-start(bf16[16,8,256]{2,1,0:T(8,128)(2,1)} %shard_map.112), calls=%async_computation.3 | async-start | bytes 131072 | tf_op jit(solution)/shard_map/all_to_all | solution.py:233
  130.9 10.6 %all-gather = bf16[2048,128]{1,0:T(8,128)(2,1)S(1)} all-gather(bf16[512,128]{1,0:T(8,128)(2,1)S(1)} %copy-done.2), channel_id=2, replica_groups=mesh['x'=4,'z'=16,'core'=2,'head'=4] {'head'}, dimensions={0}, use_global_device_ids=true | all-gather | bytes 655360 | tf_op jit(solution)/shard_map/all_gather | solution.py:211
  141.5 0.3 shard_map.109.query_ref
  141.8 0.7 all-to-all-done.3
  142.5 9.4 %all_gather.18 = bf16[512,256]{1,0:T(8,128)(2,1)S(1)} all-gather(bf16[128,256]{1,0:T(8,128)(2,1)S(1)} %bitcast.28), channel_id=1, replica_groups=mesh['x'=4,'z'=16,'core'=2,'head'=4] {'x'}, dimensions={0}, use_global_device_ids=true | all-gather | bytes 327680 | tf_op jit(solution)/shard_map/all_gather | solution.py:235
  151.9 7.6 %all_gather.19.key_value_ref = bf16[1024,256]{1,0:T(8,128)(2,1)S(1)} all-gather(bf16[512,256]{1,0:T(8,128)(2,1)S(1)} %all_gather.18), channel_id=1, replica_groups=mesh['x'=4,'z'=16,'core'=2,'head'=4] {'core'}, dimensions={0}, use_global_device_ids=true | all-gather | bytes 786432 | tf_op jit(solution)/shard_map/all_gather | solution.py:236
  159.4 3.1 %shard_map.113 = bf16[4,512,128]{2,1,0:T(8,128)(2,1)} custom-call(bf16[512,128]{1,0:T(8,128)(2,1)S(1)} %shard_map.109.query_ref, bf16[1024,256]{1,0:T(8,128)(2,1)S(1)} %all_gather.19.key_value_ref, bf16[128,512]{1,0:T(8,128)(2,1)S(1)} %copy-done.5), custom_call_target="tpu_custom_call" | custom-call | tf_op jit(solution)/shard_map/pallas_call | solution.py:237
  162.6 3.5 %all-to-all-start.4 = ((bf16[4,512,128]{2,1,0:T(8,128)(2,1)}), bf16[4,512,128]{2,1,0:T(8,128)(2,1)S(1)}, u32[]{:S(2)}, u32[]{:S(2)}) async-start(bf16[4,512,128]{2,1,0:T(8,128)(2,1)} %shard_map.113), calls=%async_computation.4 | async-start | bytes 1048576 | tf_op jit(solution)/shard_map/all_to_all | solution.py:240
  166.1 9.2 %all-to-all-done.4 = bf16[4,512,128]{2,1,0:T(8,128)(2,1)S(1)} async-done(((bf16[4,512,128]{2,1,0:T(8,128)(2,1)}), bf16[4,512,128]{2,1,0:T(8,128)(2,1)S(1)}, u32[]{:S(2)}, u32[]{:S(2)}) %all-to-all-start.4) | async-done | bytes 524320 | tf_op jit(solution)/shard_map/all_to_all | solution.py:240
  175.3 0.8 multiply_convert_fusion
  (47 shorter events, 1.6 us)
Async XLA Ops:
  6.5 0.9 copy-start.1
  7.4 0.7 copy-start.7
  8.1 0.7 copy-start.9
  8.8 17.3 %copy-start.10 = (bf16[4,64,128]{2,1,0:T(8,128)(2,1)S(1)}, bf16[4,64,128]{2,1,0:T(8,128)(2,1)}, u32[]{:S(2)}) copy-start(bf16[4,64,128]{2,1,0:T(8,128)(2,1)} %param.14) | copy-start | bytes 196612
  10.3 31.0 %all-to-all-start = ((bf16[16,80,128]{2,1,0:T(8,128)(2,1)}), bf16[16,80,128]{2,1,0:T(8,128)(2,1)S(1)}, u32[]{:S(2)}, u32[]{:S(2)}) async-start(bf16[16,80,128]{2,1,0:T(8,128)(2,1)} %shard_map.110), calls=%async_computation | async-start | bytes 655360 | tf_op jit(solution)/shard_map/all_to_all | solution.py:202
  26.0 66.0 %all-gather.3.cloned.1.call-start = ((), (), s32[]{:S(2)}) async-start(), calls=%async_computation.5 | async-start | bytes 1114112 | tf_op jit(solution)/shard_map/all_gather | solution.py:196
  41.8 23.7 %copy-start.11 = (f32[128]{0:T(128)S(1)}, f32[128]{0:T(128)}, u32[]{:S(2)}) copy-start(f32[128]{0:T(128)} %param.16) | copy-start | bytes 1540
  41.9 23.9 %copy-start.12 = (f32[128]{0:T(128)S(1)}, f32[128]{0:T(128)}, u32[]{:S(2)}) copy-start(f32[128]{0:T(128)} %param.17) | copy-start | bytes 1540
  41.9 24.1 %copy-start.13 = (f32[128]{0:T(128)S(1)}, f32[128]{0:T(128)}, u32[]{:S(2)}) copy-start(f32[128]{0:T(128)} %param.15) | copy-start | bytes 1540
  55.7 36.3 %collective-permute-start = (bf16[4,1040,128]{2,1,0:T(8,128)(2,1)S(1)}, bf16[4,1040,128]{2,1,0:T(8,128)(2,1)S(1)}, u32[]{:S(2)}, u32[]{:S(2)}) collective-permute-start(bf16[4,1040,128]{2,1,0:T(8,128)(2,1)S(1)} %all_to_all.25.near_ref), channel_id=1, source_target_pairs={{0,4},{4,0},{1,5},{5,1},{2,6},{6,2},{3,7},{7,3},{8,12},{12,8},{9,1... | collective-permute-start | bytes 3194888 | tf_op jit(solution)/shard_map/ppermute | solution.py:210
  92.0 1.2 copy-start
  93.2 28.8 %copy-start.3 = (bf16[512,128]{1,0:T(8,128)(2,1)S(1)}, bf16[512,128]{1,0:T(8,128)(2,1)}, u32[]{:S(2)}) copy-start(bf16[512,128]{1,0:T(8,128)(2,1)} %key_ref.1) | copy-start | bytes 393220
  93.2 28.8 %copy-start.4 = (bf16[512,128]{1,0:T(8,128)(2,1)S(1)}, bf16[512,128]{1,0:T(8,128)(2,1)}, u32[]{:S(2)}) copy-start(bf16[512,128]{1,0:T(8,128)(2,1)} %value_ref.1) | copy-start | bytes 393220
  93.2 37.7 %copy-start.2 = (bf16[512,128]{1,0:T(8,128)(2,1)S(1)}, bf16[512,128]{1,0:T(8,128)(2,1)}, u32[]{:S(2)}) copy-start(bf16[512,128]{1,0:T(8,128)(2,1)} %rows_ref.1) | copy-start | bytes 393220
  97.4 44.1 %copy-start.6 = (bf16[512,128]{1,0:T(8,128)(2,1)S(1)}, bf16[512,128]{1,0:T(8,128)(2,1)}, u32[]{:S(2)}) copy-start(bf16[512,128]{1,0:T(8,128)(2,1)} %weight_ref.2) | copy-start | bytes 393220
  123.4 19.1 %all-to-all-start.3 = ((bf16[16,8,256]{2,1,0:T(8,128)(2,1)}), bf16[16,8,256]{2,1,0:T(8,128)(2,1)S(1)}, u32[]{:S(2)}, u32[]{:S(2)}) async-start(bf16[16,8,256]{2,1,0:T(8,128)(2,1)} %shard_map.112), calls=%async_computation.3 | async-start | bytes 131072 | tf_op jit(solution)/shard_map/all_to_all | solution.py:233
  141.5 17.9 %copy-start.5 = (bf16[128,512]{1,0:T(8,128)(2,1)S(1)}, bf16[128,512]{1,0:T(8,128)(2,1)}, u32[]{:S(2)}) copy-start(bf16[128,512]{1,0:T(8,128)(2,1)} %weight_ref.3) | copy-start | bytes 393220
  159.4 6.6 %copy-start.8 = (s32[512]{0:T(512)S(1)}, s32[512]{0:T(512)}, u32[]{:S(2)}) copy-start(s32[512]{0:T(512)} %param.13) | copy-start | bytes 6148
  162.6 12.7 %all-to-all-start.4 = ((bf16[4,512,128]{2,1,0:T(8,128)(2,1)}), bf16[4,512,128]{2,1,0:T(8,128)(2,1)S(1)}, u32[]{:S(2)}, u32[]{:S(2)}) async-start(bf16[4,512,128]{2,1,0:T(8,128)(2,1)} %shard_map.113), calls=%async_computation.4 | async-start | bytes 1048576 | tf_op jit(solution)/shard_map/all_to_all | solution.py:240
Sparse Core Ops, SparseCore 0:
  29.0 63.0 all-gather.2

commit v2 on v1

--- a/solution.py
+++ b/solution.py
@@ -12,8 +12,10 @@
 PLANE = NX * NC
 SLOTS = 8
 ROWS = PLANE * SLOTS
-SEND = ROWS + 16
+SEND = ROWS + 32
 TOK = 512
+MOST = 240
+WIDE = TOK + 48
 LANES = 128
 BLK = 8
 PATCH = 64
@@ -31,7 +33,18 @@
     return lax.broadcasted_iota(jnp.int32, shape, dim)
 
 
-def route_kernel(rows_ref, order_ref, mask_ref, out_ref):
+def route_kernel(rows_ref, order_ref, mask_ref, tail_ref, gain_ref, shift_ref, bias_ref, out_ref, wide_ref):
+    wide_ref[0:TOK, :] = rows_ref[...]
+    whole = jnp.concatenate(
+        [gain_ref[...], shift_ref[...], bias_ref[...], jnp.zeros((13, LANES), F32)], 0
+    )
+    high = whole.astype(BF16)
+    rest = whole - high.astype(F32)
+    middle = rest.astype(BF16)
+    low = (rest - middle.astype(F32)).astype(BF16)
+    wide_ref[TOK : TOK + 16, :] = high
+    wide_ref[TOK + 16 : TOK + 32, :] = middle
+    wide_ref[TOK + 32 : WIDE, :] = low
     order = order_ref[...]
     row, col = order >> 9, order & 511
     owner = (row >> 3) * 8 + (col >> 6)
@@ -56,10 +69,11 @@
     for z in range(NZ):
         pick = jnp.where(iota((ROWS, TOK), 0) + z * ROWS == wanted, 1.0, 0.0).astype(BF16)
         out_ref[z, 0:ROWS, :] = jnp.dot(pick, rows, preferred_element_type=F32).astype(BF16)
-        out_ref[z, ROWS:SEND, :] = jnp.broadcast_to(meta[z : z + 1, :], (16, LANES)).astype(BF16)
-
-
-def conv_kernel(near_ref, far_ref, weight_ref, param_ref, out_ref, patch_ref):
+        out_ref[z, ROWS : ROWS + 16, :] = jnp.broadcast_to(meta[z : z + 1, :], (16, LANES)).astype(BF16)
+        out_ref[z, ROWS + 16 : SEND, :] = tail_ref[...]
+
+
+def place_kernel(near_ref, far_ref, out_ref, patch_ref):
     spot = (iota((TOK, LANES), 0) - 256).astype(F32)
     for owner in range(PLANE):
         total = None
@@ -74,10 +88,15 @@
                 )
                 total = part if total is None else total + part
         patch_ref[:, owner * BLK : owner * BLK + BLK, :] = total.reshape(PATCH, BLK, LANES)
+    out_ref[...] = patch_ref[...].astype(BF16)
+
+
+def conv_kernel(patch_ref, weight_ref, tail_ref, out_ref):
     acc = jnp.zeros((256, 256), F32)
     for quad in range(16):
-        left = weight_ref[:, quad * 16 : quad * 16 + 16, :].reshape(256, LANES)
-        right = patch_ref[quad * 4 : quad * 4 + 4, :, :].astype(BF16).reshape(256, LANES)
+        ref = weight_ref.at[:, quad * 16 : quad * 16 + 16, :] if quad < 15 else tail_ref
+        left = ref[...].reshape(256, LANES)
+        right = patch_ref[quad * 4 : quad * 4 + 4, :, :].reshape(256, LANES)
         acc = acc + lax.dot_general(right, left, NT, preferred_element_type=F32)
     column = iota((64, 256), 1)
     kept = jnp.zeros((64, 256), F32)
@@ -86,27 +105,48 @@
             ((column >> 2) & 3) == step, acc[step * 64 : step * 64 + 64, :], 0.0
         )
     source, lane = iota((256, LANES), 0), iota((256, LANES), 1)
-    merge = jnp.where(((source >> 4) * 4 + (source & 3)) == lane, 1.0, 0.0)
-    sums = jnp.dot(
-        kept, merge, precision=lax.Precision.HIGHEST, preferred_element_type=F32
-    )
-    sent = sums.reshape(PLANE, BLK, LANES) + param_ref[...][None]
-    for head in range(NH):
-        out_ref[:, head] = sent
-
-
-def norm_kernel(sums_ref, key_ref, value_ref, out_ref):
-    left = iota((BLK, LANES), 1) < 64
+    from_lane = (source >> 4) * 4 + (source & 3)
+    lower = jnp.where(from_lane == lane, 1.0, 0.0)
+    upper = jnp.where(from_lane + 64 == lane, 1.0, 0.0)
+
+    def merge(rows, hits):
+        return jnp.dot(rows, hits, precision=lax.Precision.HIGHEST, preferred_element_type=F32)
+
+    low = merge(kept, lower).reshape(NX, NC, BLK, LANES)
+    high = merge(kept, upper).reshape(NX, NC, BLK, LANES)
+    for c in range(NC):
+        sent = (low[0:2, c] + high[2:4, c]).reshape(16, LANES)
+        for x in range(NX):
+            for head in range(NH):
+                out_ref[x, c, head] = sent
+
+
+def norm_kernel(sums_ref, wide_ref, key_ref, value_ref, out_ref):
+    count = 32
+    left = iota((count, LANES), 1) < 64
+    source, lane = iota((LANES, LANES), 0), iota((LANES, LANES), 1)
+    hits = [(lane == (source >> 2) * 8 + c * 4 + (source & 3)) & (source < 64) for c in range(NC)]
+    backs = [(source == (lane >> 2) * 8 + c * 4 + (lane & 3)) & (lane < 64) for c in range(NC)]
     shares, gains, biases = [], [], []
     for x in range(NX):
+        whole = (
+            wide_ref[x, TOK : TOK + 16, :].astype(F32)
+            + wide_ref[x, TOK + 16 : TOK + 32, :].astype(F32)
+        ) + wide_ref[x, TOK + 32 : WIDE, :].astype(F32)
         for c in range(NC):
             total = sums_ref[x, c, 0]
             for head in range(1, NH):
                 total = total + sums_ref[x, c, head]
-            extra = pltpu.roll(sums_ref[x, c, x], 64, 1)
-            gains.append(extra[c : c + 1, :])
-            biases.append(extra[2 + c : 3 + c, :])
-            shares.append(jnp.where(left, total + extra[4 + c : 5 + c, :], 0.0))
+            total = jnp.concatenate([total, pltpu.roll(total, 64, 1)], 0)
+            extra = jnp.dot(
+                whole,
+                jnp.where(backs[c], 1.0, 0.0),
+                precision=lax.Precision.HIGHEST,
+                preferred_element_type=F32,
+            )
+            gains.append(extra[0:1, :])
+            biases.append(extra[1:2, :])
+            shares.append(jnp.where(left, total + extra[2:3, :], 0.0))
     first = shares[0]
     second = shares[0] * shares[0]
     for share in shares[1:]:
@@ -115,21 +155,19 @@
     center = jnp.sum(first, 1, keepdims=True) * (1.0 / 512)
     spread = jnp.sum(second, 1, keepdims=True) * (1.0 / 512)
     scale = lax.rsqrt(spread - center * center + 1e-05)
-    keys = jnp.zeros((BLK, LANES), F32)
-    values = jnp.zeros((BLK, LANES), F32)
-    source, lane = iota((LANES, LANES), 0), iota((LANES, LANES), 1)
+    keys = jnp.zeros((count, LANES), F32)
+    values = jnp.zeros((count, LANES), F32)
     for x in range(NX):
-        spread_out = None
+        natural = None
         for c in range(NC):
             index = x * NC + c
             normed = (shares[index] - center) * scale * gains[index] + biases[index]
             normed = jnp.where(left, normed, 0.0).astype(BF16)
-            hit = (lane == (source >> 2) * 8 + c * 4 + (source & 3)) & (source < 64)
             part = jnp.dot(
-                normed, jnp.where(hit, 1.0, 0.0).astype(BF16), preferred_element_type=F32
+                normed, jnp.where(hits[c], 1.0, 0.0).astype(BF16), preferred_element_type=F32
             )
-            spread_out = part if spread_out is None else spread_out + part
-        natural = spread_out.astype(BF16)
+            natural = part if natural is None else natural + part
+        natural = natural.astype(BF16)
         keys = keys + jnp.dot(
             natural, key_ref[x * 128 : x * 128 + 128, :], preferred_element_type=F32
         )
@@ -145,7 +183,7 @@
     total = None
     for head in range(NH):
         part = jnp.dot(
-            features_ref[head],
+            features_ref[head, 0:TOK, :],
             weight_ref[head * 128 : head * 128 + 128, :],
             preferred_element_type=F32,
         )
@@ -193,13 +231,26 @@
 ):
     shape = jax.ShapeDtypeStruct
     turned = conv_weight.transpose(1, 0, 2).reshape(256, LANES)
-    weights = lax.all_gather(turned, "z", axis=0, tiled=True).reshape(NZ, 256, LANES)
-    sorted_rows = pl.pallas_call(
+    sorted_rows, wide = pl.pallas_call(
         route_kernel,
-        out_shape=shape((NZ, SEND, LANES), BF16),
+        out_shape=(shape((NZ, SEND, LANES), BF16), shape((WIDE, LANES), BF16)),
         compiler_params=params(32),
-    )(tile_rows, tile_order.reshape(1, TOK), tissue_mask.reshape(1, TOK))
+    )(
+        tile_rows,
+        tile_order.reshape(1, TOK),
+        tissue_mask.reshape(1, TOK),
+        turned[MOST:],
+        norm_gain.reshape(1, LANES),
+        norm_bias.reshape(1, LANES),
+        conv_bias.reshape(1, LANES),
+    )
     arrived = lax.all_to_all(sorted_rows, "z", split_axis=0, concat_axis=0, tiled=True)
+    features = lax.all_gather(wide, "head", axis=0)
+    queries = pl.pallas_call(
+        query_kernel, out_shape=shape((TOK, LANES), BF16), compiler_params=params(32)
+    )(features, query_weight)
+    arrived, most, queries = lax.optimization_barrier((arrived, turned[:MOST], queries))
+    weights = lax.all_gather(most, "z", axis=0, tiled=True).reshape(NZ, MOST, LANES)
     payload = arrived[:, :ROWS].reshape(NZ, PLANE, SLOTS, LANES).transpose(1, 0, 2, 3)
     places = arrived[:, ROWS, :ROWS].reshape(NZ, PLANE, SLOTS).transpose(1, 0, 2)
     places = jnp.pad(places.reshape(PLANE, LANES), ((0, 8), (0, 0)))
@@ -207,33 +258,31 @@
     near = lax.all_to_all(
         jnp.broadcast_to(here[None], (NX,) + here.shape), "x", split_axis=0, concat_axis=0, tiled=True
     )
+    near, weights = lax.optimization_barrier((near, weights))
     far = lax.ppermute(near, "core", [(0, 1), (1, 0)])
-    features = lax.all_gather(tile_rows, "head", axis=0)
-    queries = pl.pallas_call(
-        query_kernel, out_shape=shape((TOK, LANES), BF16), compiler_params=params(32)
-    )(features, query_weight)
-    extra = jnp.stack([norm_gain, norm_bias, conv_bias]).reshape(3, NZ, NC, 4)
-    extra = jnp.pad(extra.transpose(0, 2, 1, 3).reshape(6, 64), ((0, 2), (64, 0)))
+    patches = pl.pallas_call(
+        place_kernel,
+        out_shape=shape((PATCH, 64, LANES), BF16),
+        scratch_shapes=[pltpu.VMEM((PATCH, 64, LANES), F32)],
+        compiler_params=params(48),
+    )(near, far)
     partial = pl.pallas_call(
         conv_kernel,
-        out_shape=shape((PLANE, NH, BLK, LANES), F32),
-        scratch_shapes=[pltpu.VMEM((PATCH, 64, LANES), F32)],
+        out_shape=shape((NX, NC, NH, 16, LANES), F32),
         compiler_params=params(48),
-    )(near, far, weights, extra)
+    )(patches, weights, arrived[:, ROWS + 16 :])
     sums = lax.all_to_all(
-        partial.reshape(PLANE * NH, BLK, LANES),
+        partial.reshape(PLANE * NH, 16, LANES),
         ("x", "core", "head"),
         split_axis=0,
         concat_axis=0,
         tiled=True,
     )
     key_value = pl.pallas_call(
-        norm_kernel, out_shape=shape((NZ, BLK, 256), BF16), compiler_params=params(32)
-    )(sums.reshape(NX, NC, NH, BLK, LANES), key_weight, value_weight)
+        norm_kernel, out_shape=shape((NZ, 32, 256), BF16), compiler_params=params(32)
+    )(sums.reshape(NX, NC, NH, 16, LANES), features, key_weight, value_weight)
     gathered = lax.all_to_all(key_value, "z", split_axis=0, concat_axis=0, tiled=True)
-    gathered = gathered.reshape(NZ * BLK, 256)
-    gathered = lax.all_gather(gathered, "x", axis=0, tiled=True)
-    gathered = lax.all_gather(gathered, "core", axis=0, tiled=True)
+    gathered = lax.all_gather(gathered.reshape(NZ * 32, 256), "core", axis=0, tiled=True)
     parts = pl.pallas_call(
         attend_kernel, out_shape=shape((NH, TOK, LANES), BF16), compiler_params=params(48)
     )(queries, gathered, out_weight)

time: 184 us -> 157 us (0.85)
  waiting for transfers between devices: 49.9 us -> 16.4 us
  blocking collectives: 66 us -> 86.7 us
  between operations: 13.6 us -> 0.15 us
    all_gather x1 -> x0, waiting for transfers between devices: 25.5 us -> none  [local(): lax.all_gather(turned, 'z', axis=0, tiled=True).reshape(NZ, 256, LANES)]
    all_gather x3, blocking collectives: 27.5 us -> 51.6 us  [the longest x1 32.2 us: local(): lax.all_gather(most, 'z', axis=0, tiled=True).reshape(NZ, MOST, LANES)]
    all_to_all x1, waiting for transfers between devices: 14.5 us -> 4.94 us  [local(): lax.all_to_all(sorted_rows, 'z', split_axis=0, concat_axis=0, tiled=True)]
    all_to_all x1, starting transfers between devices: 7.54 us -> 4.01 us  [local(): lax.all_to_all(jnp.broadcast_to(here[None], (NX,) + here.shape), 'x', spl...]
    all_to_all x2, blocking collectives: 38.5 us -> 35.1 us  [the longest x1 18.5 us: local(): lax.all_to_all(key_value, 'z', split_axis=0, concat_axis=0, tiled=True)]
    ppermute x1, starting transfers between devices: 9.75 us -> 12.1 us  [local(): far = lax.ppermute(near, 'core', [(0, 1), (1, 0)])]
    ppermute x1, waiting for transfers between devices: 0.01 us -> 2.27 us  [local(): far = lax.ppermute(near, 'core', [(0, 1), (1, 0)])]
    pallas_call x3 -> x4, Pallas kernels: 6.93 us -> 6.13 us  [the longest x1 2.31 us: local(): pl.pallas_call(place_kernel, out_shape=shape((PATCH, 64, LANES), BF16), s...]
  transfers between devices with their start and end apart: 5 -> 4, of which waited for: 4 -> 3; matrix products, arithmetic and copies ran while one was open for 1% -> 1% of each run, Pallas kernels for 0% -> 0%
where the time goes in v2:
time: 157 us; the launch traced here: 156 us
  blocking collectives  86.7 us (55%)
  starting transfers between devices  35.4 us (23%)
  waiting for transfers between devices  16.4 us (10%)
  Pallas kernels  9.55 us (6%)
  local copies, waits for them, and re-layouts  7.4 us (5%)
    all_gather x1, blocking collectives, local(): lax.all_gather(most, 'z', axis=0, tiled=True).reshape(NZ, MOST, LANES)  32.2 us
    all_to_all x1, blocking collectives, local(): lax.all_to_all(key_value, 'z', split_axis=0, concat_axis=0, tiled=True)  18.5 us
    all_to_all x1, blocking collectives, local(): lax.all_to_all(partial.reshape(PLANE * NH, 16, LANES), ('x', 'core', 'hea...  16.6 us
    all_to_all x1, starting transfers between devices, local(): lax.all_to_all(sorted_rows, 'z', split_axis=0, concat_axis=0, tiled=True)  15.8 us
    ppermute x1, starting transfers between devices, local(): far = lax.ppermute(near, 'core', [(0, 1), (1, 0)])  12.1 us
    all_gather x1, blocking collectives, local(): features = lax.all_gather(wide, 'head', axis=0)  11.9 us
    all_to_all x1, waiting for transfers between devices, local(): lax.all_to_all(parts, 'head', split_axis=0, concat_axis=0, tiled=True)  9.17 us
    all_gather x1, blocking collectives, local(): lax.all_gather(gathered.reshape(NZ * 32, 256), 'core', axis=0, tiled=True)  7.52 us
  transfers between devices with their start and end apart: 4, of which 3 were waited for; matrix products, arithmetic and copies ran while one was open for 1% of the time, Pallas kernels for 0%

profile of v2, /device:TPU:1, one launch (start us, length us, event | category | flops | bytes accessed | tf_op | source)
XLA Modules:
  0.0 156.4 jit_solution(18421676140073286144)
XLA Ops:
  0.0 0.7 slice.28
  0.8 0.9 copy-done.2
  1.7 0.7 copy-done.5
  2.3 0.7 copy-done.7
  5.0 1.5 shard_map.109
  6.5 15.8 %all-to-all-start = ((bf16[16,96,128]{2,1,0:T(8,128)(2,1)}), bf16[16,96,128]{2,1,0:T(8,128)(2,1)S(1)}, u32[]{:S(2)}, u32[]{:S(2)}) async-start(bf16[16,96,128]{2,1,0:T(8,128)(2,1)} %get-tuple-element.12), calls=%async_computation | async-start | bytes 786432 | tf_op jit(solution)/shard_map/all_to_all | solution.py:247
  22.3 0.9 copy.14
  23.2 11.9 %all-gather = bf16[2240,128]{1,0:T(8,128)(2,1)S(1)} all-gather(bf16[560,128]{1,0:T(8,128)(2,1)S(1)} %get-tuple-element.13), channel_id=2, replica_groups=mesh['x'=4,'z'=16,'core'=2,'head'=4] {'head'}, dimensions={0}, use_global_device_ids=true | all-gather | bytes 716800 | tf_op jit(solution)/shard_map/all_gather | solution.py:248
  35.3 4.9 %all-to-all-done = bf16[16,96,128]{2,1,0:T(8,128)(2,1)S(1)} async-done(((bf16[16,96,128]{2,1,0:T(8,128)(2,1)}), bf16[16,96,128]{2,1,0:T(8,128)(2,1)S(1)}, u32[]{:S(2)}, u32[]{:S(2)}) %all-to-all-start) | async-done | bytes 393248 | tf_op jit(solution)/shard_map/all_to_all | solution.py:247
  40.7 1.1 broadcast_in_dim.2
  41.8 4.0 %all-to-all-start.1 = ((bf16[4,1040,128]{2,1,0:T(8,128)(2,1)}), bf16[4,1040,128]{2,1,0:T(8,128)(2,1)S(1)}, u32[]{:S(2)}, u32[]{:S(2)}) async-start(bf16[4,1040,128]{2,1,0:T(8,128)(2,1)} %broadcast_in_dim.2), calls=%async_computation.1 | async-start | bytes 2129920 | tf_op jit(solution)/shard_map/all_to_all | solution.py:258
  45.8 32.2 %all_gather.14 = bf16[3840,128]{1,0:T(8,128)(2,1)S(1)} all-gather(bf16[240,128]{1,0:T(8,128)(2,1)S(1)} %bitcast.35), channel_id=1, replica_groups=mesh['x'=4,'z'=16,'core'=2,'head'=4] {'z'}, dimensions={0}, use_global_device_ids=true | all-gather | bytes 1044480 | tf_op jit(solution)/shard_map/all_gather | solution.py:253
  78.0 12.1 %collective-permute-start = (bf16[4,1040,128]{2,1,0:T(8,128)(2,1)S(1)}, bf16[4,1040,128]{2,1,0:T(8,128)(2,1)S(1)}, u32[]{:S(2)}, u32[]{:S(2)}) collective-permute-start(bf16[4,1040,128]{2,1,0:T(8,128)(2,1)S(1)} %all-to-all-done.1.near_ref), channel_id=1, source_target_pairs={{0,4},{4,0},{1,5},{5,1},{2,6},{6,2},{3,7},{7,3},{8,12},{12,8},{9,1... | collective-permute-start | bytes 3194888 | tf_op jit(solution)/shard_map/ppermute | solution.py:262
  90.2 2.3 %collective-permute-done.far_ref = bf16[4,1040,128]{2,1,0:T(8,128)(2,1)S(1)} collective-permute-done((bf16[4,1040,128]{2,1,0:T(8,128)(2,1)S(1)}, bf16[4,1040,128]{2,1,0:T(8,128)(2,1)S(1)}, u32[]{:S(2)}, u32[]{:S(2)}) %collective-permute-start) | collective-permute-done | bytes 1064992 | tf_op jit(solution)/shard_map/ppermute | solution.py:262
  92.5 2.3 %shard_map.111.patch_ref = bf16[64,64,128]{2,1,0:T(8,128)(2,1)S(1)} custom-call(bf16[4,1040,128]{2,1,0:T(8,128)(2,1)S(1)} %all-to-all-done.1.near_ref, bf16[4,1040,128]{2,1,0:T(8,128)(2,1)S(1)} %collective-permute-done.far_ref), custom_call_target="tpu_custom_call" | custom-call | tf_op jit(solution)/shard_map/pallas_call | solution.py:263
  94.8 1.1 shard_map.112
  95.9 16.6 %all_to_all.25 = f32[32,16,128]{2,1,0:T(8,128)S(1)} all-to-all(f32[32,16,128]{2,1,0:T(8,128)S(1)} %bitcast.25), channel_id=1, replica_groups=mesh['x'=4,'z'=16,'core'=2,'head'=4] {'x','core','head'}, dimensions={0} | all-to-all | bytes 524288 | tf_op jit(solution)/shard_map/all_to_all | solution.py:274
  112.5 1.2 shard_map.113
  113.7 18.5 %all_to_all.26 = bf16[16,32,256]{2,1,0:T(8,128)(2,1)S(1)} all-to-all(bf16[16,32,256]{2,1,0:T(8,128)(2,1)S(1)} %shard_map.113), channel_id=1, replica_groups=mesh['x'=4,'z'=16,'core'=2,'head'=4] {'z'}, dimensions={0} | all-to-all | bytes 524288 | tf_op jit(solution)/shard_map/all_to_all | solution.py:284
  132.2 7.5 %all_gather.15.key_value_ref = bf16[1024,256]{1,0:T(8,128)(2,1)S(1)} all-gather(bf16[512,256]{1,0:T(8,128)(2,1)S(1)} %bitcast.33), channel_id=1, replica_groups=mesh['x'=4,'z'=16,'core'=2,'head'=4] {'core'}, dimensions={0}, use_global_device_ids=true | all-gather | bytes 786432 | tf_op jit(solution)/shard_map/all_gather | solution.py:285
  139.8 3.1 %shard_map.114 = bf16[4,512,128]{2,1,0:T(8,128)(2,1)} custom-call(bf16[512,128]{1,0:T(8,128)(2,1)S(1)} %shard_map.110.query_ref, bf16[1024,256]{1,0:T(8,128)(2,1)S(1)} %all_gather.15.key_value_ref, bf16[128,512]{1,0:T(8,128)(2,1)S(1)} %copy-done.1), custom_call_target="tpu_custom_call" | custom-call | tf_op jit(solution)/shard_map/pallas_call | solution.py:286
  142.9 3.5 %all-to-all-start.4 = ((bf16[4,512,128]{2,1,0:T(8,128)(2,1)}), bf16[4,512,128]{2,1,0:T(8,128)(2,1)S(1)}, u32[]{:S(2)}, u32[]{:S(2)}) async-start(bf16[4,512,128]{2,1,0:T(8,128)(2,1)} %shard_map.114), calls=%async_computation.4 | async-start | bytes 1048576 | tf_op jit(solution)/shard_map/all_to_all | solution.py:289
  146.4 9.2 %all-to-all-done.4 = bf16[4,512,128]{2,1,0:T(8,128)(2,1)S(1)} async-done(((bf16[4,512,128]{2,1,0:T(8,128)(2,1)}), bf16[4,512,128]{2,1,0:T(8,128)(2,1)S(1)}, u32[]{:S(2)}, u32[]{:S(2)}) %all-to-all-start.4) | async-done | bytes 524320 | tf_op jit(solution)/shard_map/all_to_all | solution.py:289
  155.6 0.8 multiply_convert_fusion
  (32 shorter events, 2.8 us)
Async XLA Ops:
  0.0 35.0 %copy-start = (bf16[512,128]{1,0:T(8,128)(2,1)S(1)}, bf16[512,128]{1,0:T(8,128)(2,1)}, u32[]{:S(2)}) copy-start(bf16[512,128]{1,0:T(8,128)(2,1)} %weight_ref.2) | copy-start | bytes 393220
  0.7 0.9 copy-start.2
  1.7 0.7 copy-start.5
  2.3 0.7 copy-start.7
  3.0 0.7 copy-start.8
  3.7 0.7 copy-start.9
  4.3 0.7 copy-start.10
  6.5 33.8 %all-to-all-start = ((bf16[16,96,128]{2,1,0:T(8,128)(2,1)}), bf16[16,96,128]{2,1,0:T(8,128)(2,1)S(1)}, u32[]{:S(2)}, u32[]{:S(2)}) async-start(bf16[16,96,128]{2,1,0:T(8,128)(2,1)} %get-tuple-element.12), calls=%async_computation | async-start | bytes 786432 | tf_op jit(solution)/shard_map/all_to_all | solution.py:247
  41.8 36.2 %all-to-all-start.1 = ((bf16[4,1040,128]{2,1,0:T(8,128)(2,1)}), bf16[4,1040,128]{2,1,0:T(8,128)(2,1)S(1)}, u32[]{:S(2)}, u32[]{:S(2)}) async-start(bf16[4,1040,128]{2,1,0:T(8,128)(2,1)} %broadcast_in_dim.2), calls=%async_computation.1 | async-start | bytes 2129920 | tf_op jit(solution)/shard_map/all_to_all | solution.py:258
  78.0 14.4 %collective-permute-start = (bf16[4,1040,128]{2,1,0:T(8,128)(2,1)S(1)}, bf16[4,1040,128]{2,1,0:T(8,128)(2,1)S(1)}, u32[]{:S(2)}, u32[]{:S(2)}) collective-permute-start(bf16[4,1040,128]{2,1,0:T(8,128)(2,1)S(1)} %all-to-all-done.1.near_ref), channel_id=1, source_target_pairs={{0,4},{4,0},{1,5},{5,1},{2,6},{6,2},{3,7},{7,3},{8,12},{12,8},{9,1... | collective-permute-start | bytes 3194888 | tf_op jit(solution)/shard_map/ppermute | solution.py:262
  94.8 17.7 %copy-start.3 = (bf16[512,128]{1,0:T(8,128)(2,1)S(1)}, bf16[512,128]{1,0:T(8,128)(2,1)}, u32[]{:S(2)}) copy-start(bf16[512,128]{1,0:T(8,128)(2,1)} %key_ref.1) | copy-start | bytes 393220
  94.8 17.7 %copy-start.4 = (bf16[512,128]{1,0:T(8,128)(2,1)S(1)}, bf16[512,128]{1,0:T(8,128)(2,1)}, u32[]{:S(2)}) copy-start(bf16[512,128]{1,0:T(8,128)(2,1)} %value_ref.1) | copy-start | bytes 393220
  112.5 27.2 %copy-start.1 = (bf16[128,512]{1,0:T(8,128)(2,1)S(1)}, bf16[128,512]{1,0:T(8,128)(2,1)}, u32[]{:S(2)}) copy-start(bf16[128,512]{1,0:T(8,128)(2,1)} %weight_ref.3) | copy-start | bytes 393220
  139.8 6.6 %copy-start.6 = (s32[512]{0:T(512)S(1)}, s32[512]{0:T(512)}, u32[]{:S(2)}) copy-start(s32[512]{0:T(512)} %param.13) | copy-start | bytes 6148
  142.9 12.7 %all-to-all-start.4 = ((bf16[4,512,128]{2,1,0:T(8,128)(2,1)}), bf16[4,512,128]{2,1,0:T(8,128)(2,1)S(1)}, u32[]{:S(2)}, u32[]{:S(2)}) async-start(bf16[4,512,128]{2,1,0:T(8,128)(2,1)} %shard_map.114), calls=%async_computation.4 | async-start | bytes 1048576 | tf_op jit(solution)/shard_map/all_to_all | solution.py:289

commit v3 on v2

--- a/solution.py
+++ b/solution.py
@@ -12,9 +12,9 @@
 PLANE = NX * NC
 SLOTS = 8
 ROWS = PLANE * SLOTS
-SEND = ROWS + 32
+SEND = ROWS + 16
 TOK = 512
-MOST = 240
+MOST = 248
 WIDE = TOK + 48
 LANES = 128
 BLK = 8
@@ -33,7 +33,31 @@
     return lax.broadcasted_iota(jnp.int32, shape, dim)
 
 
-def route_kernel(rows_ref, order_ref, mask_ref, tail_ref, gain_ref, shift_ref, bias_ref, out_ref, wide_ref):
+def route_kernel(
+    rows_hbm, order_hbm, mask_hbm, kernel_hbm, gain_hbm, shift_hbm, bias_hbm,
+    out_ref, wide_ref, most_ref,
+    rows_ref, order_ref, mask_ref, kernel_ref, gain_ref, shift_ref, bias_ref, sems,
+):
+    pairs = (
+        (order_hbm, order_ref),
+        (mask_hbm, mask_ref),
+        (rows_hbm, rows_ref),
+        (kernel_hbm, kernel_ref),
+        (gain_hbm, gain_ref),
+        (shift_hbm, shift_ref),
+        (bias_hbm, bias_ref),
+    )
+    copies = [
+        pltpu.make_async_copy(source, held, sems.at[index])
+        for index, (source, held) in enumerate(pairs)
+    ]
+    for copy in copies:
+        copy.start()
+    before = jnp.where(iota((TOK, TOK), 0) < iota((TOK, TOK), 1), 1.0, 0.0).astype(BF16)
+    row256, lane256 = iota((256, 256), 0), iota((256, 256), 1)
+    turn = jnp.where(lane256 == (row256 & 3) * PATCH + (row256 >> 2), 1.0, 0.0).astype(BF16)
+    for copy in copies:
+        copy.wait()
     wide_ref[0:TOK, :] = rows_ref[...]
     whole = jnp.concatenate(
         [gain_ref[...], shift_ref[...], bias_ref[...], jnp.zeros((13, LANES), F32)], 0
@@ -45,6 +69,9 @@
     wide_ref[TOK : TOK + 16, :] = high
     wide_ref[TOK + 16 : TOK + 32, :] = middle
     wide_ref[TOK + 32 : WIDE, :] = low
+    turned = jnp.dot(turn, kernel_ref[...], preferred_element_type=F32)
+    most_ref[...] = turned[0:MOST, :].astype(BF16)
+    tail = jnp.concatenate([turned[MOST:256, :], turned[MOST:256, :]], 0)
     order = order_ref[...]
     row, col = order >> 9, order & 511
     owner = (row >> 3) * 8 + (col >> 6)
@@ -53,7 +80,6 @@
     target = ((row & 7) * 8 + (col & 7)) * BLK + ((col >> 3) & 7)
     code = plane * PLANE + place
     onehot = jnp.where(iota((128, TOK), 0) == code, 1.0, 0.0)
-    before = jnp.where(iota((TOK, TOK), 0) < iota((TOK, TOK), 1), 1.0, 0.0).astype(BF16)
     counts = jnp.dot(onehot.astype(BF16), before, preferred_element_type=F32)
     rank = jnp.sum(onehot * counts, 0, keepdims=True).astype(jnp.int32)
     slot = place * SLOTS + rank
@@ -66,37 +92,42 @@
     meta = jnp.where(valid > 0.5, values, EMPTY)
     wanted = jnp.where(mask_ref[...] != 0, plane * ROWS + slot, -1)
     rows = rows_ref[...]
+    top = iota((16, LANES), 0) < 8
     for z in range(NZ):
         pick = jnp.where(iota((ROWS, TOK), 0) + z * ROWS == wanted, 1.0, 0.0).astype(BF16)
         out_ref[z, 0:ROWS, :] = jnp.dot(pick, rows, preferred_element_type=F32).astype(BF16)
-        out_ref[z, ROWS : ROWS + 16, :] = jnp.broadcast_to(meta[z : z + 1, :], (16, LANES)).astype(BF16)
-        out_ref[z, ROWS + 16 : SEND, :] = tail_ref[...]
-
-
-def place_kernel(near_ref, far_ref, out_ref, patch_ref):
+        last = jnp.where(top, jnp.broadcast_to(meta[z : z + 1, :], (16, LANES)), tail)
+        out_ref[z, ROWS:SEND, :] = last.astype(BF16)
+
+
+def conv_kernel(tile_ref, weight_ref, tail_ref, out_ref, patch_ref):
     spot = (iota((TOK, LANES), 0) - 256).astype(F32)
+    metas = [
+        tile_ref[x, c, PLANE * 128 : PLANE * 128 + 16, :].astype(F32)
+        for x in range(NX)
+        for c in range(NC)
+    ]
     for owner in range(PLANE):
         total = None
-        for ref in (near_ref, far_ref):
-            for x in range(NX):
-                meta = ref[x, PLANE * 128 : PLANE * 128 + 16, :].astype(F32)[owner : owner + 1, :]
-                pick = jnp.where(spot == meta, 1.0, 0.0).astype(BF16)
+        for x in range(NX):
+            for c in range(NC):
+                pick = jnp.where(spot == metas[x * NC + c][owner : owner + 1, :], 1.0, 0.0)
                 part = jnp.dot(
-                    pick,
-                    ref[x, owner * 128 : owner * 128 + 128, :],
+                    pick.astype(BF16),
+                    tile_ref[x, c, owner * 128 : owner * 128 + 128, :],
                     preferred_element_type=F32,
                 )
                 total = part if total is None else total + part
         patch_ref[:, owner * BLK : owner * BLK + BLK, :] = total.reshape(PATCH, BLK, LANES)
-    out_ref[...] = patch_ref[...].astype(BF16)
-
-
-def conv_kernel(patch_ref, weight_ref, tail_ref, out_ref):
     acc = jnp.zeros((256, 256), F32)
     for quad in range(16):
-        ref = weight_ref.at[:, quad * 16 : quad * 16 + 16, :] if quad < 15 else tail_ref
-        left = ref[...].reshape(256, LANES)
-        right = patch_ref[quad * 4 : quad * 4 + 4, :, :].reshape(256, LANES)
+        if quad < 15:
+            left = weight_ref[:, quad * 16 : quad * 16 + 16, :]
+        else:
+            most = weight_ref[:, quad * 16 : MOST, :].astype(F32)
+            left = jnp.concatenate([most, tail_ref[...].astype(F32)], 1).astype(BF16)
+        left = left.reshape(256, LANES)
+        right = patch_ref[quad * 4 : quad * 4 + 4, :, :].astype(BF16).reshape(256, LANES)
         acc = acc + lax.dot_general(right, left, NT, preferred_element_type=F32)
     column = iota((64, 256), 1)
     kept = jnp.zeros((64, 256), F32)
@@ -230,16 +261,31 @@
     out_weight,
 ):
     shape = jax.ShapeDtypeStruct
-    turned = conv_weight.transpose(1, 0, 2).reshape(256, LANES)
-    sorted_rows, wide = pl.pallas_call(
+    hbm = pl.BlockSpec(memory_space=pl.ANY)
+    sorted_rows, wide, most = pl.pallas_call(
         route_kernel,
-        out_shape=(shape((NZ, SEND, LANES), BF16), shape((WIDE, LANES), BF16)),
-        compiler_params=params(32),
+        out_shape=(
+            shape((NZ, SEND, LANES), BF16),
+            shape((WIDE, LANES), BF16),
+            shape((MOST, LANES), BF16),
+        ),
+        in_specs=[hbm] * 7,
+        scratch_shapes=[
+            pltpu.VMEM((TOK, LANES), BF16),
+            pltpu.VMEM((1, TOK), jnp.int32),
+            pltpu.VMEM((1, TOK), jnp.int32),
+            pltpu.VMEM((256, LANES), BF16),
+            pltpu.VMEM((1, LANES), F32),
+            pltpu.VMEM((1, LANES), F32),
+            pltpu.VMEM((1, LANES), F32),
+            pltpu.SemaphoreType.DMA((7,)),
+        ],
+        compiler_params=params(60),
     )(
         tile_rows,
         tile_order.reshape(1, TOK),
         tissue_mask.reshape(1, TOK),
-        turned[MOST:],
+        conv_weight.reshape(256, LANES),
         norm_gain.reshape(1, LANES),
         norm_bias.reshape(1, LANES),
         conv_bias.reshape(1, LANES),
@@ -247,30 +293,25 @@
     arrived = lax.all_to_all(sorted_rows, "z", split_axis=0, concat_axis=0, tiled=True)
     features = lax.all_gather(wide, "head", axis=0)
     queries = pl.pallas_call(
-        query_kernel, out_shape=shape((TOK, LANES), BF16), compiler_params=params(32)
+        query_kernel, out_shape=shape((TOK, LANES), BF16), compiler_params=params(16)
     )(features, query_weight)
-    arrived, most, queries = lax.optimization_barrier((arrived, turned[:MOST], queries))
+    arrived, most, queries = lax.optimization_barrier((arrived, most, queries))
     weights = lax.all_gather(most, "z", axis=0, tiled=True).reshape(NZ, MOST, LANES)
-    payload = arrived[:, :ROWS].reshape(NZ, PLANE, SLOTS, LANES).transpose(1, 0, 2, 3)
-    places = arrived[:, ROWS, :ROWS].reshape(NZ, PLANE, SLOTS).transpose(1, 0, 2)
-    places = jnp.pad(places.reshape(PLANE, LANES), ((0, 8), (0, 0)))
-    here = jnp.concatenate([payload.reshape(PLANE * 128, LANES), places], 0)
-    near = lax.all_to_all(
+    both = lax.all_gather(arrived, "core", axis=0)
+    payload = both[:, :, :ROWS].reshape(NC, NZ, PLANE, SLOTS, LANES).transpose(0, 2, 1, 3, 4)
+    places = both[:, :, ROWS, :ROWS].reshape(NC, NZ, PLANE, SLOTS).transpose(0, 2, 1, 3)
+    places = jnp.pad(places.reshape(NC, PLANE, LANES), ((0, 0), (0, 8), (0, 0)))
+    here = jnp.concatenate([payload.reshape(NC, PLANE * 128, LANES), places], 1)
+    tiles = lax.all_to_all(
         jnp.broadcast_to(here[None], (NX,) + here.shape), "x", split_axis=0, concat_axis=0, tiled=True
     )
-    near, weights = lax.optimization_barrier((near, weights))
-    far = lax.ppermute(near, "core", [(0, 1), (1, 0)])
-    patches = pl.pallas_call(
-        place_kernel,
-        out_shape=shape((PATCH, 64, LANES), BF16),
-        scratch_shapes=[pltpu.VMEM((PATCH, 64, LANES), F32)],
-        compiler_params=params(48),
-    )(near, far)
+    tail = arrived[:, ROWS + 8 :]
     partial = pl.pallas_call(
         conv_kernel,
         out_shape=shape((NX, NC, NH, 16, LANES), F32),
-        compiler_params=params(48),
-    )(patches, weights, arrived[:, ROWS + 16 :])
+        scratch_shapes=[pltpu.VMEM((PATCH, 64, LANES), F32)],
+        compiler_params=params(24),
+    )(tiles, weights, tail)
     sums = lax.all_to_all(
         partial.reshape(PLANE * NH, 16, LANES),
         ("x", "core", "head"),
@@ -279,12 +320,12 @@
         tiled=True,
     )
     key_value = pl.pallas_call(
-        norm_kernel, out_shape=shape((NZ, 32, 256), BF16), compiler_params=params(32)
+        norm_kernel, out_shape=shape((NZ, 32, 256), BF16), compiler_params=params(16)
     )(sums.reshape(NX, NC, NH, 16, LANES), features, key_weight, value_weight)
     gathered = lax.all_to_all(key_value, "z", split_axis=0, concat_axis=0, tiled=True)
     gathered = lax.all_gather(gathered.reshape(NZ * 32, 256), "core", axis=0, tiled=True)
     parts = pl.pallas_call(
-        attend_kernel, out_shape=shape((NH, TOK, LANES), BF16), compiler_params=params(48)
+        attend_kernel, out_shape=shape((NH, TOK, LANES), BF16), compiler_params=params(24)
     )(queries, gathered, out_weight)
     parts = lax.all_to_all(parts, "head", split_axis=0, concat_axis=0, tiled=True)
     summed = jnp.sum(parts.astype(F32), 0)

time: 157 us -> 152 us (0.968)
  blocking collectives: 86.7 us -> 101 us
  starting transfers between devices: 35.4 us -> 23.4 us
  waiting for transfers between devices: 16.4 us -> 12 us
  local copies, waits for them, and re-layouts: 7.4 us -> 3.37 us
  Pallas kernels: 9.55 us -> 11.4 us
    ppermute x1 -> x0, starting transfers between devices: 12.1 us -> none  [local(): far = lax.ppermute(near, 'core', [(0, 1), (1, 0)])]
    all_gather x0 -> x1, blocking collectives: none -> 8.39 us  [local(): both = lax.all_gather(arrived, 'core', axis=0)]
    all_to_all x1, blocking collectives: 16.6 us -> 22.4 us  [local(): lax.all_to_all(partial.reshape(PLANE * NH, 16, LANES), ('x', 'core', 'hea...]
    pallas_call x1, Pallas kernels: 1.13 us -> 4.19 us  [local(): pl.pallas_call(conv_kernel, out_shape=shape((NX, NC, NH, 16, LANES), F32)...]
    unnamed x22 -> x14, local copies, waits for them, and re-layouts: 4.25 us -> 1.24 us
    pallas_call x1 -> x0, Pallas kernels: 2.31 us -> none  [local(): pl.pallas_call(place_kernel, out_shape=shape((PATCH, 64, LANES), BF16), s...]
    ppermute x1 -> x0, waiting for transfers between devices: 2.27 us -> none  [local(): far = lax.ppermute(near, 'core', [(0, 1), (1, 0)])]
    all_to_all x1, waiting for transfers between devices: 4.94 us -> 2.85 us  [local(): lax.all_to_all(sorted_rows, 'z', split_axis=0, concat_axis=0, tiled=True)]
  transfers between devices with their start and end apart: 4 -> 3, of which waited for: 3 -> 2; matrix products, arithmetic and copies ran while one was open for 1% -> 0% of each run, Pallas kernels for 0% -> 0%
where the time goes in v3:
time: 152 us
  blocking collectives  101 us (66%)
  starting transfers between devices  23.4 us (15%)
  waiting for transfers between devices  12 us (8%)
  Pallas kernels  11.4 us (8%)
  local copies, waits for them, and re-layouts  3.37 us (2%)
    all_gather x1, blocking collectives, local(): lax.all_gather(most, 'z', axis=0, tiled=True).reshape(NZ, MOST, LANES)  33 us
    all_to_all x1, blocking collectives, local(): lax.all_to_all(partial.reshape(PLANE * NH, 16, LANES), ('x', 'core', 'hea...  22.4 us
    all_to_all x1, blocking collectives, local(): lax.all_to_all(key_value, 'z', split_axis=0, concat_axis=0, tiled=True)  17.4 us
    all_to_all x1, starting transfers between devices, local(): lax.all_to_all(sorted_rows, 'z', split_axis=0, concat_axis=0, tiled=True)  15.8 us
    all_gather x1, blocking collectives, local(): features = lax.all_gather(wide, 'head', axis=0)  12.1 us
    all_to_all x1, waiting for transfers between devices, local(): lax.all_to_all(parts, 'head', split_axis=0, concat_axis=0, tiled=True)  9.17 us
    all_gather x1, blocking collectives, local(): both = lax.all_gather(arrived, 'core', axis=0)  8.39 us
    all_gather x1, blocking collectives, local(): lax.all_gather(gathered.reshape(NZ * 32, 256), 'core', axis=0, tiled=True)  7.52 us
  transfers between devices with their start and end apart: 3, of which 2 were waited for; matrix products, arithmetic and copies ran while one was open for 0% of the time, Pallas kernels for 0%

profile of v3, /device:TPU:1, one launch (start us, length us, event | category | flops | bytes accessed | tf_op | source)
XLA Modules:
  0.0 152.0 jit_solution(16845788740938294979)
XLA Ops:
  0.0 2.6 %shard_map.109 = (bf16[16,80,128]{2,1,0:T(8,128)(2,1)}, bf16[560,128]{1,0:T(8,128)(2,1)}, bf16[248,128]{1,0:T(8,128)(2,1)}) custom-call(bf16[512,128]{1,0:T(8,128)(2,1)} %rows_hbm.1, s32[1,512]{1,0:T(1,128)} %bitcast.34, s32[1,512]{1,0:T(1,128)} %bitcast.33, bf16[256,128]{1,0:T(8,128)(2,1)} %bitcast.32, f32[1,128]{1,0:T(1,128)} %bitcast.35, ...), custom_call_target="tpu_custom_call" | custom-call | tf_op jit(solution)/shard_map/pallas_call | solution.py:265
  2.6 15.8 %all-to-all-start = ((bf16[16,80,128]{2,1,0:T(8,128)(2,1)}), bf16[16,80,128]{2,1,0:T(8,128)(2,1)S(1)}, u32[]{:S(2)}, u32[]{:S(2)}) async-start(bf16[16,80,128]{2,1,0:T(8,128)(2,1)} %get-tuple-element.11), calls=%async_computation | async-start | bytes 655360 | tf_op jit(solution)/shard_map/all_to_all | solution.py:293
  18.4 12.1 %all-gather = bf16[2240,128]{1,0:T(8,128)(2,1)S(1)} all-gather(bf16[560,128]{1,0:T(8,128)(2,1)} %get-tuple-element.13), channel_id=2, replica_groups=mesh['x'=4,'z'=16,'core'=2,'head'=4] {'head'}, dimensions={0}, use_global_device_ids=true | all-gather | bytes 716800 | tf_op jit(solution)/shard_map/all_gather | solution.py:294
  30.5 0.3 shard_map.110.query_ref
  30.8 2.8 %all-to-all-done = bf16[16,80,128]{2,1,0:T(8,128)(2,1)S(1)} async-done(((bf16[16,80,128]{2,1,0:T(8,128)(2,1)}), bf16[16,80,128]{2,1,0:T(8,128)(2,1)S(1)}, u32[]{:S(2)}, u32[]{:S(2)}) %all-to-all-start) | async-done | bytes 327712 | tf_op jit(solution)/shard_map/all_to_all | solution.py:293
  33.6 8.4 %all-gather.1 = bf16[32,80,128]{2,1,0:T(8,128)(2,1)S(1)} all-gather(bf16[16,80,128]{2,1,0:T(8,128)(2,1)S(1)} %all-to-all-done), channel_id=3, replica_groups=mesh['x'=4,'z'=16,'core'=2,'head'=4] {'core'}, dimensions={0}, use_global_device_ids=true | all-gather | bytes 983040 | tf_op jit(solution)/shard_map/all_gather | solution.py:300
  42.1 0.1 copy.19
  42.2 0.1 copy.20
  42.3 0.1 copy.21
  42.4 0.1 reshape.50
  42.6 1.6 %broadcast_in_dim.2 = bf16[4,2,1040,128]{3,2,1,0:T(8,128)(2,1)} broadcast(bf16[2,1040,128]{2,1,0:T(8,128)(2,1)S(1)} %fusion.1), dimensions={1,2,3} | broadcast | bytes 2662400 | tf_op jit(solution)/shard_map/broadcast_in_dim | solution.py:306
  44.2 4.1 %all-to-all-start.1 = ((bf16[4,2,1040,128]{3,2,1,0:T(8,128)(2,1)}), bf16[4,2,1040,128]{3,2,1,0:T(8,128)(2,1)S(1)}, u32[]{:S(2)}, u32[]{:S(2)}) async-start(bf16[4,2,1040,128]{3,2,1,0:T(8,128)(2,1)} %broadcast_in_dim.2), calls=%async_computation.1 | async-start | bytes 4259840 | tf_op jit(solution)/shard_map/all_to_all | solution.py:305
  48.4 33.0 %all_gather.22 = bf16[3968,128]{1,0:T(8,128)(2,1)} all-gather(bf16[248,128]{1,0:T(8,128)(2,1)S(1)} %copy-done.5), channel_id=1, replica_groups=mesh['x'=4,'z'=16,'core'=2,'head'=4] {'z'}, dimensions={0}, use_global_device_ids=true | all-gather | bytes 1079296 | tf_op jit(solution)/shard_map/all_gather | solution.py:299
  81.4 1.2 copy-done
  82.6 4.2 %shard_map.111 = f32[4,2,4,16,128]{4,3,2,1,0:T(8,128)S(1)} custom-call(bf16[4,2,1040,128]{3,2,1,0:T(8,128)(2,1)S(1)} %all-to-all-done.1.tile_ref, bf16[16,248,128]{2,1,0:T(8,128)(2,1)S(1)} %bitcast.24, bf16[16,8,128]{2,1,0:T(8,128)(2,1)S(1)} %slice.11.tail_ref), custom_call_target="tpu_custom_call" | custom-call | tf_op jit(solution)/shard_map/pallas_call | solution.py:309
  86.8 22.4 %all_to_all.25 = f32[32,16,128]{2,1,0:T(8,128)S(1)} all-to-all(f32[32,16,128]{2,1,0:T(8,128)S(1)} %bitcast.26), channel_id=1, replica_groups=mesh['x'=4,'z'=16,'core'=2,'head'=4] {'x','core','head'}, dimensions={0} | all-to-all | bytes 524288 | tf_op jit(solution)/shard_map/all_to_all | solution.py:315
  109.2 1.2 shard_map.112
  110.4 17.4 %all_to_all.26 = bf16[16,32,256]{2,1,0:T(8,128)(2,1)S(1)} all-to-all(bf16[16,32,256]{2,1,0:T(8,128)(2,1)S(1)} %shard_map.112), channel_id=1, replica_groups=mesh['x'=4,'z'=16,'core'=2,'head'=4] {'z'}, dimensions={0} | all-to-all | bytes 524288 | tf_op jit(solution)/shard_map/all_to_all | solution.py:325
  127.8 7.5 %all_gather.23.key_value_ref = bf16[1024,256]{1,0:T(8,128)(2,1)S(1)} all-gather(bf16[512,256]{1,0:T(8,128)(2,1)S(1)} %bitcast.30), channel_id=1, replica_groups=mesh['x'=4,'z'=16,'core'=2,'head'=4] {'core'}, dimensions={0}, use_global_device_ids=true | all-gather | bytes 786432 | tf_op jit(solution)/shard_map/all_gather | solution.py:326
  135.3 3.1 %shard_map.113 = bf16[4,512,128]{2,1,0:T(8,128)(2,1)} custom-call(bf16[512,128]{1,0:T(8,128)(2,1)S(1)} %shard_map.110.query_ref, bf16[1024,256]{1,0:T(8,128)(2,1)S(1)} %all_gather.23.key_value_ref, bf16[128,512]{1,0:T(8,128)(2,1)S(1)} %copy-done.2), custom_call_target="tpu_custom_call" | custom-call | tf_op jit(solution)/shard_map/pallas_call | solution.py:327
  138.4 3.5 %all-to-all-start.4 = ((bf16[4,512,128]{2,1,0:T(8,128)(2,1)}), bf16[4,512,128]{2,1,0:T(8,128)(2,1)S(1)}, u32[]{:S(2)}, u32[]{:S(2)}) async-start(bf16[4,512,128]{2,1,0:T(8,128)(2,1)} %shard_map.113), calls=%async_computation.4 | async-start | bytes 1048576 | tf_op jit(solution)/shard_map/all_to_all | solution.py:330
  141.9 9.2 %all-to-all-done.4 = bf16[4,512,128]{2,1,0:T(8,128)(2,1)S(1)} async-done(((bf16[4,512,128]{2,1,0:T(8,128)(2,1)}), bf16[4,512,128]{2,1,0:T(8,128)(2,1)S(1)}, u32[]{:S(2)}, u32[]{:S(2)}) %all-to-all-start.4) | async-done | bytes 524320 | tf_op jit(solution)/shard_map/all_to_all | solution.py:330
  151.1 0.1 convert_reduce_fusion
  151.2 0.8 multiply_convert_fusion
  (19 shorter events, 0.1 us)
Async XLA Ops:
  0.0 30.5 %copy-start.1 = (bf16[512,128]{1,0:T(8,128)(2,1)S(1)}, bf16[512,128]{1,0:T(8,128)(2,1)}, u32[]{:S(2)}) copy-start(bf16[512,128]{1,0:T(8,128)(2,1)} %weight_ref.2) | copy-start | bytes 393220
  2.6 31.0 %all-to-all-start = ((bf16[16,80,128]{2,1,0:T(8,128)(2,1)}), bf16[16,80,128]{2,1,0:T(8,128)(2,1)S(1)}, u32[]{:S(2)}, u32[]{:S(2)}) async-start(bf16[16,80,128]{2,1,0:T(8,128)(2,1)} %get-tuple-element.11), calls=%async_computation | async-start | bytes 655360 | tf_op jit(solution)/shard_map/all_to_all | solution.py:293
  44.2 4.1 %copy-start.5 = (bf16[248,128]{1,0:T(8,128)(2,1)S(1)}, bf16[248,128]{1,0:T(8,128)(2,1)}, u32[]{:S(2)}) copy-start(bf16[248,128]{1,0:T(8,128)(2,1)} %get-tuple-element.16) | copy-start | bytes 190468
  44.2 37.1 %all-to-all-start.1 = ((bf16[4,2,1040,128]{3,2,1,0:T(8,128)(2,1)}), bf16[4,2,1040,128]{3,2,1,0:T(8,128)(2,1)S(1)}, u32[]{:S(2)}, u32[]{:S(2)}) async-start(bf16[4,2,1040,128]{3,2,1,0:T(8,128)(2,1)} %broadcast_in_dim.2), calls=%async_computation.1 | async-start | bytes 4259840 | tf_op jit(solution)/shard_map/all_to_all | solution.py:305
  81.4 1.2 copy-start
  82.6 26.6 %copy-start.3 = (bf16[512,128]{1,0:T(8,128)(2,1)S(1)}, bf16[512,128]{1,0:T(8,128)(2,1)}, u32[]{:S(2)}) copy-start(bf16[512,128]{1,0:T(8,128)(2,1)} %key_ref.1) | copy-start | bytes 393220
  82.6 26.6 %copy-start.4 = (bf16[512,128]{1,0:T(8,128)(2,1)S(1)}, bf16[512,128]{1,0:T(8,128)(2,1)}, u32[]{:S(2)}) copy-start(bf16[512,128]{1,0:T(8,128)(2,1)} %value_ref.1) | copy-start | bytes 393220
  109.2 26.1 %copy-start.2 = (bf16[128,512]{1,0:T(8,128)(2,1)S(1)}, bf16[128,512]{1,0:T(8,128)(2,1)}, u32[]{:S(2)}) copy-start(bf16[128,512]{1,0:T(8,128)(2,1)} %weight_ref.3) | copy-start | bytes 393220
  135.3 6.6 %copy-start.6 = (s32[512]{0:T(512)S(1)}, s32[512]{0:T(512)}, u32[]{:S(2)}) copy-start(s32[512]{0:T(512)} %param.13) | copy-start | bytes 6148
  138.4 12.7 %all-to-all-start.4 = ((bf16[4,512,128]{2,1,0:T(8,128)(2,1)}), bf16[4,512,128]{2,1,0:T(8,128)(2,1)S(1)}, u32[]{:S(2)}, u32[]{:S(2)}) async-start(bf16[4,512,128]{2,1,0:T(8,128)(2,1)} %shard_map.113), calls=%async_computation.4 | async-start | bytes 1048576 | tf_op jit(solution)/shard_map/all_to_all | solution.py:330

commit v4 on v3

--- a/solution.py
+++ b/solution.py
@@ -23,6 +23,7 @@
 F32 = jnp.float32
 BF16 = jnp.bfloat16
 NT = (((1,), (1,)), ((), ()))
+TN = (((0,), (0,)), ((), ()))
 
 
 def params(mib):
@@ -100,7 +101,7 @@
         out_ref[z, ROWS:SEND, :] = last.astype(BF16)
 
 
-def conv_kernel(tile_ref, weight_ref, tail_ref, out_ref, patch_ref):
+def place_kernel(tile_ref, out_ref, patch_ref):
     spot = (iota((TOK, LANES), 0) - 256).astype(F32)
     metas = [
         tile_ref[x, c, PLANE * 128 : PLANE * 128 + 16, :].astype(F32)
@@ -108,17 +109,20 @@
         for c in range(NC)
     ]
     for owner in range(PLANE):
-        total = None
+        picks, tiles = [], []
         for x in range(NX):
             for c in range(NC):
-                pick = jnp.where(spot == metas[x * NC + c][owner : owner + 1, :], 1.0, 0.0)
-                part = jnp.dot(
-                    pick.astype(BF16),
-                    tile_ref[x, c, owner * 128 : owner * 128 + 128, :],
-                    preferred_element_type=F32,
-                )
-                total = part if total is None else total + part
+                meta = metas[x * NC + c][owner : owner + 1, :]
+                picks.append(jnp.where(spot == meta, 1.0, 0.0).astype(BF16))
+                tiles.append(tile_ref[x, c, owner * 128 : owner * 128 + 128, :])
+        total = jnp.dot(
+            jnp.concatenate(picks, 1), jnp.concatenate(tiles, 0), preferred_element_type=F32
+        )
         patch_ref[:, owner * BLK : owner * BLK + BLK, :] = total.reshape(PATCH, BLK, LANES)
+    out_ref[...] = patch_ref[...].astype(BF16)
+
+
+def conv_kernel(patch_ref, weight_ref, tail_ref, out_ref):
     acc = jnp.zeros((256, 256), F32)
     for quad in range(16):
         if quad < 15:
@@ -127,7 +131,7 @@
             most = weight_ref[:, quad * 16 : MOST, :].astype(F32)
             left = jnp.concatenate([most, tail_ref[...].astype(F32)], 1).astype(BF16)
         left = left.reshape(256, LANES)
-        right = patch_ref[quad * 4 : quad * 4 + 4, :, :].astype(BF16).reshape(256, LANES)
+        right = patch_ref[quad * 4 : quad * 4 + 4, :, :].reshape(256, LANES)
         acc = acc + lax.dot_general(right, left, NT, preferred_element_type=F32)
     column = iota((64, 256), 1)
     kept = jnp.zeros((64, 256), F32)
@@ -143,10 +147,10 @@
     def merge(rows, hits):
         return jnp.dot(rows, hits, precision=lax.Precision.HIGHEST, preferred_element_type=F32)
 
-    low = merge(kept, lower).reshape(NX, NC, BLK, LANES)
-    high = merge(kept, upper).reshape(NX, NC, BLK, LANES)
+    low = merge(kept[0:32], lower).reshape(2, NC, BLK, LANES)
+    high = merge(kept[32:64], upper).reshape(2, NC, BLK, LANES)
     for c in range(NC):
-        sent = (low[0:2, c] + high[2:4, c]).reshape(16, LANES)
+        sent = (low[:, c] + high[:, c]).reshape(16, LANES)
         for x in range(NX):
             for head in range(NH):
                 out_ref[x, c, head] = sent
@@ -222,29 +226,26 @@
     out_ref[...] = total.astype(BF16)
 
 
-def attend_kernel(query_ref, key_value_ref, weight_ref, out_ref):
+def attend_kernel(query_ref, key_value_ref, weight_ref, mask_ref, out_ref):
     factor = math.log2(math.e) / math.sqrt(64)
-    step = 256
     keys = key_value_ref[:, 0:128]
     values = key_value_ref[:, 128:256]
-    weight = weight_ref[...]
-    lane = iota((step, LANES), 1)
-    for start in range(0, TOK, step):
-        query = query_ref[start : start + step, :]
-        mixed = []
-        for head in range(2):
-            mine = (lane >> 6) == head
-            masked = jnp.where(mine, query.astype(F32), 0.0).astype(BF16)
-            scores = lax.dot_general(masked, keys, NT, preferred_element_type=F32)
-            highest = jnp.max(scores, 1, keepdims=True)
-            weights = jnp.exp2((scores - highest) * factor)
-            totals = jnp.sum(weights, 1, keepdims=True)
-            mix = jnp.dot(weights.astype(BF16), values, preferred_element_type=F32)
-            mixed.append(mix / totals)
-        attended = jnp.where(lane < 64, mixed[0], mixed[1]).astype(BF16)
-        part = jnp.dot(attended, weight, preferred_element_type=F32).astype(BF16)
-        for group in range(NH):
-            out_ref[group, start : start + step, :] = part[:, group * 128 : group * 128 + 128]
+    query = query_ref[...]
+    lane, row = iota((TOK, LANES), 1), iota((LANES, TOK), 0)
+    mixed = []
+    for head in range(2):
+        masked = jnp.where((lane >> 6) == head, query.astype(F32), 0.0).astype(BF16)
+        scores = lax.dot_general(keys, masked, NT, preferred_element_type=F32)
+        highest = jnp.max(scores, 0, keepdims=True)
+        weights = jnp.exp2((scores - highest) * factor)
+        totals = jnp.sum(weights, 0, keepdims=True)
+        mix = lax.dot_general(values, weights.astype(BF16), TN, preferred_element_type=F32)
+        mixed.append(mix / totals)
+    attended = jnp.where(row < 64, mixed[0], mixed[1])
+    attended = jnp.where(mask_ref[...] != 0, attended, 0.0).astype(BF16)
+    part = lax.dot_general(attended, weight_ref[...], TN, preferred_element_type=F32).astype(BF16)
+    for group in range(NH):
+        out_ref[group] = part[:, group * 128 : group * 128 + 128]
 
 
 def local(
@@ -306,12 +307,17 @@
         jnp.broadcast_to(here[None], (NX,) + here.shape), "x", split_axis=0, concat_axis=0, tiled=True
     )
     tail = arrived[:, ROWS + 8 :]
+    patches = pl.pallas_call(
+        place_kernel,
+        out_shape=shape((PATCH, 64, LANES), BF16),
+        scratch_shapes=[pltpu.VMEM((PATCH, 64, LANES), F32)],
+        compiler_params=params(24),
+    )(tiles)
     partial = pl.pallas_call(
         conv_kernel,
         out_shape=shape((NX, NC, NH, 16, LANES), F32),
-        scratch_shapes=[pltpu.VMEM((PATCH, 64, LANES), F32)],
-        compiler_params=params(24),
-    )(tiles, weights, tail)
+        compiler_params=params(16),
+    )(patches, weights, tail)
     sums = lax.all_to_all(
         partial.reshape(PLANE * NH, 16, LANES),
         ("x", "core", "head"),
@@ -326,10 +332,9 @@
     gathered = lax.all_gather(gathered.reshape(NZ * 32, 256), "core", axis=0, tiled=True)
     parts = pl.pallas_call(
         attend_kernel, out_shape=shape((NH, TOK, LANES), BF16), compiler_params=params(24)
-    )(queries, gathered, out_weight)
+    )(queries, gathered, out_weight, tissue_mask.reshape(1, TOK))
     parts = lax.all_to_all(parts, "head", split_axis=0, concat_axis=0, tiled=True)
-    summed = jnp.sum(parts.astype(F32), 0)
-    return (summed * tissue_mask[:, None].astype(F32)).astype(BF16)
+    return jnp.sum(parts.astype(F32), 0).astype(BF16)
 
 
 def solution(mesh):

time: 152 us -> 148 us (0.974)
  blocking collectives: 101 us -> 112 us
  waiting for transfers between devices: 12 us -> 2.85 us
  starting transfers between devices: 23.4 us -> 19.9 us
  Pallas kernels: 11.4 us -> 9.56 us
    all_to_all x0 -> x1, blocking collectives: none -> 11.6 us  [local(): lax.all_to_all(parts, 'head', split_axis=0, concat_axis=0, tiled=True)]
    all_to_all x1 -> x0, waiting for transfers between devices: 9.17 us -> none  [local(): lax.all_to_all(parts, 'head', split_axis=0, concat_axis=0, tiled=True)]
    all_to_all x1 -> x0, starting transfers between devices: 3.47 us -> none  [local(): lax.all_to_all(parts, 'head', split_axis=0, concat_axis=0, tiled=True)]
    pallas_call x1, Pallas kernels: 4.19 us -> 1.12 us  [local(): pl.pallas_call(conv_kernel, out_shape=shape((NX, NC, NH, 16, LANES), F32)...]
    pallas_call x0 -> x1, Pallas kernels: none -> 2.33 us  [local(): pl.pallas_call(place_kernel, out_shape=shape((PATCH, 64, LANES), BF16), s...]
  transfers between devices with their start and end apart: 3 -> 2, of which waited for: 2 -> 1; matrix products, arithmetic and copies ran while one was open for 0% -> 0% of each run, Pallas kernels for 0% -> 0%
where the time goes in v4:
time: 148 us
  blocking collectives  112 us (76%)
  starting transfers between devices  19.9 us (13%)
  Pallas kernels  9.56 us (6%)
  waiting for transfers between devices  2.85 us (2%)
  local copies, waits for them, and re-layouts  2.16 us (1%)
    all_gather x1, blocking collectives, local(): lax.all_gather(most, 'z', axis=0, tiled=True).reshape(NZ, MOST, LANES)  33 us
    all_to_all x1, blocking collectives, local(): lax.all_to_all(partial.reshape(PLANE * NH, 16, LANES), ('x', 'core', 'hea...  22.4 us
    all_to_all x1, blocking collectives, local(): lax.all_to_all(key_value, 'z', split_axis=0, concat_axis=0, tiled=True)  17.4 us
    all_to_all x1, starting transfers between devices, local(): lax.all_to_all(sorted_rows, 'z', split_axis=0, concat_axis=0, tiled=True)  15.8 us
    all_gather x1, blocking collectives, local(): features = lax.all_gather(wide, 'head', axis=0)  12.1 us
    all_to_all x1, blocking collectives, local(): lax.all_to_all(parts, 'head', split_axis=0, concat_axis=0, tiled=True)  11.6 us
    all_gather x1, blocking collectives, local(): both = lax.all_gather(arrived, 'core', axis=0)  8.39 us
    all_gather x1, blocking collectives, local(): lax.all_gather(gathered.reshape(NZ * 32, 256), 'core', axis=0, tiled=True)  7.52 us
  transfers between devices with their start and end apart: 2, of which 1 were waited for; matrix products, arithmetic and copies ran while one was open for 0% of the time, Pallas kernels for 0%

profile of v4, /device:TPU:1, one launch (start us, length us, event | category | flops | bytes accessed | tf_op | source)
XLA Modules:
  0.0 147.8 jit_solution(9823333455850073549)
XLA Ops:
  0.0 2.6 %shard_map.109 = (bf16[16,80,128]{2,1,0:T(8,128)(2,1)}, bf16[560,128]{1,0:T(8,128)(2,1)}, bf16[248,128]{1,0:T(8,128)(2,1)}) custom-call(bf16[512,128]{1,0:T(8,128)(2,1)} %rows_hbm.1, s32[1,512]{1,0:T(1,128)} %bitcast.35, s32[1,512]{1,0:T(1,128)} %bitcast.27, bf16[256,128]{1,0:T(8,128)(2,1)} %bitcast.34, f32[1,128]{1,0:T(1,128)} %bitcast.36, ...), custom_call_target="tpu_custom_call" | custom-call | tf_op jit(solution)/shard_map/pallas_call | solution.py:266
  2.6 15.8 %all-to-all-start = ((bf16[16,80,128]{2,1,0:T(8,128)(2,1)}), bf16[16,80,128]{2,1,0:T(8,128)(2,1)S(1)}, u32[]{:S(2)}, u32[]{:S(2)}) async-start(bf16[16,80,128]{2,1,0:T(8,128)(2,1)} %get-tuple-element.11), calls=%async_computation | async-start | bytes 655360 | tf_op jit(solution)/shard_map/all_to_all | solution.py:294
  18.4 12.1 %all-gather = bf16[2240,128]{1,0:T(8,128)(2,1)S(1)} all-gather(bf16[560,128]{1,0:T(8,128)(2,1)} %get-tuple-element.13), channel_id=2, replica_groups=mesh['x'=4,'z'=16,'core'=2,'head'=4] {'head'}, dimensions={0}, use_global_device_ids=true | all-gather | bytes 716800 | tf_op jit(solution)/shard_map/all_gather | solution.py:295
  30.5 0.3 shard_map.110.query_ref
  30.8 2.8 %all-to-all-done = bf16[16,80,128]{2,1,0:T(8,128)(2,1)S(1)} async-done(((bf16[16,80,128]{2,1,0:T(8,128)(2,1)}), bf16[16,80,128]{2,1,0:T(8,128)(2,1)S(1)}, u32[]{:S(2)}, u32[]{:S(2)}) %all-to-all-start) | async-done | bytes 327712 | tf_op jit(solution)/shard_map/all_to_all | solution.py:294
  33.6 8.4 %all-gather.1 = bf16[32,80,128]{2,1,0:T(8,128)(2,1)S(1)} all-gather(bf16[16,80,128]{2,1,0:T(8,128)(2,1)S(1)} %all-to-all-done), channel_id=3, replica_groups=mesh['x'=4,'z'=16,'core'=2,'head'=4] {'core'}, dimensions={0}, use_global_device_ids=true | all-gather | bytes 983040 | tf_op jit(solution)/shard_map/all_gather | solution.py:301
  42.0 0.1 slice_bitcast_fusion
  42.1 0.1 copy.19
  42.2 0.1 copy.20
  42.3 0.1 copy.21
  42.4 0.1 reshape.49
  42.6 1.6 %broadcast_in_dim.2 = bf16[4,2,1040,128]{3,2,1,0:T(8,128)(2,1)} broadcast(bf16[2,1040,128]{2,1,0:T(8,128)(2,1)S(1)} %fusion.1), dimensions={1,2,3} | broadcast | bytes 2662400 | tf_op jit(solution)/shard_map/broadcast_in_dim | solution.py:307
  44.2 4.1 %all-to-all-start.1 = ((bf16[4,2,1040,128]{3,2,1,0:T(8,128)(2,1)}), bf16[4,2,1040,128]{3,2,1,0:T(8,128)(2,1)S(1)}, u32[]{:S(2)}, u32[]{:S(2)}) async-start(bf16[4,2,1040,128]{3,2,1,0:T(8,128)(2,1)} %broadcast_in_dim.2), calls=%async_computation.1 | async-start | bytes 4259840 | tf_op jit(solution)/shard_map/all_to_all | solution.py:306
  48.4 33.0 %all_gather.22 = bf16[3968,128]{1,0:T(8,128)(2,1)} all-gather(bf16[248,128]{1,0:T(8,128)(2,1)S(1)} %copy-done.6), channel_id=1, replica_groups=mesh['x'=4,'z'=16,'core'=2,'head'=4] {'z'}, dimensions={0}, use_global_device_ids=true | all-gather | bytes 1079296 | tf_op jit(solution)/shard_map/all_gather | solution.py:300
  81.4 2.3 %shard_map.111.patch_ref = bf16[64,64,128]{2,1,0:T(8,128)(2,1)S(1)} custom-call(bf16[4,2,1040,128]{3,2,1,0:T(8,128)(2,1)S(1)} %all-to-all-done.1.tile_ref), custom_call_target="tpu_custom_call" | custom-call | tf_op jit(solution)/shard_map/pallas_call | solution.py:310
  83.7 0.0 copy-start.3
  83.7 1.1 shard_map.112
  84.9 22.4 %all_to_all.25 = f32[32,16,128]{2,1,0:T(8,128)S(1)} all-to-all(f32[32,16,128]{2,1,0:T(8,128)S(1)} %bitcast.25), channel_id=1, replica_groups=mesh['x'=4,'z'=16,'core'=2,'head'=4] {'x','core','head'}, dimensions={0} | all-to-all | bytes 524288 | tf_op jit(solution)/shard_map/all_to_all | solution.py:321
  107.3 1.2 shard_map.113
  108.5 17.4 %all_to_all.26 = bf16[16,32,256]{2,1,0:T(8,128)(2,1)S(1)} all-to-all(bf16[16,32,256]{2,1,0:T(8,128)(2,1)S(1)} %shard_map.113), channel_id=1, replica_groups=mesh['x'=4,'z'=16,'core'=2,'head'=4] {'z'}, dimensions={0} | all-to-all | bytes 524288 | tf_op jit(solution)/shard_map/all_to_all | solution.py:331
  125.9 7.5 %all_gather.23.key_value_ref = bf16[1024,256]{1,0:T(8,128)(2,1)S(1)} all-gather(bf16[512,256]{1,0:T(8,128)(2,1)S(1)} %bitcast.32), channel_id=1, replica_groups=mesh['x'=4,'z'=16,'core'=2,'head'=4] {'core'}, dimensions={0}, use_global_device_ids=true | all-gather | bytes 786432 | tf_op jit(solution)/shard_map/all_gather | solution.py:332
  133.4 2.0 %shard_map.114 = bf16[4,512,128]{2,1,0:T(8,128)(2,1)S(1)} custom-call(bf16[512,128]{1,0:T(8,128)(2,1)S(1)} %shard_map.110.query_ref, bf16[1024,256]{1,0:T(8,128)(2,1)S(1)} %all_gather.23.key_value_ref, bf16[128,512]{1,0:T(8,128)(2,1)S(1)} %copy-done.2, s32[1,512]{1,0:T(1,128)S(1)} %bitcast.28), custom_call_target="tpu_custom_call" | custom-call | tf_op jit(solution)/shard_map/pallas_call | solution.py:333
  135.4 11.6 %all_to_all.27 = bf16[4,512,128]{2,1,0:T(8,128)(2,1)S(1)} all-to-all(bf16[4,512,128]{2,1,0:T(8,128)(2,1)S(1)} %shard_map.114), channel_id=1, replica_groups=mesh['x'=4,'z'=16,'core'=2,'head'=4] {'head'}, dimensions={0} | all-to-all | bytes 1048576 | tf_op jit(solution)/shard_map/all_to_all | solution.py:336
  147.0 0.7 reduce_sum.12
  (17 shorter events, 0.1 us)
Async XLA Ops:
  0.0 30.5 %copy-start.1 = (bf16[512,128]{1,0:T(8,128)(2,1)S(1)}, bf16[512,128]{1,0:T(8,128)(2,1)}, u32[]{:S(2)}) copy-start(bf16[512,128]{1,0:T(8,128)(2,1)} %weight_ref.2) | copy-start | bytes 393220
  2.6 31.0 %all-to-all-start = ((bf16[16,80,128]{2,1,0:T(8,128)(2,1)}), bf16[16,80,128]{2,1,0:T(8,128)(2,1)S(1)}, u32[]{:S(2)}, u32[]{:S(2)}) async-start(bf16[16,80,128]{2,1,0:T(8,128)(2,1)} %get-tuple-element.11), calls=%async_computation | async-start | bytes 655360 | tf_op jit(solution)/shard_map/all_to_all | solution.py:294
  44.2 4.1 %copy-start.6 = (bf16[248,128]{1,0:T(8,128)(2,1)S(1)}, bf16[248,128]{1,0:T(8,128)(2,1)}, u32[]{:S(2)}) copy-start(bf16[248,128]{1,0:T(8,128)(2,1)} %get-tuple-element.16) | copy-start | bytes 190468
  44.2 37.1 %all-to-all-start.1 = ((bf16[4,2,1040,128]{3,2,1,0:T(8,128)(2,1)}), bf16[4,2,1040,128]{3,2,1,0:T(8,128)(2,1)S(1)}, u32[]{:S(2)}, u32[]{:S(2)}) async-start(bf16[4,2,1040,128]{3,2,1,0:T(8,128)(2,1)} %broadcast_in_dim.2), calls=%async_computation.1 | async-start | bytes 4259840 | tf_op jit(solution)/shard_map/all_to_all | solution.py:306
  81.4 2.3 %copy-start = (bf16[3968,128]{1,0:T(8,128)(2,1)S(1)}, bf16[3968,128]{1,0:T(8,128)(2,1)}, u32[]{:S(2)}) copy-start(bf16[3968,128]{1,0:T(8,128)(2,1)} %all_gather.22) | copy-start | bytes 3047428
  83.7 23.6 %copy-start.3 = (bf16[512,128]{1,0:T(8,128)(2,1)S(1)}, bf16[512,128]{1,0:T(8,128)(2,1)}, u32[]{:S(2)}) copy-start(bf16[512,128]{1,0:T(8,128)(2,1)} %key_ref.1) | copy-start | bytes 393220
  83.7 23.6 %copy-start.4 = (bf16[512,128]{1,0:T(8,128)(2,1)S(1)}, bf16[512,128]{1,0:T(8,128)(2,1)}, u32[]{:S(2)}) copy-start(bf16[512,128]{1,0:T(8,128)(2,1)} %value_ref.1) | copy-start | bytes 393220
  107.3 26.1 %copy-start.2 = (bf16[128,512]{1,0:T(8,128)(2,1)S(1)}, bf16[128,512]{1,0:T(8,128)(2,1)}, u32[]{:S(2)}) copy-start(bf16[128,512]{1,0:T(8,128)(2,1)} %weight_ref.3) | copy-start | bytes 393220
  107.3 26.1 %copy-start.5 = (s32[512]{0:T(512)S(1)}, s32[512]{0:T(512)}, u32[]{:S(2)}) copy-start(s32[512]{0:T(512)} %param.13) | copy-start | bytes 6148

commit v5 on v4

--- a/solution.py
+++ b/solution.py
@@ -20,6 +20,7 @@
 BLK = 8
 PATCH = 64
 EMPTY = 1024.0
+HERE = PLANE * 128 + 16
 F32 = jnp.float32
 BF16 = jnp.bfloat16
 NT = (((1,), (1,)), ((), ()))
@@ -72,7 +73,7 @@
     wide_ref[TOK + 32 : WIDE, :] = low
     turned = jnp.dot(turn, kernel_ref[...], preferred_element_type=F32)
     most_ref[...] = turned[0:MOST, :].astype(BF16)
-    tail = jnp.concatenate([turned[MOST:256, :], turned[MOST:256, :]], 0)
+    tail = turned[MOST:256, :]
     order = order_ref[...]
     row, col = order >> 9, order & 511
     owner = (row >> 3) * 8 + (col >> 6)
@@ -84,37 +85,51 @@
     counts = jnp.dot(onehot.astype(BF16), before, preferred_element_type=F32)
     rank = jnp.sum(onehot * counts, 0, keepdims=True).astype(jnp.int32)
     slot = place * SLOTS + rank
-    here = iota((NZ, TOK), 0) == plane
-    value = jnp.where(here, (target - 256).astype(F32), 0.0).astype(BF16)
-    there = jnp.where(here, 1.0, 0.0).astype(BF16)
-    lane_of = jnp.where(iota((LANES, TOK), 0) == slot, 1.0, 0.0).astype(BF16)
+    mine = lax.axis_index("z")
+    lane_of = jnp.where(iota((LANES, TOK), 0) == mine * SLOTS + rank, 1.0, 0.0).astype(BF16)
+    value = (onehot * (target - 256).astype(F32)).astype(BF16)
     values = lax.dot_general(value, lane_of, NT, preferred_element_type=F32)
-    valid = lax.dot_general(there, lane_of, NT, preferred_element_type=F32)
-    meta = jnp.where(valid > 0.5, values, EMPTY)
+    valid = lax.dot_general(onehot.astype(BF16), lane_of, NT, preferred_element_type=F32)
+    empty = jnp.where((iota((128, LANES), 1) >> 3) == mine, EMPTY, 0.0)
+    meta = jnp.where(valid > 0.5, values, empty)
     wanted = jnp.where(mask_ref[...] != 0, plane * ROWS + slot, -1)
     rows = rows_ref[...]
-    top = iota((16, LANES), 0) < 8
     for z in range(NZ):
         pick = jnp.where(iota((ROWS, TOK), 0) + z * ROWS == wanted, 1.0, 0.0).astype(BF16)
         out_ref[z, 0:ROWS, :] = jnp.dot(pick, rows, preferred_element_type=F32).astype(BF16)
-        last = jnp.where(top, jnp.broadcast_to(meta[z : z + 1, :], (16, LANES)), tail)
+        last = jnp.concatenate([meta[z * PLANE : z * PLANE + PLANE, :], tail], 0)
         out_ref[z, ROWS:SEND, :] = last.astype(BF16)
+
+
+def spread_kernel(arrived_ref, out_hbm, here_ref, sems):
+    for owner in range(PLANE):
+        rows = arrived_ref[:, owner * SLOTS : owner * SLOTS + SLOTS, :]
+        here_ref[owner * 128 : owner * 128 + 128, :] = rows.reshape(128, LANES)
+    places = arrived_ref[0, ROWS:SEND, :].astype(F32)
+    for z in range(1, NZ):
+        places = places + arrived_ref[z, ROWS:SEND, :].astype(F32)
+    here_ref[PLANE * 128 : HERE, :] = places.astype(BF16)
+    copies = [
+        pltpu.make_async_copy(here_ref, out_hbm.at[index], sems.at[index])
+        for index in range(PLANE)
+    ]
+    for copy in copies:
+        copy.start()
+    for copy in copies:
+        copy.wait()
 
 
 def place_kernel(tile_ref, out_ref, patch_ref):
     spot = (iota((TOK, LANES), 0) - 256).astype(F32)
     metas = [
-        tile_ref[x, c, PLANE * 128 : PLANE * 128 + 16, :].astype(F32)
-        for x in range(NX)
-        for c in range(NC)
+        tile_ref[source, PLANE * 128 : HERE, :].astype(F32) for source in range(PLANE)
     ]
     for owner in range(PLANE):
         picks, tiles = [], []
-        for x in range(NX):
-            for c in range(NC):
-                meta = metas[x * NC + c][owner : owner + 1, :]
-                picks.append(jnp.where(spot == meta, 1.0, 0.0).astype(BF16))
-                tiles.append(tile_ref[x, c, owner * 128 : owner * 128 + 128, :])
+        for source in range(PLANE):
+            meta = metas[source][owner : owner + 1, :]
+            picks.append(jnp.where(spot == meta, 1.0, 0.0).astype(BF16))
+            tiles.append(tile_ref[source, owner * 128 : owner * 128 + 128, :])
         total = jnp.dot(
             jnp.concatenate(picks, 1), jnp.concatenate(tiles, 0), preferred_element_type=F32
         )
@@ -298,14 +313,14 @@
     )(features, query_weight)
     arrived, most, queries = lax.optimization_barrier((arrived, most, queries))
     weights = lax.all_gather(most, "z", axis=0, tiled=True).reshape(NZ, MOST, LANES)
-    both = lax.all_gather(arrived, "core", axis=0)
-    payload = both[:, :, :ROWS].reshape(NC, NZ, PLANE, SLOTS, LANES).transpose(0, 2, 1, 3, 4)
-    places = both[:, :, ROWS, :ROWS].reshape(NC, NZ, PLANE, SLOTS).transpose(0, 2, 1, 3)
-    places = jnp.pad(places.reshape(NC, PLANE, LANES), ((0, 0), (0, 8), (0, 0)))
-    here = jnp.concatenate([payload.reshape(NC, PLANE * 128, LANES), places], 1)
-    tiles = lax.all_to_all(
-        jnp.broadcast_to(here[None], (NX,) + here.shape), "x", split_axis=0, concat_axis=0, tiled=True
-    )
+    spread = pl.pallas_call(
+        spread_kernel,
+        out_shape=shape((PLANE, HERE, LANES), BF16),
+        out_specs=hbm,
+        scratch_shapes=[pltpu.VMEM((HERE, LANES), BF16), pltpu.SemaphoreType.DMA((PLANE,))],
+        compiler_params=params(16),
+    )(arrived)
+    tiles = lax.all_to_all(spread, ("x", "core"), split_axis=0, concat_axis=0, tiled=True)
     tail = arrived[:, ROWS + 8 :]
     patches = pl.pallas_call(
         place_kernel,

time: 148 us -> 146 us (0.986)
  blocking collectives: 112 us -> 104 us
  starting transfers between devices: 19.9 us -> 26.7 us
    all_gather x1 -> x0, blocking collectives: 8.39 us -> none  [local(): both = lax.all_gather(arrived, 'core', axis=0)]
    all_to_all x1, starting transfers between devices: 4.14 us -> 10.9 us  [local(): lax.all_to_all(spread, ('x', 'core'), split_axis=0, concat_axis=0, tiled=...]
    unnamed x14 -> x16, local copies, waits for them, and re-layouts: 0.03 us -> 2.27 us
    broadcast_in_dim x1 -> x0, local copies, waits for them, and re-layouts: 1.61 us -> none  [local(): jnp.broadcast_to(here[None], (NX,) + here.shape)]
where the time goes in v5:
time: 146 us; the launch traced here: 145 us
  blocking collectives  104 us (71%)
  starting transfers between devices  26.7 us (18%)
  Pallas kernels  9.87 us (7%)
  local copies, waits for them, and re-layouts  2.27 us (2%)
  waiting for transfers between devices  1.95 us (1%)
    all_gather x1, blocking collectives, local(): lax.all_gather(most, 'z', axis=0, tiled=True).reshape(NZ, MOST, LANES)  32.9 us
    all_to_all x1, blocking collectives, local(): lax.all_to_all(partial.reshape(PLANE * NH, 16, LANES), ('x', 'core', 'hea...  22.1 us
    all_to_all x1, blocking collectives, local(): lax.all_to_all(key_value, 'z', split_axis=0, concat_axis=0, tiled=True)  17.3 us
    all_to_all x1, starting transfers between devices, local(): lax.all_to_all(sorted_rows, 'z', split_axis=0, concat_axis=0, tiled=True)  15.8 us
    all_gather x1, blocking collectives, local(): features = lax.all_gather(wide, 'head', axis=0)  12.1 us
    all_to_all x1, blocking collectives, local(): lax.all_to_all(parts, 'head', split_axis=0, concat_axis=0, tiled=True)  11.6 us
    all_to_all x1, starting transfers between devices, local(): lax.all_to_all(spread, ('x', 'core'), split_axis=0, concat_axis=0, tiled=...  10.9 us
    all_gather x1, blocking collectives, local(): lax.all_gather(gathered.reshape(NZ * 32, 256), 'core', axis=0, tiled=True)  7.52 us
  transfers between devices with their start and end apart: 2, of which 1 were waited for; matrix products, arithmetic and copies ran while one was open for 0% of the time, Pallas kernels for 0%

profile of v5, /device:TPU:1, one launch (start us, length us, event | category | flops | bytes accessed | tf_op | source)
XLA Modules:
  0.0 145.2 jit_solution(4255100599491215611)
XLA Ops:
  0.0 2.6 %shard_map.109 = (bf16[16,80,128]{2,1,0:T(8,128)(2,1)}, bf16[560,128]{1,0:T(8,128)(2,1)}, bf16[248,128]{1,0:T(8,128)(2,1)}) custom-call(bf16[512,128]{1,0:T(8,128)(2,1)} %rows_hbm.1, s32[1,512]{1,0:T(1,128)} %bitcast.20, s32[1,512]{1,0:T(1,128)} %bitcast.16, bf16[256,128]{1,0:T(8,128)(2,1)} %bitcast.19, f32[1,128]{1,0:T(1,128)} %bitcast.21, ...), custom_call_target="tpu_custom_call" | custom-call | tf_op jit(solution)/shard_map/pallas_call | solution.py:281
  2.6 15.8 %all-to-all-start = ((bf16[16,80,128]{2,1,0:T(8,128)(2,1)}), bf16[16,80,128]{2,1,0:T(8,128)(2,1)S(1)}, u32[]{:S(2)}, u32[]{:S(2)}) async-start(bf16[16,80,128]{2,1,0:T(8,128)(2,1)} %get-tuple-element.11), calls=%async_computation | async-start | bytes 655360 | tf_op jit(solution)/shard_map/all_to_all | solution.py:309
  18.4 12.1 %all-gather = bf16[2240,128]{1,0:T(8,128)(2,1)S(1)} all-gather(bf16[560,128]{1,0:T(8,128)(2,1)} %get-tuple-element.13), channel_id=2, replica_groups=mesh['x'=4,'z'=16,'core'=2,'head'=4] {'head'}, dimensions={0}, use_global_device_ids=true | all-gather | bytes 716800 | tf_op jit(solution)/shard_map/all_gather | solution.py:310
  30.4 0.9 copy-done.2
  31.3 0.3 shard_map.110.query_ref
  31.6 1.9 %all-to-all-done.arrived_ref = bf16[16,80,128]{2,1,0:T(8,128)(2,1)S(1)} async-done(((bf16[16,80,128]{2,1,0:T(8,128)(2,1)}), bf16[16,80,128]{2,1,0:T(8,128)(2,1)S(1)}, u32[]{:S(2)}, u32[]{:S(2)}) %all-to-all-start) | async-done | bytes 327712 | tf_op jit(solution)/shard_map/all_to_all | solution.py:309
  33.6 0.3 shard_map.111
  33.9 1.3 copy-done
  35.3 10.9 %all-to-all-start.1 = ((bf16[8,1040,128]{2,1,0:T(8,128)(2,1)}), bf16[8,1040,128]{2,1,0:T(8,128)(2,1)S(1)}, u32[]{:S(2)}, u32[]{:S(2)}) async-start(bf16[8,1040,128]{2,1,0:T(8,128)(2,1)} %copy-done), calls=%async_computation.1 | async-start | bytes 4259840 | tf_op jit(solution)/shard_map/all_to_all | solution.py:323
  46.2 32.9 %all_gather.14 = bf16[3968,128]{1,0:T(8,128)(2,1)} all-gather(bf16[248,128]{1,0:T(8,128)(2,1)S(1)} %copy-done.7), channel_id=1, replica_groups=mesh['x'=4,'z'=16,'core'=2,'head'=4] {'z'}, dimensions={0}, use_global_device_ids=true | all-gather | bytes 1079296 | tf_op jit(solution)/shard_map/all_gather | solution.py:315
  79.1 0.0 all-to-all-done.1.tile_ref
  79.1 2.3 %shard_map.112.patch_ref = bf16[64,64,128]{2,1,0:T(8,128)(2,1)S(1)} custom-call(bf16[8,1040,128]{2,1,0:T(8,128)(2,1)S(1)} %all-to-all-done.1.tile_ref), custom_call_target="tpu_custom_call" | custom-call | tf_op jit(solution)/shard_map/pallas_call | solution.py:325
  81.4 0.0 copy-start.4
  81.5 0.0 copy-start.5
  81.5 1.1 shard_map.113
  82.6 0.0 copy-start.3
  82.6 0.0 copy-start.6
  82.6 22.1 %all_to_all.25 = f32[32,16,128]{2,1,0:T(8,128)S(1)} all-to-all(f32[32,16,128]{2,1,0:T(8,128)S(1)} %bitcast.14), channel_id=1, replica_groups=mesh['x'=4,'z'=16,'core'=2,'head'=4] {'x','core','head'}, dimensions={0} | all-to-all | bytes 524288 | tf_op jit(solution)/shard_map/all_to_all | solution.py:336
  104.8 1.2 shard_map.114
  105.9 17.3 %all_to_all.26 = bf16[16,32,256]{2,1,0:T(8,128)(2,1)S(1)} all-to-all(bf16[16,32,256]{2,1,0:T(8,128)(2,1)S(1)} %shard_map.114), channel_id=1, replica_groups=mesh['x'=4,'z'=16,'core'=2,'head'=4] {'z'}, dimensions={0} | all-to-all | bytes 524288 | tf_op jit(solution)/shard_map/all_to_all | solution.py:346
  123.2 7.5 %all_gather.15.key_value_ref = bf16[1024,256]{1,0:T(8,128)(2,1)S(1)} all-gather(bf16[512,256]{1,0:T(8,128)(2,1)S(1)} %bitcast.18), channel_id=1, replica_groups=mesh['x'=4,'z'=16,'core'=2,'head'=4] {'core'}, dimensions={0}, use_global_device_ids=true | all-gather | bytes 786432 | tf_op jit(solution)/shard_map/all_gather | solution.py:347
  130.8 2.0 %shard_map.115 = bf16[4,512,128]{2,1,0:T(8,128)(2,1)S(1)} custom-call(bf16[512,128]{1,0:T(8,128)(2,1)S(1)} %shard_map.110.query_ref, bf16[1024,256]{1,0:T(8,128)(2,1)S(1)} %all_gather.15.key_value_ref, bf16[128,512]{1,0:T(8,128)(2,1)S(1)} %copy-done.3, s32[1,512]{1,0:T(1,128)S(1)} %bitcast.17), custom_call_target="tpu_custom_call" | custom-call | tf_op jit(solution)/shard_map/pallas_call | solution.py:348
  132.8 11.6 %all_to_all.27 = bf16[4,512,128]{2,1,0:T(8,128)(2,1)S(1)} all-to-all(bf16[4,512,128]{2,1,0:T(8,128)(2,1)S(1)} %shard_map.115), channel_id=1, replica_groups=mesh['x'=4,'z'=16,'core'=2,'head'=4] {'head'}, dimensions={0} | all-to-all | bytes 1048576 | tf_op jit(solution)/shard_map/all_to_all | solution.py:351
  144.4 0.7 reduce_sum.12
  (11 shorter events, 0.0 us)
Async XLA Ops:
  2.6 31.0 %all-to-all-start = ((bf16[16,80,128]{2,1,0:T(8,128)(2,1)}), bf16[16,80,128]{2,1,0:T(8,128)(2,1)S(1)}, u32[]{:S(2)}, u32[]{:S(2)}) async-start(bf16[16,80,128]{2,1,0:T(8,128)(2,1)} %get-tuple-element.11), calls=%async_computation | async-start | bytes 655360 | tf_op jit(solution)/shard_map/all_to_all | solution.py:309
  30.4 0.9 copy-start.2
  33.9 1.3 copy-start
  35.3 10.9 %copy-start.7 = (bf16[248,128]{1,0:T(8,128)(2,1)S(1)}, bf16[248,128]{1,0:T(8,128)(2,1)}, u32[]{:S(2)}) copy-start(bf16[248,128]{1,0:T(8,128)(2,1)} %get-tuple-element.16) | copy-start | bytes 190468
  35.3 43.8 %all-to-all-start.1 = ((bf16[8,1040,128]{2,1,0:T(8,128)(2,1)}), bf16[8,1040,128]{2,1,0:T(8,128)(2,1)S(1)}, u32[]{:S(2)}, u32[]{:S(2)}) async-start(bf16[8,1040,128]{2,1,0:T(8,128)(2,1)} %copy-done), calls=%async_computation.1 | async-start | bytes 4259840 | tf_op jit(solution)/shard_map/all_to_all | solution.py:323
  79.1 2.4 %copy-start.1 = (bf16[3968,128]{1,0:T(8,128)(2,1)S(1)}, bf16[3968,128]{1,0:T(8,128)(2,1)}, u32[]{:S(2)}) copy-start(bf16[3968,128]{1,0:T(8,128)(2,1)} %all_gather.14) | copy-start | bytes 3047428
  81.4 23.3 %copy-start.4 = (bf16[512,128]{1,0:T(8,128)(2,1)S(1)}, bf16[512,128]{1,0:T(8,128)(2,1)}, u32[]{:S(2)}) copy-start(bf16[512,128]{1,0:T(8,128)(2,1)} %key_ref.1) | copy-start | bytes 393220
  81.5 23.3 %copy-start.5 = (bf16[512,128]{1,0:T(8,128)(2,1)S(1)}, bf16[512,128]{1,0:T(8,128)(2,1)}, u32[]{:S(2)}) copy-start(bf16[512,128]{1,0:T(8,128)(2,1)} %value_ref.1) | copy-start | bytes 393220
  82.6 48.2 %copy-start.3 = (bf16[128,512]{1,0:T(8,128)(2,1)S(1)}, bf16[128,512]{1,0:T(8,128)(2,1)}, u32[]{:S(2)}) copy-start(bf16[128,512]{1,0:T(8,128)(2,1)} %weight_ref.3) | copy-start | bytes 393220
  82.6 48.1 %copy-start.6 = (s32[512]{0:T(512)S(1)}, s32[512]{0:T(512)}, u32[]{:S(2)}) copy-start(s32[512]{0:T(512)} %param.13) | copy-start | bytes 6148

commit v6 on v5

--- a/solution.py
+++ b/solution.py
@@ -12,9 +12,9 @@
 PLANE = NX * NC
 SLOTS = 8
 ROWS = PLANE * SLOTS
-SEND = ROWS + 16
+SEND = ROWS + 8
 TOK = 512
-MOST = 248
+MOST = 252
 WIDE = TOK + 48
 LANES = 128
 BLK = 8
@@ -73,7 +73,8 @@
     wide_ref[TOK + 32 : WIDE, :] = low
     turned = jnp.dot(turn, kernel_ref[...], preferred_element_type=F32)
     most_ref[...] = turned[0:MOST, :].astype(BF16)
-    tail = turned[MOST:256, :]
+    tail = turned[MOST - 4 : 256, :]
+    lower = iota((8, LANES), 0) < 4
     order = order_ref[...]
     row, col = order >> 9, order & 511
     owner = (row >> 3) * 8 + (col >> 6)
@@ -85,19 +86,19 @@
     counts = jnp.dot(onehot.astype(BF16), before, preferred_element_type=F32)
     rank = jnp.sum(onehot * counts, 0, keepdims=True).astype(jnp.int32)
     slot = place * SLOTS + rank
-    mine = lax.axis_index("z")
-    lane_of = jnp.where(iota((LANES, TOK), 0) == mine * SLOTS + rank, 1.0, 0.0).astype(BF16)
-    value = (onehot * (target - 256).astype(F32)).astype(BF16)
+    here = iota((NZ, TOK), 0) == plane
+    value = jnp.where(here, (target - 256).astype(F32), 0.0).astype(BF16)
+    there = jnp.where(here, 1.0, 0.0).astype(BF16)
+    lane_of = jnp.where(iota((LANES, TOK), 0) == slot, 1.0, 0.0).astype(BF16)
     values = lax.dot_general(value, lane_of, NT, preferred_element_type=F32)
-    valid = lax.dot_general(onehot.astype(BF16), lane_of, NT, preferred_element_type=F32)
-    empty = jnp.where((iota((128, LANES), 1) >> 3) == mine, EMPTY, 0.0)
-    meta = jnp.where(valid > 0.5, values, empty)
+    valid = lax.dot_general(there, lane_of, NT, preferred_element_type=F32)
+    meta = jnp.where(valid > 0.5, values, EMPTY)
     wanted = jnp.where(mask_ref[...] != 0, plane * ROWS + slot, -1)
     rows = rows_ref[...]
     for z in range(NZ):
         pick = jnp.where(iota((ROWS, TOK), 0) + z * ROWS == wanted, 1.0, 0.0).astype(BF16)
         out_ref[z, 0:ROWS, :] = jnp.dot(pick, rows, preferred_element_type=F32).astype(BF16)
-        last = jnp.concatenate([meta[z * PLANE : z * PLANE + PLANE, :], tail], 0)
+        last = jnp.where(lower, jnp.broadcast_to(meta[z : z + 1, :], (8, LANES)), tail)
         out_ref[z, ROWS:SEND, :] = last.astype(BF16)
 
 
@@ -105,10 +106,17 @@
     for owner in range(PLANE):
         rows = arrived_ref[:, owner * SLOTS : owner * SLOTS + SLOTS, :]
         here_ref[owner * 128 : owner * 128 + 128, :] = rows.reshape(128, LANES)
-    places = arrived_ref[0, ROWS:SEND, :].astype(F32)
-    for z in range(1, NZ):
-        places = places + arrived_ref[z, ROWS:SEND, :].astype(F32)
-    here_ref[PLANE * 128 : HERE, :] = places.astype(BF16)
+    last = arrived_ref[:, ROWS:SEND, :].astype(F32)
+    rows = jnp.concatenate([last[z, 0:1, :] for z in range(NZ)], 0).astype(BF16)
+    source, lane = iota((LANES, LANES), 0), iota((LANES, LANES), 1)
+    own = iota((NZ, LANES), 0) == (iota((NZ, LANES), 1) >> 3)
+    found = []
+    for owner in range(PLANE):
+        pick = jnp.where(source == owner * SLOTS + (lane & 7), 1.0, 0.0).astype(BF16)
+        moved = jnp.dot(rows, pick, preferred_element_type=F32)
+        found.append(jnp.sum(jnp.where(own, moved, 0.0), 0, keepdims=True))
+    found.append(jnp.zeros((8, LANES), F32))
+    here_ref[PLANE * 128 : HERE, :] = jnp.concatenate(found, 0).astype(BF16)
     copies = [
         pltpu.make_async_copy(here_ref, out_hbm.at[index], sems.at[index])
         for index in range(PLANE)
@@ -144,7 +152,7 @@
             left = weight_ref[:, quad * 16 : quad * 16 + 16, :]
         else:
             most = weight_ref[:, quad * 16 : MOST, :].astype(F32)
-            left = jnp.concatenate([most, tail_ref[...].astype(F32)], 1).astype(BF16)
+            left = jnp.concatenate([most, tail_ref[:, 4:8, :].astype(F32)], 1).astype(BF16)
         left = left.reshape(256, LANES)
         right = patch_ref[quad * 4 : quad * 4 + 4, :, :].reshape(256, LANES)
         acc = acc + lax.dot_general(right, left, NT, preferred_element_type=F32)
@@ -312,7 +320,7 @@
         query_kernel, out_shape=shape((TOK, LANES), BF16), compiler_params=params(16)
     )(features, query_weight)
     arrived, most, queries = lax.optimization_barrier((arrived, most, queries))
-    weights = lax.all_gather(most, "z", axis=0, tiled=True).reshape(NZ, MOST, LANES)
+    weights = lax.all_gather(most, "z", axis=0)
     spread = pl.pallas_call(
         spread_kernel,
         out_shape=shape((PLANE, HERE, LANES), BF16),
@@ -321,7 +329,7 @@
         compiler_params=params(16),
     )(arrived)
     tiles = lax.all_to_all(spread, ("x", "core"), split_axis=0, concat_axis=0, tiled=True)
-    tail = arrived[:, ROWS + 8 :]
+    tail = arrived[:, ROWS:]
     patches = pl.pallas_call(
         place_kernel,
         out_shape=shape((PATCH, 64, LANES), BF16),

time: 146 us -> 145 us (level)
  waiting for transfers between devices: 1.95 us -> 0.48 us
    all_to_all x1, waiting for transfers between devices: 1.95 us -> 0.48 us  [local(): lax.all_to_all(sorted_rows, 'z', split_axis=0, concat_axis=0, tiled=True)]
where the time goes in v6:
time: 145 us; the launch traced here: 144 us
  blocking collectives  104 us (72%)
  starting transfers between devices  26.7 us (18%)
  Pallas kernels  10 us (7%)
  local copies, waits for them, and re-layouts  2.27 us (2%)
    all_gather x1, blocking collectives, local(): weights = lax.all_gather(most, 'z', axis=0)  33 us
    all_to_all x1, blocking collectives, local(): lax.all_to_all(partial.reshape(PLANE * NH, 16, LANES), ('x', 'core', 'hea...  22.2 us
    all_to_all x1, blocking collectives, local(): lax.all_to_all(key_value, 'z', split_axis=0, concat_axis=0, tiled=True)  17.3 us
    all_to_all x1, starting transfers between devices, local(): lax.all_to_all(sorted_rows, 'z', split_axis=0, concat_axis=0, tiled=True)  15.8 us
    all_gather x1, blocking collectives, local(): features = lax.all_gather(wide, 'head', axis=0)  12.1 us
    all_to_all x1, blocking collectives, local(): lax.all_to_all(parts, 'head', split_axis=0, concat_axis=0, tiled=True)  11.6 us
    all_to_all x1, starting transfers between devices, local(): lax.all_to_all(spread, ('x', 'core'), split_axis=0, concat_axis=0, tiled=...  10.9 us
    all_gather x1, blocking collectives, local(): lax.all_gather(gathered.reshape(NZ * 32, 256), 'core', axis=0, tiled=True)  7.52 us
  transfers between devices with their start and end apart: 2, of which 1 were waited for; matrix products, arithmetic and copies ran while one was open for 0% of the time, Pallas kernels for 0%

profile of v6, /device:TPU:1, one launch (start us, length us, event | category | flops | bytes accessed | tf_op | source)
XLA Modules:
  0.0 144.1 jit_solution(895597551793919071)
XLA Ops:
  0.0 2.6 %shard_map.109 = (bf16[16,72,128]{2,1,0:T(8,128)(2,1)}, bf16[560,128]{1,0:T(8,128)(2,1)}, bf16[252,128]{1,0:T(8,128)(2,1)}) custom-call(bf16[512,128]{1,0:T(8,128)(2,1)} %rows_hbm.1, s32[1,512]{1,0:T(1,128)} %bitcast.20, s32[1,512]{1,0:T(1,128)} %bitcast.15, bf16[256,128]{1,0:T(8,128)(2,1)} %bitcast.18, f32[1,128]{1,0:T(1,128)} %bitcast.21, ...), custom_call_target="tpu_custom_call" | custom-call | tf_op jit(solution)/shard_map/pallas_call | solution.py:289
  2.6 15.8 %all-to-all-start = ((bf16[16,72,128]{2,1,0:T(8,128)(2,1)}), bf16[16,72,128]{2,1,0:T(8,128)(2,1)S(1)}, u32[]{:S(2)}, u32[]{:S(2)}) async-start(bf16[16,72,128]{2,1,0:T(8,128)(2,1)} %get-tuple-element.11), calls=%async_computation | async-start | bytes 589824 | tf_op jit(solution)/shard_map/all_to_all | solution.py:317
  18.3 12.1 %all-gather = bf16[2240,128]{1,0:T(8,128)(2,1)S(1)} all-gather(bf16[560,128]{1,0:T(8,128)(2,1)} %get-tuple-element.13), channel_id=2, replica_groups=mesh['x'=4,'z'=16,'core'=2,'head'=4] {'head'}, dimensions={0}, use_global_device_ids=true | all-gather | bytes 716800 | tf_op jit(solution)/shard_map/all_gather | solution.py:318
  30.4 0.9 copy-done.2
  31.3 0.3 shard_map.110.query_ref
  31.6 0.5 all-to-all-done.arrived_ref
  32.1 0.5 shard_map.111
  32.6 1.3 copy-done
  33.9 10.9 %all-to-all-start.1 = ((bf16[8,1040,128]{2,1,0:T(8,128)(2,1)}), bf16[8,1040,128]{2,1,0:T(8,128)(2,1)S(1)}, u32[]{:S(2)}, u32[]{:S(2)}) async-start(bf16[8,1040,128]{2,1,0:T(8,128)(2,1)} %copy-done), calls=%async_computation.1 | async-start | bytes 4259840 | tf_op jit(solution)/shard_map/all_to_all | solution.py:331
  44.9 33.0 %all-gather.2.weight_ref = bf16[16,252,128]{2,1,0:T(8,128)(2,1)} all-gather(bf16[1,252,128]{2,1,0:T(8,128)(2,1)S(1)} %bitcast.19), channel_id=3, replica_groups=mesh['x'=4,'z'=16,'core'=2,'head'=4] {'z'}, dimensions={0}, use_global_device_ids=true | all-gather | bytes 1096704 | tf_op jit(solution)/shard_map/all_gather | solution.py:323
  77.9 0.0 all-to-all-done.1.tile_ref
  77.9 2.3 %shard_map.112.patch_ref = bf16[64,64,128]{2,1,0:T(8,128)(2,1)S(1)} custom-call(bf16[8,1040,128]{2,1,0:T(8,128)(2,1)S(1)} %all-to-all-done.1.tile_ref), custom_call_target="tpu_custom_call" | custom-call | tf_op jit(solution)/shard_map/pallas_call | solution.py:333
  80.3 0.0 copy-start.4
  80.3 0.0 copy-start.5
  80.3 1.1 shard_map.113
  81.4 0.0 copy-start.3
  81.4 0.0 copy-start.6
  81.4 22.2 %all_to_all.25 = f32[32,16,128]{2,1,0:T(8,128)S(1)} all-to-all(f32[32,16,128]{2,1,0:T(8,128)S(1)} %bitcast.13), channel_id=1, replica_groups=mesh['x'=4,'z'=16,'core'=2,'head'=4] {'x','core','head'}, dimensions={0} | all-to-all | bytes 524288 | tf_op jit(solution)/shard_map/all_to_all | solution.py:344
  103.7 1.2 shard_map.114
  104.9 17.3 %all_to_all.26 = bf16[16,32,256]{2,1,0:T(8,128)(2,1)S(1)} all-to-all(bf16[16,32,256]{2,1,0:T(8,128)(2,1)S(1)} %shard_map.114), channel_id=1, replica_groups=mesh['x'=4,'z'=16,'core'=2,'head'=4] {'z'}, dimensions={0} | all-to-all | bytes 524288 | tf_op jit(solution)/shard_map/all_to_all | solution.py:354
  122.2 7.5 %all_gather.19.key_value_ref = bf16[1024,256]{1,0:T(8,128)(2,1)S(1)} all-gather(bf16[512,256]{1,0:T(8,128)(2,1)S(1)} %bitcast.17), channel_id=1, replica_groups=mesh['x'=4,'z'=16,'core'=2,'head'=4] {'core'}, dimensions={0}, use_global_device_ids=true | all-gather | bytes 786432 | tf_op jit(solution)/shard_map/all_gather | solution.py:355
  129.7 2.0 %shard_map.115 = bf16[4,512,128]{2,1,0:T(8,128)(2,1)S(1)} custom-call(bf16[512,128]{1,0:T(8,128)(2,1)S(1)} %shard_map.110.query_ref, bf16[1024,256]{1,0:T(8,128)(2,1)S(1)} %all_gather.19.key_value_ref, bf16[128,512]{1,0:T(8,128)(2,1)S(1)} %copy-done.3, s32[1,512]{1,0:T(1,128)S(1)} %bitcast.16), custom_call_target="tpu_custom_call" | custom-call | tf_op jit(solution)/shard_map/pallas_call | solution.py:356
  131.8 11.6 %all_to_all.27 = bf16[4,512,128]{2,1,0:T(8,128)(2,1)S(1)} all-to-all(bf16[4,512,128]{2,1,0:T(8,128)(2,1)S(1)} %shard_map.115), channel_id=1, replica_groups=mesh['x'=4,'z'=16,'core'=2,'head'=4] {'head'}, dimensions={0} | all-to-all | bytes 1048576 | tf_op jit(solution)/shard_map/all_to_all | solution.py:359
  143.3 0.7 reduce_sum.12
  (11 shorter events, 0.0 us)
Async XLA Ops:
  2.6 29.5 %all-to-all-start = ((bf16[16,72,128]{2,1,0:T(8,128)(2,1)}), bf16[16,72,128]{2,1,0:T(8,128)(2,1)S(1)}, u32[]{:S(2)}, u32[]{:S(2)}) async-start(bf16[16,72,128]{2,1,0:T(8,128)(2,1)} %get-tuple-element.11), calls=%async_computation | async-start | bytes 589824 | tf_op jit(solution)/shard_map/all_to_all | solution.py:317
  30.4 0.9 copy-start.2
  32.6 1.3 copy-start
  33.9 10.9 %copy-start.7 = (bf16[252,128]{1,0:T(8,128)(2,1)S(1)}, bf16[252,128]{1,0:T(8,128)(2,1)}, u32[]{:S(2)}) copy-start(bf16[252,128]{1,0:T(8,128)(2,1)} %get-tuple-element.16) | copy-start | bytes 193540
  33.9 44.0 %all-to-all-start.1 = ((bf16[8,1040,128]{2,1,0:T(8,128)(2,1)}), bf16[8,1040,128]{2,1,0:T(8,128)(2,1)S(1)}, u32[]{:S(2)}, u32[]{:S(2)}) async-start(bf16[8,1040,128]{2,1,0:T(8,128)(2,1)} %copy-done), calls=%async_computation.1 | async-start | bytes 4259840 | tf_op jit(solution)/shard_map/all_to_all | solution.py:331
  77.9 2.3 %copy-start.1 = (bf16[16,252,128]{2,1,0:T(8,128)(2,1)S(1)}, bf16[16,252,128]{2,1,0:T(8,128)(2,1)}, u32[]{:S(2)}) copy-start(bf16[16,252,128]{2,1,0:T(8,128)(2,1)} %all-gather.2.weight_ref) | copy-start | bytes 3096580
  80.3 23.4 %copy-start.4 = (bf16[512,128]{1,0:T(8,128)(2,1)S(1)}, bf16[512,128]{1,0:T(8,128)(2,1)}, u32[]{:S(2)}) copy-start(bf16[512,128]{1,0:T(8,128)(2,1)} %key_ref.1) | copy-start | bytes 393220
  80.3 23.4 %copy-start.5 = (bf16[512,128]{1,0:T(8,128)(2,1)S(1)}, bf16[512,128]{1,0:T(8,128)(2,1)}, u32[]{:S(2)}) copy-start(bf16[512,128]{1,0:T(8,128)(2,1)} %value_ref.1) | copy-start | bytes 393220
  81.4 48.3 %copy-start.3 = (bf16[128,512]{1,0:T(8,128)(2,1)S(1)}, bf16[128,512]{1,0:T(8,128)(2,1)}, u32[]{:S(2)}) copy-start(bf16[128,512]{1,0:T(8,128)(2,1)} %weight_ref.3) | copy-start | bytes 393220
  81.4 48.3 %copy-start.6 = (s32[512]{0:T(512)S(1)}, s32[512]{0:T(512)}, u32[]{:S(2)}) copy-start(s32[512]{0:T(512)} %param.13) | copy-start | bytes 6148

commit v7 on v6

--- a/solution.py
+++ b/solution.py
@@ -127,7 +127,7 @@
         copy.wait()
 
 
-def place_kernel(tile_ref, out_ref, patch_ref):
+def place_kernel(tile_ref, weight_ref, out_ref, patch_ref):
     spot = (iota((TOK, LANES), 0) - 256).astype(F32)
     metas = [
         tile_ref[source, PLANE * 128 : HERE, :].astype(F32) for source in range(PLANE)
@@ -326,7 +326,7 @@
         out_shape=shape((PLANE, HERE, LANES), BF16),
         out_specs=hbm,
         scratch_shapes=[pltpu.VMEM((HERE, LANES), BF16), pltpu.SemaphoreType.DMA((PLANE,))],
-        compiler_params=params(16),
+        compiler_params=params(52),
     )(arrived)
     tiles = lax.all_to_all(spread, ("x", "core"), split_axis=0, concat_axis=0, tiled=True)
     tail = arrived[:, ROWS:]
@@ -335,7 +335,7 @@
         out_shape=shape((PATCH, 64, LANES), BF16),
         scratch_shapes=[pltpu.VMEM((PATCH, 64, LANES), F32)],
         compiler_params=params(24),
-    )(tiles)
+    )(tiles, weights)
     partial = pl.pallas_call(
         conv_kernel,
         out_shape=shape((NX, NC, NH, 16, LANES), F32),

time: 145 us -> 142 us (0.979)
  blocking collectives: 104 us -> 102 us
    all_gather x1, blocking collectives: 33 us -> 31.1 us  [local(): weights = lax.all_gather(most, 'z', axis=0)]
  transfers between devices with their start and end apart: 2 -> 2, of which waited for: 1 -> 0; matrix products, arithmetic and copies ran while one was open for 0% -> 0% of each run, Pallas kernels for 0% -> 0%
where the time goes in v7:
time: 142 us
  blocking collectives  102 us (72%)
  starting transfers between devices  26.3 us (19%)
  Pallas kernels  11.1 us (8%)
  local copies, waits for them, and re-layouts  1.77 us (1%)
    all_gather x1, blocking collectives, local(): weights = lax.all_gather(most, 'z', axis=0)  31.1 us
    all_to_all x1, blocking collectives, local(): lax.all_to_all(partial.reshape(PLANE * NH, 16, LANES), ('x', 'core', 'hea...  21.7 us
    all_to_all x1, blocking collectives, local(): lax.all_to_all(key_value, 'z', split_axis=0, concat_axis=0, tiled=True)  17.5 us
    all_to_all x1, starting transfers between devices, local(): lax.all_to_all(sorted_rows, 'z', split_axis=0, concat_axis=0, tiled=True)  15.8 us
    all_gather x1, blocking collectives, local(): features = lax.all_gather(wide, 'head', axis=0)  12.1 us
    all_to_all x1, blocking collectives, local(): lax.all_to_all(parts, 'head', split_axis=0, concat_axis=0, tiled=True)  11.6 us
    all_to_all x1, starting transfers between devices, local(): lax.all_to_all(spread, ('x', 'core'), split_axis=0, concat_axis=0, tiled=...  10.6 us
    all_gather x1, blocking collectives, local(): lax.all_gather(gathered.reshape(NZ * 32, 256), 'core', axis=0, tiled=True)  7.52 us
  transfers between devices with their start and end apart: 2, of which 0 were waited for; matrix products, arithmetic and copies ran while one was open for 0% of the time, Pallas kernels for 0%

profile of v7, /device:TPU:1, one launch (start us, length us, event | category | flops | bytes accessed | tf_op | source)
XLA Modules:
  0.0 141.7 jit_solution(5109664265083448683)
XLA Ops:
  0.0 2.6 %shard_map.109 = (bf16[16,72,128]{2,1,0:T(8,128)(2,1)}, bf16[560,128]{1,0:T(8,128)(2,1)}, bf16[252,128]{1,0:T(8,128)(2,1)}) custom-call(bf16[512,128]{1,0:T(8,128)(2,1)} %rows_hbm.1, s32[1,512]{1,0:T(1,128)} %bitcast.20, s32[1,512]{1,0:T(1,128)} %bitcast.15, bf16[256,128]{1,0:T(8,128)(2,1)} %bitcast.18, f32[1,128]{1,0:T(1,128)} %bitcast.21, ...), custom_call_target="tpu_custom_call" | custom-call | tf_op jit(solution)/shard_map/pallas_call | solution.py:289
  2.6 15.8 %all-to-all-start = ((bf16[16,72,128]{2,1,0:T(8,128)(2,1)}), bf16[16,72,128]{2,1,0:T(8,128)(2,1)S(1)}, u32[]{:S(2)}, u32[]{:S(2)}) async-start(bf16[16,72,128]{2,1,0:T(8,128)(2,1)} %get-tuple-element.11), calls=%async_computation | async-start | bytes 589824 | tf_op jit(solution)/shard_map/all_to_all | solution.py:317
  18.3 12.1 %all-gather = bf16[2240,128]{1,0:T(8,128)(2,1)S(1)} all-gather(bf16[560,128]{1,0:T(8,128)(2,1)} %get-tuple-element.13), channel_id=2, replica_groups=mesh['x'=4,'z'=16,'core'=2,'head'=4] {'head'}, dimensions={0}, use_global_device_ids=true | all-gather | bytes 716800 | tf_op jit(solution)/shard_map/all_gather | solution.py:318
  30.4 0.9 copy-done.2
  31.3 0.3 shard_map.110.query_ref
  31.6 0.8 copy-done
  32.5 0.0 all-to-all-done.arrived_ref
  32.5 1.6 %shard_map.111 = bf16[8,1040,128]{2,1,0:T(8,128)(2,1)} custom-call(bf16[16,72,128]{2,1,0:T(8,128)(2,1)S(1)} %all-to-all-done.arrived_ref), custom_call_target="tpu_custom_call" | custom-call | tf_op jit(solution)/shard_map/pallas_call | solution.py:324
  34.0 0.0 copy-start.7
  34.1 10.6 %all-to-all-start.1 = ((bf16[8,1040,128]{2,1,0:T(8,128)(2,1)}), bf16[8,1040,128]{2,1,0:T(8,128)(2,1)S(1)}, u32[]{:S(2)}, u32[]{:S(2)}) async-start(bf16[8,1040,128]{2,1,0:T(8,128)(2,1)} %shard_map.111), calls=%async_computation.1 | async-start | bytes 4259840 | tf_op jit(solution)/shard_map/all_to_all | solution.py:331
  44.6 31.1 %all-gather.2.weight_ref = bf16[16,252,128]{2,1,0:T(8,128)(2,1)S(1)} all-gather(bf16[1,252,128]{2,1,0:T(8,128)(2,1)S(1)} %bitcast.19), channel_id=3, replica_groups=mesh['x'=4,'z'=16,'core'=2,'head'=4] {'z'}, dimensions={0}, use_global_device_ids=true | all-gather | bytes 1096704 | tf_op jit(solution)/shard_map/all_gather | solution.py:323
  75.8 2.3 %shard_map.112.patch_ref = bf16[64,64,128]{2,1,0:T(8,128)(2,1)S(1)} custom-call(bf16[8,1040,128]{2,1,0:T(8,128)(2,1)S(1)} %all-to-all-done.1.tile_ref, bf16[16,252,128]{2,1,0:T(8,128)(2,1)S(1)} %all-gather.2.weight_ref), custom_call_target="tpu_custom_call" | custom-call | tf_op jit(solution)/shard_map/pallas_call | solution.py:333
  78.1 0.0 copy-start.4
  78.1 0.0 copy-start.5
  78.1 1.1 shard_map.113
  79.3 0.0 copy-start.3
  79.3 0.0 copy-start.6
  79.3 21.7 %all_to_all.25 = f32[32,16,128]{2,1,0:T(8,128)S(1)} all-to-all(f32[32,16,128]{2,1,0:T(8,128)S(1)} %bitcast.13), channel_id=1, replica_groups=mesh['x'=4,'z'=16,'core'=2,'head'=4] {'x','core','head'}, dimensions={0} | all-to-all | bytes 524288 | tf_op jit(solution)/shard_map/all_to_all | solution.py:344
  101.0 1.2 shard_map.114
  102.2 17.5 %all_to_all.26 = bf16[16,32,256]{2,1,0:T(8,128)(2,1)S(1)} all-to-all(bf16[16,32,256]{2,1,0:T(8,128)(2,1)S(1)} %shard_map.114), channel_id=1, replica_groups=mesh['x'=4,'z'=16,'core'=2,'head'=4] {'z'}, dimensions={0} | all-to-all | bytes 524288 | tf_op jit(solution)/shard_map/all_to_all | solution.py:354
  119.7 7.5 %all_gather.19.key_value_ref = bf16[1024,256]{1,0:T(8,128)(2,1)S(1)} all-gather(bf16[512,256]{1,0:T(8,128)(2,1)S(1)} %bitcast.17), channel_id=1, replica_groups=mesh['x'=4,'z'=16,'core'=2,'head'=4] {'core'}, dimensions={0}, use_global_device_ids=true | all-gather | bytes 786432 | tf_op jit(solution)/shard_map/all_gather | solution.py:355
  127.2 2.1 %shard_map.115 = bf16[4,512,128]{2,1,0:T(8,128)(2,1)S(1)} custom-call(bf16[512,128]{1,0:T(8,128)(2,1)S(1)} %shard_map.110.query_ref, bf16[1024,256]{1,0:T(8,128)(2,1)S(1)} %all_gather.19.key_value_ref, bf16[128,512]{1,0:T(8,128)(2,1)S(1)} %copy-done.3, s32[1,512]{1,0:T(1,128)S(1)} %bitcast.16), custom_call_target="tpu_custom_call" | custom-call | tf_op jit(solution)/shard_map/pallas_call | solution.py:356
  129.3 11.6 %all_to_all.27 = bf16[4,512,128]{2,1,0:T(8,128)(2,1)S(1)} all-to-all(bf16[4,512,128]{2,1,0:T(8,128)(2,1)S(1)} %shard_map.115), channel_id=1, replica_groups=mesh['x'=4,'z'=16,'core'=2,'head'=4] {'head'}, dimensions={0} | all-to-all | bytes 1048576 | tf_op jit(solution)/shard_map/all_to_all | solution.py:359
  140.9 0.7 reduce_sum.12
  (11 shorter events, 0.0 us)
Async XLA Ops:
  2.6 29.9 %all-to-all-start = ((bf16[16,72,128]{2,1,0:T(8,128)(2,1)}), bf16[16,72,128]{2,1,0:T(8,128)(2,1)S(1)}, u32[]{:S(2)}, u32[]{:S(2)}) async-start(bf16[16,72,128]{2,1,0:T(8,128)(2,1)} %get-tuple-element.11), calls=%async_computation | async-start | bytes 589824 | tf_op jit(solution)/shard_map/all_to_all | solution.py:317
  30.4 0.9 copy-start.2
  31.6 0.8 copy-start
  34.0 10.6 %copy-start.7 = (bf16[252,128]{1,0:T(8,128)(2,1)S(1)}, bf16[252,128]{1,0:T(8,128)(2,1)}, u32[]{:S(2)}) copy-start(bf16[252,128]{1,0:T(8,128)(2,1)} %get-tuple-element.16) | copy-start | bytes 193540
  34.1 41.7 %all-to-all-start.1 = ((bf16[8,1040,128]{2,1,0:T(8,128)(2,1)}), bf16[8,1040,128]{2,1,0:T(8,128)(2,1)S(1)}, u32[]{:S(2)}, u32[]{:S(2)}) async-start(bf16[8,1040,128]{2,1,0:T(8,128)(2,1)} %shard_map.111), calls=%async_computation.1 | async-start | bytes 4259840 | tf_op jit(solution)/shard_map/all_to_all | solution.py:331
  78.1 22.9 %copy-start.1 = (bf16[2240,128]{1,0:T(8,128)(2,1)S(1)}, bf16[2240,128]{1,0:T(8,128)(2,1)}, u32[]{:S(2)}) copy-start(bf16[2240,128]{1,0:T(8,128)(2,1)} %copy-done) | copy-start | bytes 1720324
  78.1 22.9 %copy-start.4 = (bf16[512,128]{1,0:T(8,128)(2,1)S(1)}, bf16[512,128]{1,0:T(8,128)(2,1)}, u32[]{:S(2)}) copy-start(bf16[512,128]{1,0:T(8,128)(2,1)} %key_ref.1) | copy-start | bytes 393220
  78.1 22.8 %copy-start.5 = (bf16[512,128]{1,0:T(8,128)(2,1)S(1)}, bf16[512,128]{1,0:T(8,128)(2,1)}, u32[]{:S(2)}) copy-start(bf16[512,128]{1,0:T(8,128)(2,1)} %value_ref.1) | copy-start | bytes 393220
  79.3 48.0 %copy-start.3 = (bf16[128,512]{1,0:T(8,128)(2,1)S(1)}, bf16[128,512]{1,0:T(8,128)(2,1)}, u32[]{:S(2)}) copy-start(bf16[128,512]{1,0:T(8,128)(2,1)} %weight_ref.3) | copy-start | bytes 393220
  79.3 48.0 %copy-start.6 = (s32[512]{0:T(512)S(1)}, s32[512]{0:T(512)}, u32[]{:S(2)}) copy-start(s32[512]{0:T(512)} %param.13) | copy-start | bytes 6148

commit v8 on v7

--- a/solution.py
+++ b/solution.py
@@ -128,20 +128,29 @@
 
 
 def place_kernel(tile_ref, weight_ref, out_ref, patch_ref):
-    spot = (iota((TOK, LANES), 0) - 256).astype(F32)
-    metas = [
-        tile_ref[source, PLANE * 128 : HERE, :].astype(F32) for source in range(PLANE)
-    ]
+    half = TOK // 2
+    spot = (iota((half, LANES), 0) - half).astype(F32)
+    eye = jnp.where(iota((LANES, LANES), 0) == iota((LANES, LANES), 1), 1.0, 0.0).astype(BF16)
+    metas, highs = [], []
+    for source in range(PLANE):
+        places = tile_ref[source, PLANE * 128 : HERE, :].astype(F32)
+        high = jnp.where(places >= 0, 1.0, 0.0)
+        metas.append(places - half * high)
+        highs.append(lax.dot_general(eye, high.astype(BF16), NT, preferred_element_type=F32))
     for owner in range(PLANE):
         picks, tiles = [], []
         for source in range(PLANE):
             meta = metas[source][owner : owner + 1, :]
             picks.append(jnp.where(spot == meta, 1.0, 0.0).astype(BF16))
-            tiles.append(tile_ref[source, owner * 128 : owner * 128 + 128, :])
+            rows = tile_ref[source, owner * 128 : owner * 128 + 128, :]
+            upper = rows * highs[source][:, owner : owner + 1].astype(BF16)
+            tiles.append(jnp.concatenate([rows - upper, upper], 1))
         total = jnp.dot(
             jnp.concatenate(picks, 1), jnp.concatenate(tiles, 0), preferred_element_type=F32
         )
-        patch_ref[:, owner * BLK : owner * BLK + BLK, :] = total.reshape(PATCH, BLK, LANES)
+        at = slice(owner * BLK, owner * BLK + BLK)
+        patch_ref[0:32, at, :] = total[:, 0:LANES].reshape(32, BLK, LANES)
+        patch_ref[32:PATCH, at, :] = total[:, LANES:].reshape(32, BLK, LANES)
     out_ref[...] = patch_ref[...].astype(BF16)
 
 

time: 142 us -> 141 us (level)
  no operation moved by 1% of the time
where the time goes in v8:
time: 141 us
  blocking collectives  102 us (72%)
  starting transfers between devices  26.3 us (19%)
  Pallas kernels  10.4 us (7%)
  local copies, waits for them, and re-layouts  1.77 us (1%)
    all_gather x1, blocking collectives, local(): weights = lax.all_gather(most, 'z', axis=0)  31.1 us
    all_to_all x1, blocking collectives, local(): lax.all_to_all(partial.reshape(PLANE * NH, 16, LANES), ('x', 'core', 'hea...  21.7 us
    all_to_all x1, blocking collectives, local(): lax.all_to_all(key_value, 'z', split_axis=0, concat_axis=0, tiled=True)  17.5 us
    all_to_all x1, starting transfers between devices, local(): lax.all_to_all(sorted_rows, 'z', split_axis=0, concat_axis=0, tiled=True)  15.8 us
    all_gather x1, blocking collectives, local(): features = lax.all_gather(wide, 'head', axis=0)  12.1 us
    all_to_all x1, blocking collectives, local(): lax.all_to_all(parts, 'head', split_axis=0, concat_axis=0, tiled=True)  11.6 us
    all_to_all x1, starting transfers between devices, local(): lax.all_to_all(spread, ('x', 'core'), split_axis=0, concat_axis=0, tiled=...  10.6 us
    all_gather x1, blocking collectives, local(): lax.all_gather(gathered.reshape(NZ * 32, 256), 'core', axis=0, tiled=True)  7.52 us
  transfers between devices with their start and end apart: 2, of which 0 were waited for; matrix products, arithmetic and copies ran while one was open for 0% of the time, Pallas kernels for 0%

profile of v8, /device:TPU:1, one launch (start us, length us, event | category | flops | bytes accessed | tf_op | source)
XLA Modules:
  0.0 140.9 jit_solution(10077858818061871697)
XLA Ops:
  0.0 2.6 %shard_map.109 = (bf16[16,72,128]{2,1,0:T(8,128)(2,1)}, bf16[560,128]{1,0:T(8,128)(2,1)}, bf16[252,128]{1,0:T(8,128)(2,1)}) custom-call(bf16[512,128]{1,0:T(8,128)(2,1)} %rows_hbm.1, s32[1,512]{1,0:T(1,128)} %bitcast.20, s32[1,512]{1,0:T(1,128)} %bitcast.15, bf16[256,128]{1,0:T(8,128)(2,1)} %bitcast.18, f32[1,128]{1,0:T(1,128)} %bitcast.21, ...), custom_call_target="tpu_custom_call" | custom-call | tf_op jit(solution)/shard_map/pallas_call | solution.py:298
  2.6 15.8 %all-to-all-start = ((bf16[16,72,128]{2,1,0:T(8,128)(2,1)}), bf16[16,72,128]{2,1,0:T(8,128)(2,1)S(1)}, u32[]{:S(2)}, u32[]{:S(2)}) async-start(bf16[16,72,128]{2,1,0:T(8,128)(2,1)} %get-tuple-element.11), calls=%async_computation | async-start | bytes 589824 | tf_op jit(solution)/shard_map/all_to_all | solution.py:326
  18.3 12.1 %all-gather = bf16[2240,128]{1,0:T(8,128)(2,1)S(1)} all-gather(bf16[560,128]{1,0:T(8,128)(2,1)} %get-tuple-element.13), channel_id=2, replica_groups=mesh['x'=4,'z'=16,'core'=2,'head'=4] {'head'}, dimensions={0}, use_global_device_ids=true | all-gather | bytes 716800 | tf_op jit(solution)/shard_map/all_gather | solution.py:327
  30.4 0.9 copy-done.2
  31.3 0.3 shard_map.110.query_ref
  31.6 0.8 copy-done
  32.5 0.0 all-to-all-done.arrived_ref
  32.5 1.6 %shard_map.111 = bf16[8,1040,128]{2,1,0:T(8,128)(2,1)} custom-call(bf16[16,72,128]{2,1,0:T(8,128)(2,1)S(1)} %all-to-all-done.arrived_ref), custom_call_target="tpu_custom_call" | custom-call | tf_op jit(solution)/shard_map/pallas_call | solution.py:333
  34.0 0.0 copy-start.7
  34.1 10.6 %all-to-all-start.1 = ((bf16[8,1040,128]{2,1,0:T(8,128)(2,1)}), bf16[8,1040,128]{2,1,0:T(8,128)(2,1)S(1)}, u32[]{:S(2)}, u32[]{:S(2)}) async-start(bf16[8,1040,128]{2,1,0:T(8,128)(2,1)} %shard_map.111), calls=%async_computation.1 | async-start | bytes 4259840 | tf_op jit(solution)/shard_map/all_to_all | solution.py:340
  44.6 31.1 %all-gather.2.weight_ref = bf16[16,252,128]{2,1,0:T(8,128)(2,1)S(1)} all-gather(bf16[1,252,128]{2,1,0:T(8,128)(2,1)S(1)} %bitcast.19), channel_id=3, replica_groups=mesh['x'=4,'z'=16,'core'=2,'head'=4] {'z'}, dimensions={0}, use_global_device_ids=true | all-gather | bytes 1096704 | tf_op jit(solution)/shard_map/all_gather | solution.py:332
  75.8 1.6 %shard_map.112.patch_ref = bf16[64,64,128]{2,1,0:T(8,128)(2,1)S(1)} custom-call(bf16[8,1040,128]{2,1,0:T(8,128)(2,1)S(1)} %all-to-all-done.1.tile_ref, bf16[16,252,128]{2,1,0:T(8,128)(2,1)S(1)} %all-gather.2.weight_ref), custom_call_target="tpu_custom_call" | custom-call | tf_op jit(solution)/shard_map/pallas_call | solution.py:342
  77.4 0.0 copy-start.4
  77.4 0.0 copy-start.5
  77.4 1.1 shard_map.113
  78.5 0.0 copy-start.3
  78.6 0.0 copy-start.6
  78.6 21.7 %all_to_all.25 = f32[32,16,128]{2,1,0:T(8,128)S(1)} all-to-all(f32[32,16,128]{2,1,0:T(8,128)S(1)} %bitcast.13), channel_id=1, replica_groups=mesh['x'=4,'z'=16,'core'=2,'head'=4] {'x','core','head'}, dimensions={0} | all-to-all | bytes 524288 | tf_op jit(solution)/shard_map/all_to_all | solution.py:353
  100.2 1.2 shard_map.114
  101.4 17.5 %all_to_all.26 = bf16[16,32,256]{2,1,0:T(8,128)(2,1)S(1)} all-to-all(bf16[16,32,256]{2,1,0:T(8,128)(2,1)S(1)} %shard_map.114), channel_id=1, replica_groups=mesh['x'=4,'z'=16,'core'=2,'head'=4] {'z'}, dimensions={0} | all-to-all | bytes 524288 | tf_op jit(solution)/shard_map/all_to_all | solution.py:363
  119.0 7.5 %all_gather.19.key_value_ref = bf16[1024,256]{1,0:T(8,128)(2,1)S(1)} all-gather(bf16[512,256]{1,0:T(8,128)(2,1)S(1)} %bitcast.17), channel_id=1, replica_groups=mesh['x'=4,'z'=16,'core'=2,'head'=4] {'core'}, dimensions={0}, use_global_device_ids=true | all-gather | bytes 786432 | tf_op jit(solution)/shard_map/all_gather | solution.py:364
  126.5 2.1 %shard_map.115 = bf16[4,512,128]{2,1,0:T(8,128)(2,1)S(1)} custom-call(bf16[512,128]{1,0:T(8,128)(2,1)S(1)} %shard_map.110.query_ref, bf16[1024,256]{1,0:T(8,128)(2,1)S(1)} %all_gather.19.key_value_ref, bf16[128,512]{1,0:T(8,128)(2,1)S(1)} %copy-done.3, s32[1,512]{1,0:T(1,128)S(1)} %bitcast.16), custom_call_target="tpu_custom_call" | custom-call | tf_op jit(solution)/shard_map/pallas_call | solution.py:365
  128.6 11.6 %all_to_all.27 = bf16[4,512,128]{2,1,0:T(8,128)(2,1)S(1)} all-to-all(bf16[4,512,128]{2,1,0:T(8,128)(2,1)S(1)} %shard_map.115), channel_id=1, replica_groups=mesh['x'=4,'z'=16,'core'=2,'head'=4] {'head'}, dimensions={0} | all-to-all | bytes 1048576 | tf_op jit(solution)/shard_map/all_to_all | solution.py:368
  140.2 0.7 reduce_sum.12
  (11 shorter events, 0.0 us)
Async XLA Ops:
  2.6 29.9 %all-to-all-start = ((bf16[16,72,128]{2,1,0:T(8,128)(2,1)}), bf16[16,72,128]{2,1,0:T(8,128)(2,1)S(1)}, u32[]{:S(2)}, u32[]{:S(2)}) async-start(bf16[16,72,128]{2,1,0:T(8,128)(2,1)} %get-tuple-element.11), calls=%async_computation | async-start | bytes 589824 | tf_op jit(solution)/shard_map/all_to_all | solution.py:326
  30.4 0.9 copy-start.2
  31.6 0.8 copy-start
  34.0 10.6 %copy-start.7 = (bf16[252,128]{1,0:T(8,128)(2,1)S(1)}, bf16[252,128]{1,0:T(8,128)(2,1)}, u32[]{:S(2)}) copy-start(bf16[252,128]{1,0:T(8,128)(2,1)} %get-tuple-element.16) | copy-start | bytes 193540
  34.1 41.7 %all-to-all-start.1 = ((bf16[8,1040,128]{2,1,0:T(8,128)(2,1)}), bf16[8,1040,128]{2,1,0:T(8,128)(2,1)S(1)}, u32[]{:S(2)}, u32[]{:S(2)}) async-start(bf16[8,1040,128]{2,1,0:T(8,128)(2,1)} %shard_map.111), calls=%async_computation.1 | async-start | bytes 4259840 | tf_op jit(solution)/shard_map/all_to_all | solution.py:340
  77.4 22.9 %copy-start.1 = (bf16[2240,128]{1,0:T(8,128)(2,1)S(1)}, bf16[2240,128]{1,0:T(8,128)(2,1)}, u32[]{:S(2)}) copy-start(bf16[2240,128]{1,0:T(8,128)(2,1)} %copy-done) | copy-start | bytes 1720324
  77.4 22.9 %copy-start.4 = (bf16[512,128]{1,0:T(8,128)(2,1)S(1)}, bf16[512,128]{1,0:T(8,128)(2,1)}, u32[]{:S(2)}) copy-start(bf16[512,128]{1,0:T(8,128)(2,1)} %key_ref.1) | copy-start | bytes 393220
  77.4 22.8 %copy-start.5 = (bf16[512,128]{1,0:T(8,128)(2,1)S(1)}, bf16[512,128]{1,0:T(8,128)(2,1)}, u32[]{:S(2)}) copy-start(bf16[512,128]{1,0:T(8,128)(2,1)} %value_ref.1) | copy-start | bytes 393220
  78.5 48.0 %copy-start.3 = (bf16[128,512]{1,0:T(8,128)(2,1)S(1)}, bf16[128,512]{1,0:T(8,128)(2,1)}, u32[]{:S(2)}) copy-start(bf16[128,512]{1,0:T(8,128)(2,1)} %weight_ref.3) | copy-start | bytes 393220
  78.6 48.0 %copy-start.6 = (s32[512]{0:T(512)S(1)}, s32[512]{0:T(512)}, u32[]{:S(2)}) copy-start(s32[512]{0:T(512)} %param.13) | copy-start | bytes 6148

commit v9 on v8

--- a/solution.py
+++ b/solution.py
@@ -188,29 +188,19 @@
                 out_ref[x, c, head] = sent
 
 
-def norm_kernel(sums_ref, wide_ref, key_ref, value_ref, out_ref):
+def norm_kernel(sums_ref, extra_ref, key_ref, value_ref, out_ref):
     count = 32
     left = iota((count, LANES), 1) < 64
     source, lane = iota((LANES, LANES), 0), iota((LANES, LANES), 1)
     hits = [(lane == (source >> 2) * 8 + c * 4 + (source & 3)) & (source < 64) for c in range(NC)]
-    backs = [(source == (lane >> 2) * 8 + c * 4 + (lane & 3)) & (lane < 64) for c in range(NC)]
     shares, gains, biases = [], [], []
     for x in range(NX):
-        whole = (
-            wide_ref[x, TOK : TOK + 16, :].astype(F32)
-            + wide_ref[x, TOK + 16 : TOK + 32, :].astype(F32)
-        ) + wide_ref[x, TOK + 32 : WIDE, :].astype(F32)
         for c in range(NC):
             total = sums_ref[x, c, 0]
             for head in range(1, NH):
                 total = total + sums_ref[x, c, head]
             total = jnp.concatenate([total, pltpu.roll(total, 64, 1)], 0)
-            extra = jnp.dot(
-                whole,
-                jnp.where(backs[c], 1.0, 0.0),
-                precision=lax.Precision.HIGHEST,
-                preferred_element_type=F32,
-            )
+            extra = extra_ref[x * NC + c]
             gains.append(extra[0:1, :])
             biases.append(extra[1:2, :])
             shares.append(jnp.where(left, total + extra[2:3, :], 0.0))
@@ -246,7 +236,7 @@
         out_ref[z] = both
 
 
-def query_kernel(features_ref, weight_ref, out_ref):
+def query_kernel(features_ref, weight_ref, out_ref, extra_ref):
     total = None
     for head in range(NH):
         part = jnp.dot(
@@ -256,6 +246,21 @@
         )
         total = part if total is None else total + part
     out_ref[...] = total.astype(BF16)
+    source, lane = iota((LANES, LANES), 0), iota((LANES, LANES), 1)
+    for x in range(NX):
+        whole = (
+            features_ref[x, TOK : TOK + 16, :].astype(F32)
+            + features_ref[x, TOK + 16 : TOK + 32, :].astype(F32)
+        ) + features_ref[x, TOK + 32 : WIDE, :].astype(F32)
+        for c in range(NC):
+            back = (source == (lane >> 2) * 8 + c * 4 + (lane & 3)) & (lane < 64)
+            extra = jnp.dot(
+                whole,
+                jnp.where(back, 1.0, 0.0),
+                precision=lax.Precision.HIGHEST,
+                preferred_element_type=F32,
+            )
+            extra_ref[x * NC + c] = extra[0:8, :]
 
 
 def attend_kernel(query_ref, key_value_ref, weight_ref, mask_ref, out_ref):
@@ -325,8 +330,10 @@
     )
     arrived = lax.all_to_all(sorted_rows, "z", split_axis=0, concat_axis=0, tiled=True)
     features = lax.all_gather(wide, "head", axis=0)
-    queries = pl.pallas_call(
-        query_kernel, out_shape=shape((TOK, LANES), BF16), compiler_params=params(16)
+    queries, extra = pl.pallas_call(
+        query_kernel,
+        out_shape=(shape((TOK, LANES), BF16), shape((PLANE, 8, LANES), F32)),
+        compiler_params=params(16),
     )(features, query_weight)
     arrived, most, queries = lax.optimization_barrier((arrived, most, queries))
     weights = lax.all_gather(most, "z", axis=0)
@@ -359,7 +366,7 @@
     )
     key_value = pl.pallas_call(
         norm_kernel, out_shape=shape((NZ, 32, 256), BF16), compiler_params=params(16)
-    )(sums.reshape(NX, NC, NH, 16, LANES), features, key_weight, value_weight)
+    )(sums.reshape(NX, NC, NH, 16, LANES), extra, key_weight, value_weight)
     gathered = lax.all_to_all(key_value, "z", split_axis=0, concat_axis=0, tiled=True)
     gathered = lax.all_gather(gathered.reshape(NZ * 32, 256), "core", axis=0, tiled=True)
     parts = pl.pallas_call(

time: 141 us -> 141 us (level)
  transfers between devices with their start and end apart: 2 -> 2, of which waited for: 0 -> 1; matrix products, arithmetic and copies ran while one was open for 0% -> 0% of each run, Pallas kernels for 0% -> 0%
where the time goes in v9:
time: 141 us; the launch traced here: 140 us
  blocking collectives  101 us (72%)
  starting transfers between devices  26.7 us (19%)
  Pallas kernels  10.2 us (7%)
    all_gather x1, blocking collectives, local(): weights = lax.all_gather(most, 'z', axis=0)  31.1 us
    all_to_all x1, blocking collectives, local(): lax.all_to_all(partial.reshape(PLANE * NH, 16, LANES), ('x', 'core', 'hea...  21.5 us
    all_to_all x1, blocking collectives, local(): lax.all_to_all(key_value, 'z', split_axis=0, concat_axis=0, tiled=True)  17.5 us
    all_to_all x1, starting transfers between devices, local(): lax.all_to_all(sorted_rows, 'z', split_axis=0, concat_axis=0, tiled=True)  15.8 us
    all_gather x1, blocking collectives, local(): features = lax.all_gather(wide, 'head', axis=0)  12.1 us
    all_to_all x1, blocking collectives, local(): lax.all_to_all(parts, 'head', split_axis=0, concat_axis=0, tiled=True)  11.6 us
    all_to_all x1, starting transfers between devices, local(): lax.all_to_all(spread, ('x', 'core'), split_axis=0, concat_axis=0, tiled=...  10.9 us
    all_gather x1, blocking collectives, local(): lax.all_gather(gathered.reshape(NZ * 32, 256), 'core', axis=0, tiled=True)  7.52 us
  transfers between devices with their start and end apart: 2, of which 1 were waited for; matrix products, arithmetic and copies ran while one was open for 0% of the time, Pallas kernels for 0%

profile of v9, /device:TPU:1, one launch (start us, length us, event | category | flops | bytes accessed | tf_op | source)
XLA Modules:
  0.0 140.3 jit_solution(15507112599746297658)
XLA Ops:
  0.0 2.6 %shard_map.109 = (bf16[16,72,128]{2,1,0:T(8,128)(2,1)}, bf16[560,128]{1,0:T(8,128)(2,1)}, bf16[252,128]{1,0:T(8,128)(2,1)}) custom-call(bf16[512,128]{1,0:T(8,128)(2,1)} %rows_hbm.1, s32[1,512]{1,0:T(1,128)} %bitcast.19, s32[1,512]{1,0:T(1,128)} %bitcast.14, bf16[256,128]{1,0:T(8,128)(2,1)} %bitcast.17, f32[1,128]{1,0:T(1,128)} %bitcast.20, ...), custom_call_target="tpu_custom_call" | custom-call | tf_op jit(solution)/shard_map/pallas_call | solution.py:303
  2.6 15.8 %all-to-all-start = ((bf16[16,72,128]{2,1,0:T(8,128)(2,1)}), bf16[16,72,128]{2,1,0:T(8,128)(2,1)S(1)}, u32[]{:S(2)}, u32[]{:S(2)}) async-start(bf16[16,72,128]{2,1,0:T(8,128)(2,1)} %get-tuple-element.13), calls=%async_computation | async-start | bytes 589824 | tf_op jit(solution)/shard_map/all_to_all | solution.py:331
  18.3 12.1 %all-gather = bf16[2240,128]{1,0:T(8,128)(2,1)S(1)} all-gather(bf16[560,128]{1,0:T(8,128)(2,1)} %get-tuple-element.15), channel_id=2, replica_groups=mesh['x'=4,'z'=16,'core'=2,'head'=4] {'head'}, dimensions={0}, use_global_device_ids=true | all-gather | bytes 716800 | tf_op jit(solution)/shard_map/all_gather | solution.py:332
  30.4 0.9 copy-done.3
  31.3 0.6 shard_map.110
  31.9 0.2 all-to-all-done.arrived_ref
  32.1 1.6 %shard_map.111 = bf16[8,1040,128]{2,1,0:T(8,128)(2,1)} custom-call(bf16[16,72,128]{2,1,0:T(8,128)(2,1)S(1)} %all-to-all-done.arrived_ref), custom_call_target="tpu_custom_call" | custom-call | tf_op jit(solution)/shard_map/pallas_call | solution.py:340
  33.7 0.0 copy-start.5
  33.7 10.9 %all-to-all-start.1 = ((bf16[8,1040,128]{2,1,0:T(8,128)(2,1)}), bf16[8,1040,128]{2,1,0:T(8,128)(2,1)S(1)}, u32[]{:S(2)}, u32[]{:S(2)}) async-start(bf16[8,1040,128]{2,1,0:T(8,128)(2,1)} %shard_map.111), calls=%async_computation.1 | async-start | bytes 4259840 | tf_op jit(solution)/shard_map/all_to_all | solution.py:347
  44.6 31.1 %all-gather.2.weight_ref = bf16[16,252,128]{2,1,0:T(8,128)(2,1)S(1)} all-gather(bf16[1,252,128]{2,1,0:T(8,128)(2,1)S(1)} %bitcast.18), channel_id=3, replica_groups=mesh['x'=4,'z'=16,'core'=2,'head'=4] {'z'}, dimensions={0}, use_global_device_ids=true | all-gather | bytes 1096704 | tf_op jit(solution)/shard_map/all_gather | solution.py:339
  75.8 0.0 all-to-all-done.1.tile_ref
  75.8 1.6 %shard_map.112.patch_ref = bf16[64,64,128]{2,1,0:T(8,128)(2,1)S(1)} custom-call(bf16[8,1040,128]{2,1,0:T(8,128)(2,1)S(1)} %all-to-all-done.1.tile_ref, bf16[16,252,128]{2,1,0:T(8,128)(2,1)S(1)} %all-gather.2.weight_ref), custom_call_target="tpu_custom_call" | custom-call | tf_op jit(solution)/shard_map/pallas_call | solution.py:349
  77.4 0.0 copy-start
  77.4 0.0 copy-start.1
  77.4 0.0 copy-start.2
  77.4 0.0 copy-start.4
  77.4 1.1 shard_map.113
  78.6 21.5 %all_to_all.25 = f32[32,16,128]{2,1,0:T(8,128)S(1)} all-to-all(f32[32,16,128]{2,1,0:T(8,128)S(1)} %bitcast.12), channel_id=1, replica_groups=mesh['x'=4,'z'=16,'core'=2,'head'=4] {'x','core','head'}, dimensions={0} | all-to-all | bytes 524288 | tf_op jit(solution)/shard_map/all_to_all | solution.py:360
  100.1 0.7 shard_map.114
  100.8 17.5 %all_to_all.26 = bf16[16,32,256]{2,1,0:T(8,128)(2,1)S(1)} all-to-all(bf16[16,32,256]{2,1,0:T(8,128)(2,1)S(1)} %shard_map.114), channel_id=1, replica_groups=mesh['x'=4,'z'=16,'core'=2,'head'=4] {'z'}, dimensions={0} | all-to-all | bytes 524288 | tf_op jit(solution)/shard_map/all_to_all | solution.py:370
  118.4 7.5 %all_gather.19.key_value_ref = bf16[1024,256]{1,0:T(8,128)(2,1)S(1)} all-gather(bf16[512,256]{1,0:T(8,128)(2,1)S(1)} %bitcast.16), channel_id=1, replica_groups=mesh['x'=4,'z'=16,'core'=2,'head'=4] {'core'}, dimensions={0}, use_global_device_ids=true | all-gather | bytes 786432 | tf_op jit(solution)/shard_map/all_gather | solution.py:371
  125.9 2.1 %shard_map.115 = bf16[4,512,128]{2,1,0:T(8,128)(2,1)S(1)} custom-call(bf16[512,128]{1,0:T(8,128)(2,1)S(1)} %get-tuple-element.17.query_ref, bf16[1024,256]{1,0:T(8,128)(2,1)S(1)} %all_gather.19.key_value_ref, bf16[128,512]{1,0:T(8,128)(2,1)S(1)} %copy-done.2, s32[1,512]{1,0:T(1,128)S(1)} %bitcast.15), custom_call_target="tpu_custom_call" | custom-call | tf_op jit(solution)/shard_map/pallas_call | solution.py:372
  128.0 11.6 %all_to_all.27 = bf16[4,512,128]{2,1,0:T(8,128)(2,1)S(1)} all-to-all(bf16[4,512,128]{2,1,0:T(8,128)(2,1)S(1)} %shard_map.115), channel_id=1, replica_groups=mesh['x'=4,'z'=16,'core'=2,'head'=4] {'head'}, dimensions={0} | all-to-all | bytes 1048576 | tf_op jit(solution)/shard_map/all_to_all | solution.py:375
  139.5 0.7 reduce_sum.12
  (7 shorter events, 0.0 us)
Async XLA Ops:
  2.6 29.5 %all-to-all-start = ((bf16[16,72,128]{2,1,0:T(8,128)(2,1)}), bf16[16,72,128]{2,1,0:T(8,128)(2,1)S(1)}, u32[]{:S(2)}, u32[]{:S(2)}) async-start(bf16[16,72,128]{2,1,0:T(8,128)(2,1)} %get-tuple-element.13), calls=%async_computation | async-start | bytes 589824 | tf_op jit(solution)/shard_map/all_to_all | solution.py:331
  30.4 0.9 copy-start.3
  33.7 10.9 %copy-start.5 = (bf16[252,128]{1,0:T(8,128)(2,1)S(1)}, bf16[252,128]{1,0:T(8,128)(2,1)}, u32[]{:S(2)}) copy-start(bf16[252,128]{1,0:T(8,128)(2,1)} %get-tuple-element.19) | copy-start | bytes 193540
  33.7 42.1 %all-to-all-start.1 = ((bf16[8,1040,128]{2,1,0:T(8,128)(2,1)}), bf16[8,1040,128]{2,1,0:T(8,128)(2,1)S(1)}, u32[]{:S(2)}, u32[]{:S(2)}) async-start(bf16[8,1040,128]{2,1,0:T(8,128)(2,1)} %shard_map.111), calls=%async_computation.1 | async-start | bytes 4259840 | tf_op jit(solution)/shard_map/all_to_all | solution.py:347
  77.4 22.7 %copy-start = (bf16[512,128]{1,0:T(8,128)(2,1)S(1)}, bf16[512,128]{1,0:T(8,128)(2,1)}, u32[]{:S(2)}) copy-start(bf16[512,128]{1,0:T(8,128)(2,1)} %key_ref.1) | copy-start | bytes 393220
  77.4 22.7 %copy-start.1 = (bf16[512,128]{1,0:T(8,128)(2,1)S(1)}, bf16[512,128]{1,0:T(8,128)(2,1)}, u32[]{:S(2)}) copy-start(bf16[512,128]{1,0:T(8,128)(2,1)} %value_ref.1) | copy-start | bytes 393220
  77.4 48.5 %copy-start.2 = (bf16[128,512]{1,0:T(8,128)(2,1)S(1)}, bf16[128,512]{1,0:T(8,128)(2,1)}, u32[]{:S(2)}) copy-start(bf16[128,512]{1,0:T(8,128)(2,1)} %weight_ref.3) | copy-start | bytes 393220
  77.4 48.5 %copy-start.4 = (s32[512]{0:T(512)S(1)}, s32[512]{0:T(512)}, u32[]{:S(2)}) copy-start(s32[512]{0:T(512)} %param.13) | copy-start | bytes 6148

commit v10 on v9

--- a/solution.py
+++ b/solution.py
@@ -277,7 +277,7 @@
         weights = jnp.exp2((scores - highest) * factor)
         totals = jnp.sum(weights, 0, keepdims=True)
         mix = lax.dot_general(values, weights.astype(BF16), TN, preferred_element_type=F32)
-        mixed.append(mix / totals)
+        mixed.append(mix * (1.0 / totals))
     attended = jnp.where(row < 64, mixed[0], mixed[1])
     attended = jnp.where(mask_ref[...] != 0, attended, 0.0).astype(BF16)
     part = lax.dot_general(attended, weight_ref[...], TN, preferred_element_type=F32).astype(BF16)

time: 141 us -> 141 us (level)
  no operation moved by 1% of the time
where the time goes in v10:
time: 141 us; the launch traced here: 140 us
  blocking collectives  101 us (72%)
  starting transfers between devices  26.7 us (19%)
  Pallas kernels  10.2 us (7%)
    all_gather x1, blocking collectives, local(): weights = lax.all_gather(most, 'z', axis=0)  31.1 us
    all_to_all x1, blocking collectives, local(): lax.all_to_all(partial.reshape(PLANE * NH, 16, LANES), ('x', 'core', 'hea...  21.5 us
    all_to_all x1, blocking collectives, local(): lax.all_to_all(key_value, 'z', split_axis=0, concat_axis=0, tiled=True)  17.5 us
    all_to_all x1, starting transfers between devices, local(): lax.all_to_all(sorted_rows, 'z', split_axis=0, concat_axis=0, tiled=True)  15.8 us
    all_gather x1, blocking collectives, local(): features = lax.all_gather(wide, 'head', axis=0)  12.1 us
    all_to_all x1, blocking collectives, local(): lax.all_to_all(parts, 'head', split_axis=0, concat_axis=0, tiled=True)  11.6 us
    all_to_all x1, starting transfers between devices, local(): lax.all_to_all(spread, ('x', 'core'), split_axis=0, concat_axis=0, tiled=...  10.9 us
    all_gather x1, blocking collectives, local(): lax.all_gather(gathered.reshape(NZ * 32, 256), 'core', axis=0, tiled=True)  7.52 us
  transfers between devices with their start and end apart: 2, of which 1 were waited for; matrix products, arithmetic and copies ran while one was open for 0% of the time, Pallas kernels for 0%

profile of v10, /device:TPU:1, one launch (start us, length us, event | category | flops | bytes accessed | tf_op | source)
XLA Modules:
  0.0 140.3 jit_solution(15507112599746297658)
XLA Ops:
  0.0 2.6 %shard_map.109 = (bf16[16,72,128]{2,1,0:T(8,128)(2,1)}, bf16[560,128]{1,0:T(8,128)(2,1)}, bf16[252,128]{1,0:T(8,128)(2,1)}) custom-call(bf16[512,128]{1,0:T(8,128)(2,1)} %rows_hbm.1, s32[1,512]{1,0:T(1,128)} %bitcast.19, s32[1,512]{1,0:T(1,128)} %bitcast.14, bf16[256,128]{1,0:T(8,128)(2,1)} %bitcast.17, f32[1,128]{1,0:T(1,128)} %bitcast.20, ...), custom_call_target="tpu_custom_call" | custom-call | tf_op jit(solution)/shard_map/pallas_call | solution.py:303
  2.6 15.8 %all-to-all-start = ((bf16[16,72,128]{2,1,0:T(8,128)(2,1)}), bf16[16,72,128]{2,1,0:T(8,128)(2,1)S(1)}, u32[]{:S(2)}, u32[]{:S(2)}) async-start(bf16[16,72,128]{2,1,0:T(8,128)(2,1)} %get-tuple-element.13), calls=%async_computation | async-start | bytes 589824 | tf_op jit(solution)/shard_map/all_to_all | solution.py:331
  18.3 12.1 %all-gather = bf16[2240,128]{1,0:T(8,128)(2,1)S(1)} all-gather(bf16[560,128]{1,0:T(8,128)(2,1)} %get-tuple-element.15), channel_id=2, replica_groups=mesh['x'=4,'z'=16,'core'=2,'head'=4] {'head'}, dimensions={0}, use_global_device_ids=true | all-gather | bytes 716800 | tf_op jit(solution)/shard_map/all_gather | solution.py:332
  30.4 0.9 copy-done.3
  31.3 0.6 shard_map.110
  31.9 0.2 all-to-all-done.arrived_ref
  32.1 1.6 %shard_map.111 = bf16[8,1040,128]{2,1,0:T(8,128)(2,1)} custom-call(bf16[16,72,128]{2,1,0:T(8,128)(2,1)S(1)} %all-to-all-done.arrived_ref), custom_call_target="tpu_custom_call" | custom-call | tf_op jit(solution)/shard_map/pallas_call | solution.py:340
  33.7 0.0 copy-start.5
  33.7 10.9 %all-to-all-start.1 = ((bf16[8,1040,128]{2,1,0:T(8,128)(2,1)}), bf16[8,1040,128]{2,1,0:T(8,128)(2,1)S(1)}, u32[]{:S(2)}, u32[]{:S(2)}) async-start(bf16[8,1040,128]{2,1,0:T(8,128)(2,1)} %shard_map.111), calls=%async_computation.1 | async-start | bytes 4259840 | tf_op jit(solution)/shard_map/all_to_all | solution.py:347
  44.6 31.1 %all-gather.2.weight_ref = bf16[16,252,128]{2,1,0:T(8,128)(2,1)S(1)} all-gather(bf16[1,252,128]{2,1,0:T(8,128)(2,1)S(1)} %bitcast.18), channel_id=3, replica_groups=mesh['x'=4,'z'=16,'core'=2,'head'=4] {'z'}, dimensions={0}, use_global_device_ids=true | all-gather | bytes 1096704 | tf_op jit(solution)/shard_map/all_gather | solution.py:339
  75.8 0.0 all-to-all-done.1.tile_ref
  75.8 1.6 %shard_map.112.patch_ref = bf16[64,64,128]{2,1,0:T(8,128)(2,1)S(1)} custom-call(bf16[8,1040,128]{2,1,0:T(8,128)(2,1)S(1)} %all-to-all-done.1.tile_ref, bf16[16,252,128]{2,1,0:T(8,128)(2,1)S(1)} %all-gather.2.weight_ref), custom_call_target="tpu_custom_call" | custom-call | tf_op jit(solution)/shard_map/pallas_call | solution.py:349
  77.4 0.0 copy-start
  77.4 0.0 copy-start.1
  77.4 0.0 copy-start.2
  77.4 0.0 copy-start.4
  77.4 1.1 shard_map.113
  78.6 21.5 %all_to_all.25 = f32[32,16,128]{2,1,0:T(8,128)S(1)} all-to-all(f32[32,16,128]{2,1,0:T(8,128)S(1)} %bitcast.12), channel_id=1, replica_groups=mesh['x'=4,'z'=16,'core'=2,'head'=4] {'x','core','head'}, dimensions={0} | all-to-all | bytes 524288 | tf_op jit(solution)/shard_map/all_to_all | solution.py:360
  100.1 0.7 shard_map.114
  100.8 17.5 %all_to_all.26 = bf16[16,32,256]{2,1,0:T(8,128)(2,1)S(1)} all-to-all(bf16[16,32,256]{2,1,0:T(8,128)(2,1)S(1)} %shard_map.114), channel_id=1, replica_groups=mesh['x'=4,'z'=16,'core'=2,'head'=4] {'z'}, dimensions={0} | all-to-all | bytes 524288 | tf_op jit(solution)/shard_map/all_to_all | solution.py:370
  118.4 7.5 %all_gather.19.key_value_ref = bf16[1024,256]{1,0:T(8,128)(2,1)S(1)} all-gather(bf16[512,256]{1,0:T(8,128)(2,1)S(1)} %bitcast.16), channel_id=1, replica_groups=mesh['x'=4,'z'=16,'core'=2,'head'=4] {'core'}, dimensions={0}, use_global_device_ids=true | all-gather | bytes 786432 | tf_op jit(solution)/shard_map/all_gather | solution.py:371
  125.9 2.1 %shard_map.115 = bf16[4,512,128]{2,1,0:T(8,128)(2,1)S(1)} custom-call(bf16[512,128]{1,0:T(8,128)(2,1)S(1)} %get-tuple-element.17.query_ref, bf16[1024,256]{1,0:T(8,128)(2,1)S(1)} %all_gather.19.key_value_ref, bf16[128,512]{1,0:T(8,128)(2,1)S(1)} %copy-done.2, s32[1,512]{1,0:T(1,128)S(1)} %bitcast.15), custom_call_target="tpu_custom_call" | custom-call | tf_op jit(solution)/shard_map/pallas_call | solution.py:372
  128.0 11.6 %all_to_all.27 = bf16[4,512,128]{2,1,0:T(8,128)(2,1)S(1)} all-to-all(bf16[4,512,128]{2,1,0:T(8,128)(2,1)S(1)} %shard_map.115), channel_id=1, replica_groups=mesh['x'=4,'z'=16,'core'=2,'head'=4] {'head'}, dimensions={0} | all-to-all | bytes 1048576 | tf_op jit(solution)/shard_map/all_to_all | solution.py:375
  139.5 0.7 reduce_sum.12
  (7 shorter events, 0.0 us)
Async XLA Ops:
  2.6 29.5 %all-to-all-start = ((bf16[16,72,128]{2,1,0:T(8,128)(2,1)}), bf16[16,72,128]{2,1,0:T(8,128)(2,1)S(1)}, u32[]{:S(2)}, u32[]{:S(2)}) async-start(bf16[16,72,128]{2,1,0:T(8,128)(2,1)} %get-tuple-element.13), calls=%async_computation | async-start | bytes 589824 | tf_op jit(solution)/shard_map/all_to_all | solution.py:331
  30.4 0.9 copy-start.3
  33.7 10.9 %copy-start.5 = (bf16[252,128]{1,0:T(8,128)(2,1)S(1)}, bf16[252,128]{1,0:T(8,128)(2,1)}, u32[]{:S(2)}) copy-start(bf16[252,128]{1,0:T(8,128)(2,1)} %get-tuple-element.19) | copy-start | bytes 193540
  33.7 42.1 %all-to-all-start.1 = ((bf16[8,1040,128]{2,1,0:T(8,128)(2,1)}), bf16[8,1040,128]{2,1,0:T(8,128)(2,1)S(1)}, u32[]{:S(2)}, u32[]{:S(2)}) async-start(bf16[8,1040,128]{2,1,0:T(8,128)(2,1)} %shard_map.111), calls=%async_computation.1 | async-start | bytes 4259840 | tf_op jit(solution)/shard_map/all_to_all | solution.py:347
  77.4 22.7 %copy-start = (bf16[512,128]{1,0:T(8,128)(2,1)S(1)}, bf16[512,128]{1,0:T(8,128)(2,1)}, u32[]{:S(2)}) copy-start(bf16[512,128]{1,0:T(8,128)(2,1)} %key_ref.1) | copy-start | bytes 393220
  77.4 22.7 %copy-start.1 = (bf16[512,128]{1,0:T(8,128)(2,1)S(1)}, bf16[512,128]{1,0:T(8,128)(2,1)}, u32[]{:S(2)}) copy-start(bf16[512,128]{1,0:T(8,128)(2,1)} %value_ref.1) | copy-start | bytes 393220
  77.4 48.5 %copy-start.2 = (bf16[128,512]{1,0:T(8,128)(2,1)S(1)}, bf16[128,512]{1,0:T(8,128)(2,1)}, u32[]{:S(2)}) copy-start(bf16[128,512]{1,0:T(8,128)(2,1)} %weight_ref.3) | copy-start | bytes 393220
  77.4 48.5 %copy-start.4 = (s32[512]{0:T(512)S(1)}, s32[512]{0:T(512)}, u32[]{:S(2)}) copy-start(s32[512]{0:T(512)} %param.13) | copy-start | bytes 6148
